TPU v7x, 256 devices: a whole 4x4x8 slice. The times are simulated.
256 devices in a mesh: tm: 8 (over y, core), space: 8 (over x, z_lo), clip: 4 (over z_hi).
Axes of the slice: x: 4, y: 4, z: 8 (z_hi: 4, z_lo: 2; z = z_hi * 2 + z_lo), core: 2. Of those that a mesh axis runs over, the one named last changes fastest.
Arguments:
- video: bfloat16 [16, 16, 1024, 512], P('clip', 'tm', 'space'), may hold values from -6 to 6
- conv_weight: bfloat16 [3, 512, 512], replicated, may hold values from -0.25 to 0.25
- norm_gain: float32 [512], replicated, may hold values from 0.1 to 1.9
- qkv_weight: bfloat16 [512, 1536], replicated
- out_weight: bfloat16 [512, 512], replicated, may hold values from -0.25 to 0.25
- cotangent: bfloat16 [16, 16, 1024, 512], P('clip', 'tm', 'space'), may hold values from -6 to 6
- lengths: int32 [16], P('clip'), may hold values from 5 to 16, as said below
Outputs:
- block_out: bfloat16 [16, 16, 1024, 512], P('clip', 'tm', 'space')
- out_weight_grad: float32 [512, 512], replicated
Inputs may be any that keep to these rules, and one draw needn't show every extreme that they name: `lengths`: some clip has exactly 16 valid frames in every draw.
All inputs are finite; a program needn't handle non-finite values.
Results may differ from a plain program's by a relative error of at most 0.017.
Values may be sent and summed in bfloat16 or wider, within the bound.
No kernel may reach another device: no remote copies, remote signals or barrier semaphores. Data moves between devices by JAX's collectives and lax.ppermute only.
A program may use at most 64 MiB of HBM per device.

v0:
```python
import jax
import jax.numpy as jnp
from jax import lax
from jax.sharding import PartitionSpec as P


def passed_along(shard, axis, by):
    peers = lax.axis_size(axis)
    pairs = [(i, i + by) for i in range(peers) if 0 <= i + by < peers]
    return lax.ppermute(shard, axis, pairs)


def attend_frame(frame):
    query_rows, key_rows, value_rows = frame
    scores = jnp.dot(query_rows, key_rows.T, preferred_element_type=jnp.float32) / jnp.sqrt(
        jnp.float32(query_rows.shape[-1])
    )
    top = jnp.max(scores, axis=-1, keepdims=True)
    expo = jnp.exp(scores - top)
    weights = (expo / jnp.sum(expo, axis=-1, keepdims=True)).astype(jnp.bfloat16)
    return jnp.dot(weights, value_rows, preferred_element_type=jnp.float32).astype(jnp.bfloat16)


def body(video, conv_weight, norm_gain, qkv_weight, out_weight, cotangent, lengths):
    clip_count, frame_count, pixel_count, channels = video.shape
    earlier = passed_along(video, "tm", 1)
    extended = jnp.concatenate([earlier, video], axis=1)
    conv_sum = jnp.zeros((clip_count * frame_count * pixel_count, channels), jnp.float32)
    for offset in range(3):
        window = extended[:, 2 - offset : 2 - offset + frame_count].reshape(-1, channels)
        conv_sum = conv_sum + jnp.dot(
            window, conv_weight[offset], preferred_element_type=jnp.float32
        )
    hidden = (video.reshape(-1, channels).astype(jnp.float32) + conv_sum).astype(jnp.bfloat16)
    wide = hidden.astype(jnp.float32)
    normed = (
        wide * lax.rsqrt(jnp.mean(wide * wide, axis=-1, keepdims=True) + 1e-06) * norm_gain
    ).astype(jnp.bfloat16)
    all_frames = clip_count * frame_count
    projected = jnp.dot(normed, qkv_weight, preferred_element_type=jnp.float32).astype(jnp.bfloat16)
    projected = projected.reshape(all_frames, pixel_count, 3 * channels)
    query_rows, key_rows, value_rows = (
        lax.all_to_all(projected[..., :channels], "space", split_axis=0, concat_axis=1, tiled=True),
        lax.all_to_all(
            projected[..., channels : 2 * channels],
            "space",
            split_axis=0,
            concat_axis=1,
            tiled=True,
        ),
        lax.all_to_all(
            projected[..., 2 * channels :], "space", split_axis=0, concat_axis=1, tiled=True
        ),
    )
    attended = lax.map(attend_frame, (query_rows, key_rows, value_rows))
    returned = lax.all_to_all(attended, "space", split_axis=1, concat_axis=0, tiled=True)
    attended_rows = returned.reshape(-1, channels)
    block_out = (
        hidden.astype(jnp.float32)
        + jnp.dot(attended_rows, out_weight, preferred_element_type=jnp.float32)
    ).astype(jnp.bfloat16)
    frame_index = lax.axis_index("tm") * frame_count + jnp.arange(frame_count, dtype=jnp.int32)
    live_mask = (frame_index[None, :] < lengths[:, None]).astype(jnp.bfloat16)
    masked = (cotangent * live_mask[:, :, None, None]).reshape(-1, channels)
    partial_grad = lax.dot_general(
        attended_rows, masked, (((0,), (0,)), ((), ())), preferred_element_type=jnp.float32
    )
    out_weight_grad = lax.psum(partial_grad, ("tm", "space", "clip"))
    return (block_out.reshape(video.shape), out_weight_grad)


def solution(mesh):
    in_specs = (
        P("clip", "tm", "space", None),
        P(),
        P(),
        P(),
        P(),
        P("clip", "tm", "space", None),
        P("clip"),
    )
    out_specs = (P("clip", "tm", "space", None), P())
    return jax.shard_map(body, mesh=mesh, in_specs=in_specs, out_specs=out_specs, check_vma=False)
```

profile of v0, /device:TPU:1, one launch (start us, length us, event | category | flops | bytes accessed | tf_op | source)
XLA Modules:
  0.0 389.5 jit_solution(15262767635633661964)
XLA Ops:
  7.2 4.7 %collective-permute-start = (bf16[4,2,128,512]{3,2,1,0:T(8,128)(2,1)}, bf16[4,2,128,512]{3,2,1,0:T(8,128)(2,1)S(1)}, u32[]{:S(2)}, u32[]{:S(2)}) collective-permute-start(bf16[4,2,128,512]{3,2,1,0:T(8,128)(2,1)} %param.7), channel_id=1, source_target_pairs={{0,32},{32,64},{64,96},{96,128},{128,160},{160,192},{192,224},{1,3... | collective-permute-start | bytes 3145736 | tf_op jit(solution)/shard_map/ppermute | solution.py:10
  11.9 2.1 fusion.17
  14.0 10.0 %collective-permute-done = bf16[4,2,128,512]{3,2,1,0:T(8,128)(2,1)S(1)} collective-permute-done((bf16[4,2,128,512]{3,2,1,0:T(8,128)(2,1)}, bf16[4,2,128,512]{3,2,1,0:T(8,128)(2,1)S(1)}, u32[]{:S(2)}, u32[]{:S(2)}) %collective-permute-start) | collective-permute-done | bytes 1048608 | tf_op jit(solution)/shard_map/ppermute | solution.py:10
  24.8 1.0 fusion.1
  25.8 1.9 convolution_convert_fusion
  27.7 1.2 fusion.25
  28.9 16.1 %all_to_all.16 = bf16[8,128,512]{2,1,0:T(8,128)(2,1)} all-to-all(bf16[8,128,512]{2,1,0:T(8,128)(2,1)S(1)} %get-tuple-element.14), channel_id=1, replica_groups=mesh['tm'=8,'space'=8,'clip'=4] {'space'}, dimensions={0} | all-to-all | bytes 2097152 | tf_op jit(solution)/shard_map/all_to_all | solution.py:43
  45.0 13.4 %all_to_all.17 = bf16[8,128,512]{2,1,0:T(8,128)(2,1)} all-to-all(bf16[8,128,512]{2,1,0:T(8,128)(2,1)S(1)} %get-tuple-element.12), channel_id=1, replica_groups=mesh['tm'=8,'space'=8,'clip'=4] {'space'}, dimensions={0} | all-to-all | bytes 2097152 | tf_op jit(solution)/shard_map/all_to_all | solution.py:44
  58.5 3.7 all-to-all-start.2
  62.2 2.8 multiply_reduce_fusion
  65.0 1.9 copy-done.2
  67.7 4.6 %all-to-all-done.2 = bf16[8,128,512]{2,1,0:T(8,128)(2,1)S(1)} async-done(((bf16[8,128,512]{2,1,0:T(8,128)(2,1)}), bf16[8,128,512]{2,1,0:T(8,128)(2,1)S(1)}, u32[]{:S(2)}, u32[]{:S(2)}) %all-to-all-start.2) | async-done | bytes 1048608 | tf_op jit(solution)/shard_map/all_to_all | solution.py:51
  72.3 3.5 fusion.7
  75.8 3.0 copy.21
  79.3 8.0 %reduce = bf16[1024,512]{1,0:T(8,128)(2,1)S(1)} reduce(bf16[1024,1,512]{2,1,0:T(2,128)(2,1)} %bitcast.42, bf16[]{:T(256)} %broadcast.51), dimensions={1}, to_apply=%bitcast.39.reduce_sub_computation | reduce | bytes 2097154
  87.4 1.6 reshape.93
  88.9 3.6 all-to-all-start.3
  92.7 2.3 broadcast_multiply_fusion
  95.0 8.2 %all-to-all-done.3 = bf16[8,2,32768]{2,1,0:T(2,128)(2,1)S(1)} async-done(((bf16[8,2,32768]{2,1,0:T(2,128)(2,1)}), bf16[8,2,32768]{2,1,0:T(2,128)(2,1)S(1)}, u32[]{:S(2)}, u32[]{:S(2)}) %all-to-all-start.3) | async-done | bytes 1048608 | tf_op jit(solution)/shard_map/all_to_all | solution.py:56
  103.2 3.4 reshape.94
  106.6 3.7 fusion.9
  110.3 3.3 fusion.4
  113.6 266.8 %all-reduce.2.cloned.1.call-done = f32[512,512]{1,0:T(8,128)} async-done(((f32[512,512]{1,0:T(8,128)}), f32[512,512]{1,0:T(8,128)}) %all-reduce.2.cloned.1.call-update) | async-done | bytes 1048592 | tf_op jit(solution)/shard_map/psum | solution.py:68
  380.4 2.3 copy.23
  (26 shorter events, 2.2 us)
Async XLA Ops:
  7.2 18.6 %copy-start = (bf16[512,1536]{1,0:T(8,128)(2,1)S(1)}, bf16[512,1536]{1,0:T(8,128)(2,1)}, u32[]{:S(2)}) copy-start(bf16[512,1536]{1,0:T(8,128)(2,1)} %param.10) | copy-start | bytes 4718596
  7.2 16.8 %copy-start.1 = (bf16[4,2,128,512]{3,2,1,0:T(8,128)(2,1)S(1)}, bf16[4,2,128,512]{3,2,1,0:T(8,128)(2,1)}, u32[]{:S(2)}) copy-start(bf16[4,2,128,512]{3,2,1,0:T(8,128)(2,1)} %param.7) | copy-start | bytes 3145732
  7.2 16.8 %collective-permute-start = (bf16[4,2,128,512]{3,2,1,0:T(8,128)(2,1)}, bf16[4,2,128,512]{3,2,1,0:T(8,128)(2,1)S(1)}, u32[]{:S(2)}, u32[]{:S(2)}) collective-permute-start(bf16[4,2,128,512]{3,2,1,0:T(8,128)(2,1)} %param.7), channel_id=1, source_target_pairs={{0,32},{32,64},{64,96},{96,128},{128,160},{160,192},{192,224},{1,3... | collective-permute-start | bytes 3145736 | tf_op jit(solution)/shard_map/ppermute | solution.py:10
  14.0 10.1 %copy-start.3 = (bf16[3,512,512]{2,1,0:T(8,128)(2,1)S(1)}, bf16[3,512,512]{2,1,0:T(8,128)(2,1)}, u32[]{:S(2)}) copy-start(bf16[3,512,512]{2,1,0:T(8,128)(2,1)} %param.8) | copy-start | bytes 4718596
  24.8 1.0 copy-start.8
  25.8 1.9 copy-start.4
  58.5 13.9 %all-to-all-start.2 = ((bf16[8,128,512]{2,1,0:T(8,128)(2,1)}), bf16[8,128,512]{2,1,0:T(8,128)(2,1)S(1)}, u32[]{:S(2)}, u32[]{:S(2)}) async-start(bf16[8,128,512]{2,1,0:T(8,128)(2,1)} %get-tuple-element.13), calls=%async_computation.2 | async-start | bytes 2097152 | tf_op jit(solution)/shard_map/all_to_all | solution.py:51
  65.0 1.9 copy-start.2
  87.3 5.2 %copy-start.6 = (s32[4]{0:T(128)S(1)}, s32[4]{0:T(128)}, u32[]{:S(2)}) copy-start(s32[4]{0:T(128)} %param.13) | copy-start | bytes 52
  88.9 14.2 %all-to-all-start.3 = ((bf16[8,2,32768]{2,1,0:T(2,128)(2,1)}), bf16[8,2,32768]{2,1,0:T(2,128)(2,1)S(1)}, u32[]{:S(2)}, u32[]{:S(2)}) async-start(bf16[8,2,32768]{2,1,0:T(2,128)(2,1)} %reshape.93), calls=%async_computation.3 | async-start | bytes 2097152 | tf_op jit(solution)/shard_map/all_to_all | solution.py:56
  92.5 287.9 %all-reduce.2.cloned.1.call-start = ((), (), s32[]{:S(2)}) async-start(), calls=%async_computation.4 | async-start | bytes 2097152 | tf_op jit(solution)/shard_map/psum | solution.py:68
  106.6 3.7 copy-start.5
  106.6 3.7 copy-start.7
Sparse Core Ops, SparseCore 0:
  110.4 269.9 all-reduce.1
where the time goes:
time: 391 us; the launch traced here: 390 us
  waiting for transfers between devices  290 us (74%)
  blocking collectives  29.5 us (8%)
  matrix products  18.9 us (5%)
  between operations  14.2 us (4%)
  local copies, waits for them, and re-layouts  13.9 us (4%)
  starting transfers between devices  12.1 us (3%)
  other arithmetic  11.3 us (3%)
    psum x1, waiting for transfers between devices, body(): out_weight_grad = lax.psum(partial_grad, ('tm', 'space', 'clip'))  267 us
    all_to_all x1, blocking collectives, body(): lax.all_to_all(projected[..., :channels], 'space', split_axis=0, concat_a...  16.1 us
    all_to_all x1, blocking collectives, body(): lax.all_to_all(projected[..., channels:2 * channels], 'space', split_axis...  13.4 us
    ppermute x1, waiting for transfers between devices, passed_along(): return lax.ppermute(shard, axis, pairs)  9.97 us
    unnamed x22, local copies, waits for them, and re-layouts  9.73 us
    all_to_all x1, waiting for transfers between devices, body(): lax.all_to_all(attended, 'space', split_axis=1, concat_axis=0, tiled=True)  8.17 us
    unnamed x1, other arithmetic  8.04 us
  transfers between devices with their start and end apart: 4, of which 4 were waited for; matrix products, arithmetic and copies ran while one was open for 3% of the time, Pallas kernels for 0%

commit v1 on v0

v1 whole, which is shorter than its diff:
```python
import functools

import jax
import jax.numpy as jnp
from jax import lax
from jax.experimental import pallas as pl
from jax.experimental.pallas import tpu as pltpu
from jax.sharding import Mesh, PartitionSpec as P

BF, F32 = jnp.bfloat16, jnp.float32
TIME = ("y", "core")
TILE = ("x", "zl")


def swap(x, axis, other):
    return lax.all_to_all(x, axis, split_axis=0, concat_axis=0, tiled=True)


def a2a(x, axes):
    return lax.all_to_all(x, axes, split_axis=0, concat_axis=0, tiled=True)


def group_size(axes):
    size = 1
    for axis in axes:
        size *= lax.axis_size(axis)
    return size


def conv_kernel(video_ref, early_ref, weight_ref, out_ref):
    half = video_ref.shape[2]

    def dot(rows, tap):
        return jnp.dot(rows, weight_ref[tap], preferred_element_type=F32)

    for clip in range(video_ref.shape[0]):
        v0, v1 = video_ref[clip, 0], video_ref[clip, 1]
        e0, e1 = early_ref[clip, 0], early_ref[clip, 1]
        out_ref[clip, 0] = (
            v0.astype(F32) + (dot(v0, 0) + dot(e1, 1) + dot(e0, 2))
        ).astype(BF)
        out_ref[clip, 1] = (
            v1.astype(F32) + (dot(v1, 0) + dot(v0, 1) + dot(e1, 2))
        ).astype(BF)


def attend_kernel(live_ref, hidden_ref, cot_ref, gain_ref, qkv_ref, wo_ref, out_ref, grad_ref, q_s, k_s, v_s):
    pixels, channels = hidden_ref.shape
    step = 256
    for i in range(pixels // step):
        rows = pl.ds(i * step, step)
        wide = hidden_ref[rows, :].astype(F32)
        mean = jnp.mean(wide * wide, axis=-1, keepdims=True)
        normed = (wide * lax.rsqrt(mean + 1e-06) * gain_ref[...]).astype(BF)
        for j, dst in enumerate((q_s, k_s, v_s)):
            dst[rows, :] = jnp.dot(
                normed, qkv_ref[:, j * channels : (j + 1) * channels], preferred_element_type=F32
            ).astype(BF)
    scale = 1.4426950408889634 / channels**0.5
    grad = jnp.zeros((channels, channels), F32)
    for i in range(pixels // step):
        rows = pl.ds(i * step, step)
        scores = lax.dot_general(
            q_s[rows, :], k_s[...], (((1,), (1,)), ((), ())), preferred_element_type=F32
        )
        top = jnp.max(scores, axis=-1, keepdims=True)
        expo = jnp.exp2((scores - top) * scale)
        total = jnp.sum(expo, axis=-1, keepdims=True)
        attended = (
            jnp.dot(expo.astype(BF), v_s[...], preferred_element_type=F32) / total
        ).astype(BF)
        out_ref[rows, :] = (
            hidden_ref[rows, :].astype(F32)
            + jnp.dot(attended, wo_ref[...], preferred_element_type=F32)
        ).astype(BF)
        grad = grad + lax.dot_general(
            attended, cot_ref[rows, :], (((0,), (0,)), ((), ())), preferred_element_type=F32
        )
    grad_ref[...] = grad * live_ref[0]


def scattered_sum(x, axes):
    n = group_size(axes)
    parts = a2a(x.astype(BF).reshape(n, x.shape[0] // n, x.shape[1]), axes)
    return jnp.sum(parts.astype(F32), axis=0)


def gathered(x, axes):
    n = group_size(axes)
    return a2a(jnp.broadcast_to(x[None], (n,) + x.shape), axes).reshape(n * x.shape[0], x.shape[1])


def exchanged(x, axis, by):
    n = lax.axis_size(axis)
    return lax.ppermute(x, axis, [(i, i ^ by) for i in range(n)])


def total_sum(grad):
    rows = grad.shape[0] // 2
    core = lax.axis_index("core")
    mine = lax.dynamic_slice_in_dim(grad, core * rows, rows, 0)
    other = lax.dynamic_slice_in_dim(grad, (1 - core) * rows, rows, 0).astype(BF)
    x = mine + exchanged(other, "core", 1).astype(F32)
    x = scattered_sum(x, ("y",) + TILE)
    for by in (1, 2):
        x = x + exchanged(x.astype(BF), "clip", by).astype(F32)
    x = gathered(x.astype(BF), ("y",) + TILE)
    other = exchanged(x, "core", 1)
    first = jnp.where(core == 0, x, other)
    second = jnp.where(core == 0, other, x)
    return jnp.concatenate([first, second], 0).astype(F32)


def body(video, conv_weight, norm_gain, qkv_weight, out_weight, cotangent, lengths):
    clips, frames, tile, channels = video.shape
    peers = clips * frames
    slabs = lax.axis_size(TIME)
    early = lax.ppermute(video, TIME, [(i, i + 1) for i in range(slabs - 1)])
    cot = a2a(cotangent.reshape(peers, tile, channels), TILE).reshape(peers * tile, channels)
    vmem = pl.BlockSpec(memory_space=pltpu.VMEM)
    params = pltpu.CompilerParams(vmem_limit_bytes=48 * 1024 * 1024)
    hidden = pl.pallas_call(
        conv_kernel,
        out_shape=jax.ShapeDtypeStruct(video.shape, BF),
        in_specs=[vmem] * 3,
        out_specs=vmem,
        compiler_params=params,
        name="conv",
    )(video, early, conv_weight)
    frame = a2a(hidden.reshape(peers, tile, channels), TILE).reshape(peers * tile, channels)
    place = lax.axis_index(TILE)
    moment = lax.axis_index(TIME) * frames + place % frames
    live = (moment < lengths[place // frames]).astype(F32).reshape(1)
    out, grad = pl.pallas_call(
        attend_kernel,
        out_shape=(
            jax.ShapeDtypeStruct(frame.shape, BF),
            jax.ShapeDtypeStruct((channels, channels), F32),
        ),
        in_specs=[pl.BlockSpec(memory_space=pltpu.SMEM)] + [vmem] * 5,
        out_specs=(vmem, vmem),
        scratch_shapes=[pltpu.VMEM(frame.shape, BF)] * 3,
        compiler_params=params,
        name="attend",
    )(live, frame, cot, norm_gain.reshape(1, channels), qkv_weight, out_weight)
    block_out = a2a(out.reshape(peers, tile, channels), TILE).reshape(video.shape)
    return block_out, total_sum(grad)


def solution(mesh):
    fine = Mesh(mesh.devices.reshape(4, 2, 4, 2, 4), ("y", "core", "x", "zl", "clip"))
    part = P("clip", TIME, TILE, None)
    in_specs = (part, P(), P(), P(), P(), part, P("clip"))
    return jax.shard_map(body, mesh=fine, in_specs=in_specs, out_specs=(part, P()), check_vma=False)
```

time: 391 us -> 116 us (0.30)
  the two profiles are of different devices: /device:TPU:1 before, /device:TPU:64 now
where the time goes in v1:
time: 116 us
  waiting for transfers between devices  40.4 us (35%)
  blocking collectives  33.2 us (29%)
  starting transfers between devices  24.2 us (21%)
  Pallas kernels  11.3 us (10%)
  local copies, waits for them, and re-layouts  3.89 us (3%)
  between operations  1.41 us (1%)
  other arithmetic  1.29 us (1%)
    all_to_all x2, blocking collectives, a2a(): return lax.all_to_all(x, axes, split_axis=0, concat_axis=0, tiled=True)  33.2 us
    all_to_all x3, waiting for transfers between devices, a2a(): return lax.all_to_all(x, axes, split_axis=0, concat_axis=0, tiled=True)  27.7 us
    all_to_all x3, starting transfers between devices, a2a(): return lax.all_to_all(x, axes, split_axis=0, concat_axis=0, tiled=True)  12.9 us
    ppermute x4, waiting for transfers between devices, exchanged(): return lax.ppermute(x, axis, [(i, i ^ by) for i in range(n)])  10.3 us
    ppermute x4, starting transfers between devices, exchanged(): return lax.ppermute(x, axis, [(i, i ^ by) for i in range(n)])  9.8 us
    pallas_call x1, Pallas kernels, body(): pl.pallas_call(attend_kernel, out_shape=(jax.ShapeDtypeStruct(frame.shape...  8.58 us
    unnamed x11, local copies, waits for them, and re-layouts  3.25 us
    pallas_call x1, Pallas kernels, body(): pl.pallas_call(conv_kernel, out_shape=jax.ShapeDtypeStruct(video.shape, B...  2.77 us
  transfers between devices with their start and end apart: 8, of which 8 were waited for; matrix products, arithmetic and copies ran while one was open for 1% of the time, Pallas kernels for 2%

profile of v1, /device:TPU:64, one launch (start us, length us, event | category | flops | bytes accessed | tf_op | source)
XLA Modules:
  0.0 115.8 jit_solution(9338547959047745065)
XLA Ops:
  0.6 5.8 %all-to-all-start.1 = ((bf16[8,128,512]{2,1,0:T(8,128)(2,1)}), bf16[8,128,512]{2,1,0:T(8,128)(2,1)S(1)}, u32[]{:S(2)}, u32[]{:S(2)}) async-start(bf16[8,128,512]{2,1,0:T(8,128)(2,1)} %bitcast.18), calls=%async_computation.1 | async-start | bytes 2097152 | tf_op jit(solution)/shard_map/all_to_all | solution.py:20
  6.4 1.5 %collective-permute-start = (bf16[4,2,128,512]{3,2,1,0:T(8,128)(2,1)}, bf16[4,2,128,512]{3,2,1,0:T(8,128)(2,1)S(1)}, u32[]{:S(2)}, u32[]{:S(2)}) collective-permute-start(bf16[4,2,128,512]{3,2,1,0:T(8,128)(2,1)} %video_ref.1), channel_id=1, source_target_pairs={{0,32},{32,64},{64,96},{96,128},{128,160},{160,192},{192,224},{1,3... | collective-permute-start | bytes 3145736 | tf_op jit(solution)/shard_map/ppermute | solution.py:118
  8.0 2.4 %collective-permute-done.early_ref = bf16[4,2,128,512]{3,2,1,0:T(8,128)(2,1)S(1)} collective-permute-done((bf16[4,2,128,512]{3,2,1,0:T(8,128)(2,1)}, bf16[4,2,128,512]{3,2,1,0:T(8,128)(2,1)S(1)}, u32[]{:S(2)}, u32[]{:S(2)}) %collective-permute-start) | collective-permute-done | bytes 1048608 | tf_op jit(solution)/shard_map/ppermute | solution.py:118
  10.4 1.2 %copy-done.1 = bf16[4,2,128,512]{3,2,1,0:T(8,128)(2,1)S(1)} copy-done((bf16[4,2,128,512]{3,2,1,0:T(8,128)(2,1)S(1)}, bf16[4,2,128,512]{3,2,1,0:T(8,128)(2,1)}, u32[]{:S(2)}) %copy-start.1) | copy-done | bytes 1048600
  11.6 2.8 %conv.1 = bf16[4,2,128,512]{3,2,1,0:T(8,128)(2,1)} custom-call(bf16[4,2,128,512]{3,2,1,0:T(8,128)(2,1)S(1)} %copy-done.1, bf16[4,2,128,512]{3,2,1,0:T(8,128)(2,1)S(1)} %collective-permute-done.early_ref, bf16[3,512,512]{2,1,0:T(8,128)(2,1)S(1)} %copy-done), custom_call_target="tpu_custom_call" | custom-call | tf_op jit(solution)/shard_map/conv/pallas_call | solution.py:122
  14.4 7.8 %all-to-all-done.1 = bf16[8,128,512]{2,1,0:T(8,128)(2,1)S(1)} async-done(((bf16[8,128,512]{2,1,0:T(8,128)(2,1)}), bf16[8,128,512]{2,1,0:T(8,128)(2,1)S(1)}, u32[]{:S(2)}, u32[]{:S(2)}) %all-to-all-start.1) | async-done | bytes 1048608 | tf_op jit(solution)/shard_map/all_to_all | solution.py:20
  22.1 3.6 %all-to-all-start = ((bf16[8,128,512]{2,1,0:T(8,128)(2,1)}), bf16[8,128,512]{2,1,0:T(8,128)(2,1)S(1)}, u32[]{:S(2)}, u32[]{:S(2)}) async-start(bf16[8,128,512]{2,1,0:T(8,128)(2,1)} %bitcast.2), calls=%async_computation | async-start | bytes 2097152 | tf_op jit(solution)/shard_map/all_to_all | solution.py:20
  25.7 0.6 dynamic_slice.9
  27.0 10.8 %all-to-all-done = bf16[8,128,512]{2,1,0:T(8,128)(2,1)S(1)} async-done(((bf16[8,128,512]{2,1,0:T(8,128)(2,1)}), bf16[8,128,512]{2,1,0:T(8,128)(2,1)S(1)}, u32[]{:S(2)}, u32[]{:S(2)}) %all-to-all-start) | async-done | bytes 1048608 | tf_op jit(solution)/shard_map/all_to_all | solution.py:20
  37.8 1.0 copy-done.2
  38.8 8.6 %attend.1 = (bf16[1024,512]{1,0:T(8,128)(2,1)}, f32[512,512]{1,0:T(8,128)S(1)}) custom-call(f32[1]{0:T(128)} %bitcast.1.live_ref, bf16[1024,512]{1,0:T(8,128)(2,1)S(1)} %bitcast.15, bf16[1024,512]{1,0:T(8,128)(2,1)S(1)} %bitcast.14, f32[1,512]{1,0:T(1,128)S(1)} %bitcast.16, bf16[512,1536]{1,0:T(8,128)(2,1)} %qkv_ref.1, bf16[512,512]{1,0:T(8,128)(2,1)S(1)} %copy-done.2), custom_call_target="tpu_custom_call" | custom-call | tf_op jit(solution)/shard_map/attend/pallas_call | solution.py:134
  47.4 5.1 %collective-permute-start.1 = (bf16[256,512]{1,0:T(8,128)(2,1)S(1)}, bf16[256,512]{1,0:T(8,128)(2,1)S(1)}, u32[]{:S(2)}, u32[]{:S(2)}) collective-permute-start(bf16[256,512]{1,0:T(8,128)(2,1)S(1)} %dynamic-slice_convert_fusion), channel_id=1, source_target_pairs={{0,32},{32,0},{1,33},{33,1},{2,34},{34,2},{3,35},{35,3},{4,36},{36... | collective-permute-start | bytes 786440 | tf_op jit(solution)/shard_map/ppermute | solution.py:95
  52.5 1.2 %collective-permute-done.1 = bf16[256,512]{1,0:T(8,128)(2,1)S(1)} collective-permute-done((bf16[256,512]{1,0:T(8,128)(2,1)S(1)}, bf16[256,512]{1,0:T(8,128)(2,1)S(1)}, u32[]{:S(2)}, u32[]{:S(2)}) %collective-permute-start.1) | collective-permute-done | bytes 262176 | tf_op jit(solution)/shard_map/ppermute | solution.py:95
  53.8 20.4 %all_to_all.25 = bf16[32,8,512]{2,1,0:T(8,128)(2,1)S(1)} all-to-all(bf16[32,8,512]{2,1,0:T(8,128)(2,1)S(1)} %fusion), channel_id=1, replica_groups=mesh['y'=4,'core'=2,'x'=4,'zl'=2,'clip'=4] {'y','x','zl'}, dimensions={0} | all-to-all | bytes 524288 | tf_op jit(solution)/shard_map/all_to_all | solution.py:20
  74.3 4.5 %collective-permute-done.2 = bf16[8,512]{1,0:T(8,128)(2,1)S(1)} collective-permute-done((bf16[8,512]{1,0:T(8,128)(2,1)S(1)}, bf16[8,512]{1,0:T(8,128)(2,1)S(1)}, u32[]{:S(2)}, u32[]{:S(2)}) %collective-permute-start.2) | collective-permute-done | bytes 8224 | tf_op jit(solution)/shard_map/ppermute | solution.py:95
  78.8 4.5 %collective-permute-start.3 = (bf16[8,512]{1,0:T(8,128)(2,1)S(1)}, bf16[8,512]{1,0:T(8,128)(2,1)S(1)}, u32[]{:S(2)}, u32[]{:S(2)}) collective-permute-start(bf16[8,512]{1,0:T(8,128)(2,1)S(1)} %fusion.1), channel_id=1, source_target_pairs={{0,2},{1,3},{2,0},{3,1},{4,6},{5,7},{6,4},{7,5},{8,10},{9,11},{10,... | collective-permute-start | bytes 24584 | tf_op jit(solution)/shard_map/ppermute | solution.py:95
  83.3 3.1 %collective-permute-done.3 = bf16[8,512]{1,0:T(8,128)(2,1)S(1)} collective-permute-done((bf16[8,512]{1,0:T(8,128)(2,1)S(1)}, bf16[8,512]{1,0:T(8,128)(2,1)S(1)}, u32[]{:S(2)}, u32[]{:S(2)}) %collective-permute-start.3) | collective-permute-done | bytes 8224 | tf_op jit(solution)/shard_map/ppermute | solution.py:95
  86.4 12.9 %all_to_all.26 = bf16[32,8,512]{2,1,0:T(8,128)(2,1)S(1)} all-to-all(bf16[32,8,512]{2,1,0:T(8,128)(2,1)S(1)} %broadcast_in_dim.2), channel_id=1, replica_groups=mesh['y'=4,'core'=2,'x'=4,'zl'=2,'clip'=4] {'y','x','zl'}, dimensions={0} | all-to-all | bytes 524288 | tf_op jit(solution)/shard_map/all_to_all | solution.py:20
  99.3 3.6 %all-to-all-start.2 = ((bf16[8,128,512]{2,1,0:T(8,128)(2,1)}), bf16[8,128,512]{2,1,0:T(8,128)(2,1)S(1)}, u32[]{:S(2)}, u32[]{:S(2)}) async-start(bf16[8,128,512]{2,1,0:T(8,128)(2,1)} %bitcast.7), calls=%async_computation.2 | async-start | bytes 2097152 | tf_op jit(solution)/shard_map/all_to_all | solution.py:20
  102.9 0.1 collective-permute-start.4
  103.0 1.5 %collective-permute-done.4 = bf16[256,512]{1,0:T(8,128)(2,1)S(1)} collective-permute-done((bf16[256,512]{1,0:T(8,128)(2,1)S(1)}, bf16[256,512]{1,0:T(8,128)(2,1)S(1)}, u32[]{:S(2)}, u32[]{:S(2)}) %collective-permute-start.4) | collective-permute-done | bytes 262176 | tf_op jit(solution)/shard_map/ppermute | solution.py:95
  104.5 1.1 maximum_convert_fusion
  105.6 9.2 %all-to-all-done.2 = bf16[8,128,512]{2,1,0:T(8,128)(2,1)S(1)} async-done(((bf16[8,128,512]{2,1,0:T(8,128)(2,1)}), bf16[8,128,512]{2,1,0:T(8,128)(2,1)S(1)}, u32[]{:S(2)}, u32[]{:S(2)}) %all-to-all-start.2) | async-done | bytes 1048608 | tf_op jit(solution)/shard_map/all_to_all | solution.py:20
  114.9 1.0 copy.10
  (17 shorter events, 0.3 us)
Async XLA Ops:
  0.6 9.7 %copy-start = (bf16[3,512,512]{2,1,0:T(8,128)(2,1)S(1)}, bf16[3,512,512]{2,1,0:T(8,128)(2,1)}, u32[]{:S(2)}) copy-start(bf16[3,512,512]{2,1,0:T(8,128)(2,1)} %weight_ref.1) | copy-start | bytes 4718596
  0.6 21.5 %all-to-all-start.1 = ((bf16[8,128,512]{2,1,0:T(8,128)(2,1)}), bf16[8,128,512]{2,1,0:T(8,128)(2,1)S(1)}, u32[]{:S(2)}, u32[]{:S(2)}) async-start(bf16[8,128,512]{2,1,0:T(8,128)(2,1)} %bitcast.18), calls=%async_computation.1 | async-start | bytes 2097152 | tf_op jit(solution)/shard_map/all_to_all | solution.py:20
  6.4 3.9 %collective-permute-start = (bf16[4,2,128,512]{3,2,1,0:T(8,128)(2,1)}, bf16[4,2,128,512]{3,2,1,0:T(8,128)(2,1)S(1)}, u32[]{:S(2)}, u32[]{:S(2)}) collective-permute-start(bf16[4,2,128,512]{3,2,1,0:T(8,128)(2,1)} %video_ref.1), channel_id=1, source_target_pairs={{0,32},{32,64},{64,96},{96,128},{128,160},{160,192},{192,224},{1,3... | collective-permute-start | bytes 3145736 | tf_op jit(solution)/shard_map/ppermute | solution.py:118
  10.4 1.2 %copy-start.1 = (bf16[4,2,128,512]{3,2,1,0:T(8,128)(2,1)S(1)}, bf16[4,2,128,512]{3,2,1,0:T(8,128)(2,1)}, u32[]{:S(2)}) copy-start(bf16[4,2,128,512]{3,2,1,0:T(8,128)(2,1)} %video_ref.1) | copy-start | bytes 3145732
  14.4 11.4 %copy-start.4 = (s32[4]{0:T(128)S(1)}, s32[4]{0:T(128)}, u32[]{:S(2)}) copy-start(s32[4]{0:T(128)} %param.13) | copy-start | bytes 52
  14.4 23.4 %copy-start.3 = (f32[512]{0:T(512)S(1)}, f32[512]{0:T(512)}, u32[]{:S(2)}) copy-start(f32[512]{0:T(512)} %param.9) | copy-start | bytes 6148
  22.1 15.6 %all-to-all-start = ((bf16[8,128,512]{2,1,0:T(8,128)(2,1)}), bf16[8,128,512]{2,1,0:T(8,128)(2,1)S(1)}, u32[]{:S(2)}, u32[]{:S(2)}) async-start(bf16[8,128,512]{2,1,0:T(8,128)(2,1)} %bitcast.2), calls=%async_computation | async-start | bytes 2097152 | tf_op jit(solution)/shard_map/all_to_all | solution.py:20
  37.8 1.0 copy-start.2
  47.4 6.3 %collective-permute-start.1 = (bf16[256,512]{1,0:T(8,128)(2,1)S(1)}, bf16[256,512]{1,0:T(8,128)(2,1)S(1)}, u32[]{:S(2)}, u32[]{:S(2)}) collective-permute-start(bf16[256,512]{1,0:T(8,128)(2,1)S(1)} %dynamic-slice_convert_fusion), channel_id=1, source_target_pairs={{0,32},{32,0},{1,33},{33,1},{2,34},{34,2},{3,35},{35,3},{4,36},{36... | collective-permute-start | bytes 786440 | tf_op jit(solution)/shard_map/ppermute | solution.py:95
  74.2 4.6 %collective-permute-start.2 = (bf16[8,512]{1,0:T(8,128)(2,1)S(1)}, bf16[8,512]{1,0:T(8,128)(2,1)S(1)}, u32[]{:S(2)}, u32[]{:S(2)}) collective-permute-start(bf16[8,512]{1,0:T(8,128)(2,1)S(1)} %convert_element_type.35), channel_id=1, source_target_pairs={{0,1},{1,0},{2,3},{3,2},{4,5},{5,4},{6,7},{7,6},{8,9},{9,8},{10,11... | collective-permute-start | bytes 24584 | tf_op jit(solution)/shard_map/ppermute | solution.py:95
  78.8 7.6 %collective-permute-start.3 = (bf16[8,512]{1,0:T(8,128)(2,1)S(1)}, bf16[8,512]{1,0:T(8,128)(2,1)S(1)}, u32[]{:S(2)}, u32[]{:S(2)}) collective-permute-start(bf16[8,512]{1,0:T(8,128)(2,1)S(1)} %fusion.1), channel_id=1, source_target_pairs={{0,2},{1,3},{2,0},{3,1},{4,6},{5,7},{6,4},{7,5},{8,10},{9,11},{10,... | collective-permute-start | bytes 24584 | tf_op jit(solution)/shard_map/ppermute | solution.py:95
  99.3 15.6 %all-to-all-start.2 = ((bf16[8,128,512]{2,1,0:T(8,128)(2,1)}), bf16[8,128,512]{2,1,0:T(8,128)(2,1)S(1)}, u32[]{:S(2)}, u32[]{:S(2)}) async-start(bf16[8,128,512]{2,1,0:T(8,128)(2,1)} %bitcast.7), calls=%async_computation.2 | async-start | bytes 2097152 | tf_op jit(solution)/shard_map/all_to_all | solution.py:20
  102.9 1.6 %collective-permute-start.4 = (bf16[256,512]{1,0:T(8,128)(2,1)S(1)}, bf16[256,512]{1,0:T(8,128)(2,1)S(1)}, u32[]{:S(2)}, u32[]{:S(2)}) collective-permute-start(bf16[256,512]{1,0:T(8,128)(2,1)S(1)} %bitcast.19), channel_id=1, source_target_pairs={{0,32},{32,0},{1,33},{33,1},{2,34},{34,2},{3,35},{35,3},{4,36},{36... | collective-permute-start | bytes 786440 | tf_op jit(solution)/shard_map/ppermute | solution.py:95

commit v2 on v1

v2 whole, which is shorter than its diff:
```python
import jax
import jax.numpy as jnp
from jax import lax
from jax.experimental import pallas as pl
from jax.experimental.pallas import tpu as pltpu
from jax.sharding import Mesh, PartitionSpec as P

BF, F32 = jnp.bfloat16, jnp.float32
TIME = ("y", "core")
TILE = ("x", "zl")
PLANE = ("y", "x")
DEPTH = ("zl", "clip")
ANY = pl.BlockSpec(memory_space=pl.ANY)
VMEM = pl.BlockSpec(memory_space=pltpu.VMEM)
SMEM = pl.BlockSpec(memory_space=pltpu.SMEM)
PARAMS = pltpu.CompilerParams(vmem_limit_bytes=12 * 1024 * 1024)


def a2a(x, axes):
    return lax.all_to_all(x, axes, split_axis=0, concat_axis=0, tiled=True)


def group_size(axes):
    size = 1
    for axis in axes:
        size *= lax.axis_size(axis)
    return size


def call(kernel, name, out_shape, in_specs, out_specs, *args, **more):
    return pl.pallas_call(
        kernel,
        out_shape=out_shape,
        in_specs=in_specs,
        out_specs=out_specs,
        compiler_params=PARAMS,
        name=name,
        **more,
    )(*args)


def after(x, *others):
    def kernel(*refs):
        pass

    return call(
        kernel,
        "after",
        jax.ShapeDtypeStruct(x.shape, x.dtype),
        [ANY] * (1 + len(others)),
        ANY,
        x,
        *others,
        input_output_aliases={0: 0},
    )


def own_kernel(video_ref, weight_ref, own_ref):
    def dot(rows, tap):
        return jnp.dot(rows, weight_ref[tap], preferred_element_type=F32)

    rows = (own_ref.shape[0] * own_ref.shape[2], own_ref.shape[3])
    v0, v1 = video_ref[:, 0].reshape(rows), video_ref[:, 1].reshape(rows)
    own_ref[:, 0] = (v0.astype(F32) + dot(v0, 0)).reshape(own_ref[:, 0].shape)
    own_ref[:, 1] = (v1.astype(F32) + (dot(v1, 0) + dot(v0, 1))).reshape(own_ref[:, 0].shape)


def early_kernel(own_ref, early_ref, weight_ref, out_ref):
    def dot(rows, tap):
        return jnp.dot(rows, weight_ref[tap], preferred_element_type=F32)

    rows = (own_ref.shape[0] * own_ref.shape[2], own_ref.shape[3])
    e0, e1 = early_ref[:, 0].reshape(rows), early_ref[:, 1].reshape(rows)
    h0 = own_ref[:, 0].reshape(rows) + (dot(e1, 1) + dot(e0, 2))
    h1 = own_ref[:, 1].reshape(rows) + dot(e1, 2)
    out_ref[:, 0] = h0.astype(BF).reshape(out_ref[:, 0].shape)
    out_ref[:, 1] = h1.astype(BF).reshape(out_ref[:, 1].shape)


def attend_kernel(
    hidden_ref, gain_ref, qkv_ref, att_ref, q_s, k_s, v_s
):
    pixels, channels = att_ref.shape
    step = 256
    steps = pixels // step

    def chunk(i):
        return pl.ds(i * step, step)

    def normed(i):
        wide = hidden_ref[chunk(i), :].astype(F32)
        mean = jnp.mean(wide * wide, axis=-1, keepdims=True)
        return (wide * lax.rsqrt(mean + 1e-06) * gain_ref[...]).astype(BF)

    ready = normed(0)
    for i in range(steps):
        following = normed(i + 1) if i + 1 < steps else None
        for j, dst in enumerate((q_s, k_s, v_s)):
            dst[chunk(i), :] = jnp.dot(
                ready, qkv_ref[:, j * channels : (j + 1) * channels], preferred_element_type=F32
            ).astype(BF)
        ready = following
    scale = 1.4426950408889634 / channels**0.5

    def scored(i):
        return lax.dot_general(
            q_s[chunk(i), :], k_s[...], (((1,), (1,)), ((), ())), preferred_element_type=F32
        )

    def weighed(scores):
        top = jnp.max(scores, axis=-1, keepdims=True)
        expo = jnp.exp2((scores - top) * scale)
        return expo.astype(BF), jnp.sum(expo, axis=-1, keepdims=True)

    def attended(expo, total):
        mixed = jnp.dot(expo, v_s[...], preferred_element_type=F32)
        return (mixed * (1.0 / total)).astype(BF)

    stages = [{} for _ in range(2)]
    for t in range(steps + 2):
        if t < steps:
            stages[0][t] = scored(t)
        if 0 <= t - 1 < steps:
            stages[1][t - 1] = weighed(stages[0].pop(t - 1))
        if 0 <= t - 2 < steps:
            att_ref[chunk(t - 2), :] = attended(*stages[1].pop(t - 2))


def grad_kernel(place_ref, lengths_ref, att_ref, cot_ref, mine_ref, other_ref, cot_s, g_s):
    clips, frames, tile, channels = cot_ref.shape
    for clip in range(clips):
        for frame in range(frames):
            live = place_ref[0] * frames + frame < lengths_ref[clip]
            rows = pl.ds((clip * frames + frame) * tile, tile)
            cot_s[rows, :] = cot_ref[clip, frame] * jnp.where(live, 1.0, 0.0).astype(BF)
    g_s[...] = lax.dot_general(
        att_ref[...], cot_s[...], (((0,), (0,)), ((), ())), preferred_element_type=F32
    )
    core = place_ref[1]
    split = channels // 2
    mine_ref[...] = g_s[pl.ds(pl.multiple_of(core * split, split), split), :]
    other_ref[...] = g_s[pl.ds(pl.multiple_of((1 - core) * split, split), split), :].astype(BF)


def out_kernel(hidden_ref, att_ref, wo_ref, out_ref):
    out_ref[...] = (
        hidden_ref[...].astype(F32)
        + jnp.dot(att_ref[...], wo_ref[...], preferred_element_type=F32)
    ).astype(BF)


def exchanged(x, axis, by):
    n = lax.axis_size(axis)
    return lax.ppermute(x, axis, [(i, i ^ by) for i in range(n)])


def spread(x, axes):
    n = group_size(axes)
    return a2a(jnp.broadcast_to(x.astype(BF)[None], (n,) + x.shape), axes)


def total_sum(mine, other):
    core = lax.axis_index("core")
    x = mine + exchanged(other, "core", 1).astype(F32)
    n = group_size(PLANE)
    x = a2a(x.astype(BF).reshape(n, x.shape[0] // n, x.shape[1]), PLANE)
    x = jnp.sum(x.astype(F32), axis=0)
    x = jnp.sum(spread(x, DEPTH).astype(F32), axis=0).astype(BF)
    x = spread(x, PLANE).reshape(mine.shape)
    other = exchanged(x, "core", 1)
    first = jnp.where(core == 0, x, other)
    second = jnp.where(core == 0, other, x)
    return jnp.concatenate([first, second], 0).astype(F32)


def body(video, conv_weight, norm_gain, qkv_weight, out_weight, cotangent, lengths):
    clips, frames, tile, channels = video.shape
    peers = clips * frames
    slabs = lax.axis_size(TIME)
    early = lax.ppermute(video, TIME, [(i, i + 1) for i in range(slabs - 1)])
    own = call(
        own_kernel,
        "own",
        jax.ShapeDtypeStruct(video.shape, F32),
        [VMEM] * 2,
        VMEM,
        video, conv_weight,
    )
    hidden = call(
        early_kernel,
        "early",
        jax.ShapeDtypeStruct(video.shape, BF),
        [VMEM] * 3,
        VMEM,
        own, early, conv_weight,
        cost_estimate=pl.CostEstimate(flops=30_000_000_000, bytes_accessed=1 << 22, transcendentals=0),
    )
    rows = jax.ShapeDtypeStruct((peers * tile, channels), BF)
    frame = a2a(hidden.reshape(peers, tile, channels), TILE).reshape(rows.shape)
    att = call(
        attend_kernel,
        "attend",
        rows,
        [VMEM] * 3,
        VMEM,
        frame, norm_gain.reshape(1, channels), qkv_weight,
        scratch_shapes=[pltpu.VMEM(rows.shape, BF)] * 3,
    )
    att = a2a(att.reshape(peers, tile, channels), TILE).reshape(rows.shape)
    places = jnp.stack([lax.axis_index(TIME), lax.axis_index("core")])
    split = jax.ShapeDtypeStruct((channels // 2, channels), F32)
    mine, other = call(
        grad_kernel,
        "grad",
        (split, jax.ShapeDtypeStruct(split.shape, BF)),
        [SMEM, SMEM, VMEM, VMEM],
        (VMEM, VMEM),
        places, lengths, att, cotangent,
        scratch_shapes=[pltpu.VMEM(rows.shape, BF), pltpu.VMEM((channels, channels), F32)],
    )
    out = call(
        out_kernel,
        "out",
        rows,
        [VMEM] * 3,
        VMEM,
        hidden.reshape(rows.shape), att, out_weight,
    )
    return out.reshape(video.shape), total_sum(mine, other)


def solution(mesh):
    fine = Mesh(mesh.devices.reshape(4, 2, 4, 2, 4), ("y", "core", "x", "zl", "clip"))
    part = P("clip", TIME, TILE, None)
    in_specs = (part, P(), P(), P(), P(), part, P("clip"))
    return jax.shard_map(body, mesh=fine, in_specs=in_specs, out_specs=(part, P()), check_vma=False)
```

time: 116 us -> 111 us (0.957)
  the two profiles are of different devices: /device:TPU:64 before, /device:TPU:1 now
where the time goes in v2:
time: 111 us; the launch traced here: 110 us
  blocking collectives  62.3 us (56%)
  waiting for transfers between devices  20.2 us (18%)
  starting transfers between devices  12.7 us (11%)
  Pallas kernels  10.2 us (9%)
  local copies, waits for them, and re-layouts  2.68 us (2%)
  other arithmetic  1.37 us (1%)
    all_to_all x4, blocking collectives, a2a(): return lax.all_to_all(x, axes, split_axis=0, concat_axis=0, tiled=True)  62.3 us
    all_to_all x1, waiting for transfers between devices, a2a(): return lax.all_to_all(x, axes, split_axis=0, concat_axis=0, tiled=True)  10.2 us
    pallas_call x5, Pallas kernels, call(): pl.pallas_call(kernel, out_shape=out_shape, in_specs=in_specs, out_specs=...  10.2 us
    ppermute x1, waiting for transfers between devices, body(): early = lax.ppermute(video, TIME, [(i, i + 1) for i in range(slabs - 1)])  8.42 us
    ppermute x1, starting transfers between devices, body(): early = lax.ppermute(video, TIME, [(i, i + 1) for i in range(slabs - 1)])  4.59 us
    ppermute x2, starting transfers between devices, exchanged(): return lax.ppermute(x, axis, [(i, i ^ by) for i in range(n)])  4.45 us
    all_to_all x1, starting transfers between devices, a2a(): return lax.all_to_all(x, axes, split_axis=0, concat_axis=0, tiled=True)  3.69 us
    unnamed x14, local copies, waits for them, and re-layouts  2.65 us
  transfers between devices with their start and end apart: 4, of which 3 were waited for; matrix products, arithmetic and copies ran while one was open for 0% of the time, Pallas kernels for 2%

profile of v2, /device:TPU:1, one launch (start us, length us, event | category | flops | bytes accessed | tf_op | source)
XLA Modules:
  0.0 110.2 jit_solution(10084977756561307861)
XLA Ops:
  0.6 4.6 %collective-permute-start = (bf16[4,2,128,512]{3,2,1,0:T(8,128)(2,1)}, bf16[4,2,128,512]{3,2,1,0:T(8,128)(2,1)S(1)}, u32[]{:S(2)}, u32[]{:S(2)}) collective-permute-start(bf16[4,2,128,512]{3,2,1,0:T(8,128)(2,1)} %video_ref.1), channel_id=1, source_target_pairs={{0,32},{32,64},{64,96},{96,128},{128,160},{160,192},{192,224},{1,3... | collective-permute-start | bytes 3145736 | tf_op jit(solution)/shard_map/ppermute | solution.py:180
  5.2 1.4 %copy-done.1 = bf16[3,512,512]{2,1,0:T(8,128)(2,1)S(1)} copy-done((bf16[3,512,512]{2,1,0:T(8,128)(2,1)S(1)}, bf16[3,512,512]{2,1,0:T(8,128)(2,1)}, u32[]{:S(2)}) %copy-start.1) | copy-done | bytes 1572888
  6.6 1.2 %copy-done.3 = bf16[4,2,128,512]{3,2,1,0:T(8,128)(2,1)S(1)} copy-done((bf16[4,2,128,512]{3,2,1,0:T(8,128)(2,1)S(1)}, bf16[4,2,128,512]{3,2,1,0:T(8,128)(2,1)}, u32[]{:S(2)}) %copy-start.3) | copy-done | bytes 1048600
  7.9 1.0 own.1.own_ref
  8.8 8.4 %collective-permute-done.early_ref = bf16[4,2,128,512]{3,2,1,0:T(8,128)(2,1)S(1)} collective-permute-done((bf16[4,2,128,512]{3,2,1,0:T(8,128)(2,1)}, bf16[4,2,128,512]{3,2,1,0:T(8,128)(2,1)S(1)}, u32[]{:S(2)}, u32[]{:S(2)}) %collective-permute-start) | collective-permute-done | bytes 1048608 | tf_op jit(solution)/shard_map/ppermute | solution.py:180
  17.3 1.0 early.1
  18.3 0.0 copy-start
  18.3 0.0 copy-start.5
  18.3 15.6 %all_to_all.25 = bf16[8,128,512]{2,1,0:T(8,128)(2,1)S(1)} all-to-all(bf16[8,128,512]{2,1,0:T(8,128)(2,1)S(1)} %bitcast.15), channel_id=1, replica_groups=mesh['y'=4,'core'=2,'x'=4,'zl'=2,'clip'=4] {'x','zl'}, dimensions={0} | all-to-all | bytes 2097152 | tf_op jit(solution)/shard_map/all_to_all | solution.py:20
  33.9 5.2 %attend.1 = bf16[1024,512]{1,0:T(8,128)(2,1)} custom-call(bf16[1024,512]{1,0:T(8,128)(2,1)S(1)} %bitcast.17, f32[1,512]{1,0:T(1,128)S(1)} %bitcast.18, bf16[512,1536]{1,0:T(8,128)(2,1)S(1)} %copy-done), custom_call_target="tpu_custom_call" | custom-call | tf_op jit(solution)/shard_map/attend/pallas_call | solution.py:31
  39.1 3.7 %all-to-all-start.1 = ((bf16[8,128,512]{2,1,0:T(8,128)(2,1)}), bf16[8,128,512]{2,1,0:T(8,128)(2,1)S(1)}, u32[]{:S(2)}, u32[]{:S(2)}) async-start(bf16[8,128,512]{2,1,0:T(8,128)(2,1)} %bitcast.4), calls=%async_computation.1 | async-start | bytes 2097152 | tf_op jit(solution)/shard_map/all_to_all | solution.py:20
  42.8 0.1 pad_add_fusion.place_ref
  42.9 10.2 %all-to-all-done.1 = bf16[8,128,512]{2,1,0:T(8,128)(2,1)S(1)} async-done(((bf16[8,128,512]{2,1,0:T(8,128)(2,1)}), bf16[8,128,512]{2,1,0:T(8,128)(2,1)S(1)}, u32[]{:S(2)}, u32[]{:S(2)}) %all-to-all-start.1) | async-done | bytes 1048608 | tf_op jit(solution)/shard_map/all_to_all | solution.py:20
  53.2 1.3 %grad.1 = (f32[256,512]{1,0:T(8,128)S(1)}, bf16[256,512]{1,0:T(8,128)(2,1)S(1)}) custom-call(s32[2]{0:T(128)S(1)} %pad_add_fusion.place_ref, s32[4]{0:T(128)S(1)} %copy-done.6, bf16[1024,512]{1,0:T(8,128)(2,1)S(1)} %bitcast.13, bf16[4,2,128,512]{3,2,1,0:T(8,128)(2,1)S(1)} %copy-done.2), custom_call_target="tpu_custom_call" | custom-call | tf_op jit(solution)/shard_map/grad/pallas_call | solution.py:31
  54.5 0.1 collective-permute-start.1
  54.6 1.5 %collective-permute-done.1 = bf16[256,512]{1,0:T(8,128)(2,1)S(1)} collective-permute-done((bf16[256,512]{1,0:T(8,128)(2,1)S(1)}, bf16[256,512]{1,0:T(8,128)(2,1)S(1)}, u32[]{:S(2)}, u32[]{:S(2)}) %collective-permute-start.1) | collective-permute-done | bytes 262176 | tf_op jit(solution)/shard_map/ppermute | solution.py:154
  56.1 0.1 add_convert_fusion
  56.2 22.4 %all_to_all.26 = bf16[16,16,512]{2,1,0:T(8,128)(2,1)S(1)} all-to-all(bf16[16,16,512]{2,1,0:T(8,128)(2,1)S(1)} %bitcast.21), channel_id=1, replica_groups=mesh['y'=4,'core'=2,'x'=4,'zl'=2,'clip'=4] {'y','x'}, dimensions={0} | all-to-all | bytes 524288 | tf_op jit(solution)/shard_map/all_to_all | solution.py:20
  78.6 14.1 %all_to_all.27 = bf16[8,16,512]{2,1,0:T(8,128)(2,1)S(1)} all-to-all(bf16[8,16,512]{2,1,0:T(8,128)(2,1)S(1)} %broadcast_in_dim.4), channel_id=1, replica_groups=mesh['y'=4,'core'=2,'x'=4,'zl'=2,'clip'=4] {'zl','clip'}, dimensions={0} | all-to-all | bytes 262144 | tf_op jit(solution)/shard_map/all_to_all | solution.py:20
  92.8 10.2 %all_to_all.28 = bf16[16,16,512]{2,1,0:T(8,128)(2,1)S(1)} all-to-all(bf16[16,16,512]{2,1,0:T(8,128)(2,1)S(1)} %broadcast_in_dim.5), channel_id=1, replica_groups=mesh['y'=4,'core'=2,'x'=4,'zl'=2,'clip'=4] {'y','x'}, dimensions={0} | all-to-all | bytes 524288 | tf_op jit(solution)/shard_map/all_to_all | solution.py:20
  103.0 4.4 %collective-permute-start.2 = (bf16[256,512]{1,0:T(8,128)(2,1)S(1)}, bf16[256,512]{1,0:T(8,128)(2,1)S(1)}, u32[]{:S(2)}, u32[]{:S(2)}) collective-permute-start(bf16[256,512]{1,0:T(8,128)(2,1)S(1)} %bitcast.20), channel_id=1, source_target_pairs={{0,32},{32,0},{1,33},{33,1},{2,34},{34,2},{3,35},{35,3},{4,36},{36... | collective-permute-start | bytes 786440 | tf_op jit(solution)/shard_map/ppermute | solution.py:154
  107.3 1.7 %out.1 = bf16[1024,512]{1,0:T(8,128)(2,1)} custom-call(bf16[1024,512]{1,0:T(8,128)(2,1)S(1)} %bitcast.16, bf16[1024,512]{1,0:T(8,128)(2,1)S(1)} %bitcast.14, bf16[512,512]{1,0:T(8,128)(2,1)S(1)} %copy-done.4), custom_call_target="tpu_custom_call" | custom-call | tf_op jit(solution)/shard_map/out/pallas_call | solution.py:31
  109.0 0.1 broadcast_select_fusion.1
  109.1 1.1 %maximum_convert_fusion = f32[512,512]{1,0:T(8,128)} fusion(bf16[256,512]{1,0:T(8,128)(2,1)S(1)} %get-tuple-element.7, bf16[256,512]{1,0:T(8,128)(2,1)S(1)} %get-tuple-element.6), kind=kLoop, calls=%fused_computation | loop fusion | flops 1048576 | bytes 1572864 | tf_op jit(solution)/shard_map/convert_element_type | solution.py:173
  (15 shorter events, 0.1 us)
Async XLA Ops:
  0.6 16.6 %collective-permute-start = (bf16[4,2,128,512]{3,2,1,0:T(8,128)(2,1)}, bf16[4,2,128,512]{3,2,1,0:T(8,128)(2,1)S(1)}, u32[]{:S(2)}, u32[]{:S(2)}) collective-permute-start(bf16[4,2,128,512]{3,2,1,0:T(8,128)(2,1)} %video_ref.1), channel_id=1, source_target_pairs={{0,32},{32,64},{64,96},{96,128},{128,160},{160,192},{192,224},{1,3... | collective-permute-start | bytes 3145736 | tf_op jit(solution)/shard_map/ppermute | solution.py:180
  5.2 1.4 %copy-start.1 = (bf16[3,512,512]{2,1,0:T(8,128)(2,1)S(1)}, bf16[3,512,512]{2,1,0:T(8,128)(2,1)}, u32[]{:S(2)}) copy-start(bf16[3,512,512]{2,1,0:T(8,128)(2,1)} %weight_ref.3) | copy-start | bytes 4718596
  6.6 1.2 %copy-start.3 = (bf16[4,2,128,512]{3,2,1,0:T(8,128)(2,1)S(1)}, bf16[4,2,128,512]{3,2,1,0:T(8,128)(2,1)}, u32[]{:S(2)}) copy-start(bf16[4,2,128,512]{3,2,1,0:T(8,128)(2,1)} %video_ref.1) | copy-start | bytes 3145732
  18.3 15.7 %copy-start = (bf16[512,1536]{1,0:T(8,128)(2,1)S(1)}, bf16[512,1536]{1,0:T(8,128)(2,1)}, u32[]{:S(2)}) copy-start(bf16[512,1536]{1,0:T(8,128)(2,1)} %qkv_ref.1) | copy-start | bytes 4718596
  18.3 15.7 %copy-start.5 = (f32[512]{0:T(512)S(1)}, f32[512]{0:T(512)}, u32[]{:S(2)}) copy-start(f32[512]{0:T(512)} %param.9) | copy-start | bytes 6148
  39.1 14.0 %copy-start.2 = (bf16[4,2,128,512]{3,2,1,0:T(8,128)(2,1)S(1)}, bf16[4,2,128,512]{3,2,1,0:T(8,128)(2,1)}, u32[]{:S(2)}) copy-start(bf16[4,2,128,512]{3,2,1,0:T(8,128)(2,1)} %cot_ref.1) | copy-start | bytes 3145732
  39.1 14.0 %copy-start.6 = (s32[4]{0:T(128)S(1)}, s32[4]{0:T(128)}, u32[]{:S(2)}) copy-start(s32[4]{0:T(128)} %lengths_ref.1) | copy-start | bytes 52
  39.1 14.0 %all-to-all-start.1 = ((bf16[8,128,512]{2,1,0:T(8,128)(2,1)}), bf16[8,128,512]{2,1,0:T(8,128)(2,1)S(1)}, u32[]{:S(2)}, u32[]{:S(2)}) async-start(bf16[8,128,512]{2,1,0:T(8,128)(2,1)} %bitcast.4), calls=%async_computation.1 | async-start | bytes 2097152 | tf_op jit(solution)/shard_map/all_to_all | solution.py:20
  54.5 1.6 %collective-permute-start.1 = (bf16[256,512]{1,0:T(8,128)(2,1)S(1)}, bf16[256,512]{1,0:T(8,128)(2,1)S(1)}, u32[]{:S(2)}, u32[]{:S(2)}) collective-permute-start(bf16[256,512]{1,0:T(8,128)(2,1)S(1)} %get-tuple-element.5), channel_id=1, source_target_pairs={{0,32},{32,0},{1,33},{33,1},{2,34},{34,2},{3,35},{35,3},{4,36},{36... | collective-permute-start | bytes 786440 | tf_op jit(solution)/shard_map/ppermute | solution.py:154
  56.1 51.2 %copy-start.4 = (bf16[512,512]{1,0:T(8,128)(2,1)S(1)}, bf16[512,512]{1,0:T(8,128)(2,1)}, u32[]{:S(2)}) copy-start(bf16[512,512]{1,0:T(8,128)(2,1)} %wo_ref.1) | copy-start | bytes 1572868
  103.0 6.0 %collective-permute-start.2 = (bf16[256,512]{1,0:T(8,128)(2,1)S(1)}, bf16[256,512]{1,0:T(8,128)(2,1)S(1)}, u32[]{:S(2)}, u32[]{:S(2)}) collective-permute-start(bf16[256,512]{1,0:T(8,128)(2,1)S(1)} %bitcast.20), channel_id=1, source_target_pairs={{0,32},{32,0},{1,33},{33,1},{2,34},{34,2},{3,35},{35,3},{4,36},{36... | collective-permute-start | bytes 786440 | tf_op jit(solution)/shard_map/ppermute | solution.py:154

commit v3 on v2

--- a/solution.py
+++ b/solution.py
@@ -65,16 +65,21 @@
     own_ref[:, 1] = (v1.astype(F32) + (dot(v1, 0) + dot(v0, 1))).reshape(own_ref[:, 0].shape)
 
 
-def early_kernel(own_ref, early_ref, weight_ref, out_ref):
+def early_kernel(own_ref, first_ref, second_ref, weight_ref, out_ref):
+    half = first_ref.shape[0]
+    shape = (half,) + own_ref.shape[2:]
+    rows = (shape[0] * shape[1], shape[2])
+
     def dot(rows, tap):
         return jnp.dot(rows, weight_ref[tap], preferred_element_type=F32)
 
-    rows = (own_ref.shape[0] * own_ref.shape[2], own_ref.shape[3])
-    e0, e1 = early_ref[:, 0].reshape(rows), early_ref[:, 1].reshape(rows)
-    h0 = own_ref[:, 0].reshape(rows) + (dot(e1, 1) + dot(e0, 2))
-    h1 = own_ref[:, 1].reshape(rows) + dot(e1, 2)
-    out_ref[:, 0] = h0.astype(BF).reshape(out_ref[:, 0].shape)
-    out_ref[:, 1] = h1.astype(BF).reshape(out_ref[:, 1].shape)
+    for i, early_ref in enumerate((first_ref, second_ref)):
+        at = pl.ds(i * half, half)
+        e0, e1 = early_ref[:, 0].reshape(rows), early_ref[:, 1].reshape(rows)
+        h0 = own_ref[at, 0].reshape(rows) + (dot(e1, 1) + dot(e0, 2))
+        h1 = own_ref[at, 1].reshape(rows) + dot(e1, 2)
+        out_ref[at, 0] = h0.astype(BF).reshape(shape)
+        out_ref[at, 1] = h1.astype(BF).reshape(shape)
 
 
 def attend_kernel(
@@ -177,7 +182,11 @@
     clips, frames, tile, channels = video.shape
     peers = clips * frames
     slabs = lax.axis_size(TIME)
-    early = lax.ppermute(video, TIME, [(i, i + 1) for i in range(slabs - 1)])
+    half = clips // 2
+    early = [lax.ppermute(video[:half], TIME, [(i, i + 1) for i in range(slabs - 1)])]
+    near = exchanged(video, "core", 1)[half:]
+    ahead = [(i, i + 2) for i in range(0, slabs - 2, 2)]
+    early.append(lax.ppermute(near, TIME, ahead + [(i, i) for i in range(1, slabs, 2)]))
     own = call(
         own_kernel,
         "own",
@@ -190,9 +199,9 @@
         early_kernel,
         "early",
         jax.ShapeDtypeStruct(video.shape, BF),
-        [VMEM] * 3,
-        VMEM,
-        own, early, conv_weight,
+        [VMEM] * 4,
+        VMEM,
+        own, *early, conv_weight,
         cost_estimate=pl.CostEstimate(flops=30_000_000_000, bytes_accessed=1 << 22, transcendentals=0),
     )
     rows = jax.ShapeDtypeStruct((peers * tile, channels), BF)

time: 111 us -> 106 us (0.955)
  blocking collectives: 62.3 us -> 52.6 us
  starting transfers between devices: 12.7 us -> 20.1 us
  waiting for transfers between devices: 20.2 us -> 17.9 us
    all_to_all x4, blocking collectives: 62.3 us -> 52.6 us  [a2a(): return lax.all_to_all(x, axes, split_axis=0, concat_axis=0, tiled=True)]
    ppermute x2 -> x3, starting transfers between devices: 4.45 us -> 13.8 us  [exchanged(): return lax.ppermute(x, axis, [(i, i ^ by) for i in range(n)])]
    ppermute x1 -> x2, waiting for transfers between devices: 8.42 us -> 6 us  [the longest x1 6 us: body(): lax.ppermute(video[:half], TIME, [(i, i + 1) for i in range(slabs - 1)])]
    ppermute x1 -> x2, starting transfers between devices: 4.59 us -> 2.61 us  [the longest x1 1.92 us: body(): lax.ppermute(video[:half], TIME, [(i, i + 1) for i in range(slabs - 1)])]
    unnamed x14, local copies, waits for them, and re-layouts: 2.65 us -> 1.43 us
    slice x0 -> x2, local copies, waits for them, and re-layouts: none -> 1.11 us  [the longest x1 1.08 us: body(): video[:half]]
  transfers between devices with their start and end apart: 4 -> 6, of which waited for: 3 -> 3; matrix products, arithmetic and copies ran while one was open for 0% -> 1% of each run, Pallas kernels for 2% -> 3%
where the time goes in v3:
time: 106 us
  blocking collectives  52.6 us (50%)
  starting transfers between devices  20.1 us (19%)
  waiting for transfers between devices  17.9 us (17%)
  Pallas kernels  10.2 us (10%)
  local copies, waits for them, and re-layouts  2.57 us (2%)
  other arithmetic  1.37 us (1%)
    all_to_all x4, blocking collectives, a2a(): return lax.all_to_all(x, axes, split_axis=0, concat_axis=0, tiled=True)  52.6 us
    ppermute x3, starting transfers between devices, exchanged(): return lax.ppermute(x, axis, [(i, i ^ by) for i in range(n)])  13.8 us
    all_to_all x1, waiting for transfers between devices, a2a(): return lax.all_to_all(x, axes, split_axis=0, concat_axis=0, tiled=True)  10.7 us
    pallas_call x5, Pallas kernels, call(): pl.pallas_call(kernel, out_shape=out_shape, in_specs=in_specs, out_specs=...  10.2 us
    ppermute x1, waiting for transfers between devices, body(): lax.ppermute(video[:half], TIME, [(i, i + 1) for i in range(slabs - 1)])  6 us
    all_to_all x1, starting transfers between devices, a2a(): return lax.all_to_all(x, axes, split_axis=0, concat_axis=0, tiled=True)  3.69 us
  transfers between devices with their start and end apart: 6, of which 3 were waited for; matrix products, arithmetic and copies ran while one was open for 1% of the time, Pallas kernels for 3%

profile of v3, /device:TPU:1, one launch (start us, length us, event | category | flops | bytes accessed | tf_op | source)
XLA Modules:
  0.0 105.5 jit_solution(4139196114826164098)
XLA Ops:
  0.6 3.3 %collective-permute-start.1 = (bf16[4,2,128,512]{3,2,1,0:T(8,128)(2,1)}, bf16[4,2,128,512]{3,2,1,0:T(8,128)(2,1)S(1)}, u32[]{:S(2)}, u32[]{:S(2)}) collective-permute-start(bf16[4,2,128,512]{3,2,1,0:T(8,128)(2,1)} %video_ref.1), channel_id=1, source_target_pairs={{0,32},{32,0},{1,33},{33,1},{2,34},{34,2},{3,35},{35,3},{4,36},{36... | collective-permute-start | bytes 3145736 | tf_op jit(solution)/shard_map/ppermute | solution.py:159
  4.0 1.1 %slice.6 = bf16[2,2,128,512]{3,2,1,0:T(8,128)(2,1)S(1)} slice(bf16[4,2,128,512]{3,2,1,0:T(8,128)(2,1)} %video_ref.1), slice={[0:2], [0:2], [0:128], [0:512]} | slice | bytes 1048576 | tf_op jit(solution)/shard_map/slice | solution.py:186
  5.0 1.9 %collective-permute-start = (bf16[2,2,128,512]{3,2,1,0:T(8,128)(2,1)S(1)}, bf16[2,2,128,512]{3,2,1,0:T(8,128)(2,1)S(1)}, u32[]{:S(2)}, u32[]{:S(2)}) collective-permute-start(bf16[2,2,128,512]{3,2,1,0:T(8,128)(2,1)S(1)} %slice.6), channel_id=1, source_target_pairs={{0,32},{32,64},{64,96},{96,128},{128,160},{160,192},{192,224},{1,3... | collective-permute-start | bytes 1572872 | tf_op jit(solution)/shard_map/ppermute | solution.py:186
  7.0 0.7 collective-permute-start.2
  7.8 1.4 %copy-done.2 = bf16[3,512,512]{2,1,0:T(8,128)(2,1)S(1)} copy-done((bf16[3,512,512]{2,1,0:T(8,128)(2,1)S(1)}, bf16[3,512,512]{2,1,0:T(8,128)(2,1)}, u32[]{:S(2)}) %copy-start.2) | copy-done | bytes 1572888
  9.2 1.0 own.1.own_ref
  10.1 6.0 %collective-permute-done.first_ref = bf16[2,2,128,512]{3,2,1,0:T(8,128)(2,1)S(1)} collective-permute-done((bf16[2,2,128,512]{3,2,1,0:T(8,128)(2,1)S(1)}, bf16[2,2,128,512]{3,2,1,0:T(8,128)(2,1)S(1)}, u32[]{:S(2)}, u32[]{:S(2)}) %collective-permute-start) | collective-permute-done | bytes 524320 | tf_op jit(solution)/shard_map/ppermute | solution.py:186
  16.1 1.0 early.1
  17.1 16.4 %all_to_all.25 = bf16[8,128,512]{2,1,0:T(8,128)(2,1)S(1)} all-to-all(bf16[8,128,512]{2,1,0:T(8,128)(2,1)S(1)} %bitcast.15), channel_id=1, replica_groups=mesh['y'=4,'core'=2,'x'=4,'zl'=2,'clip'=4] {'x','zl'}, dimensions={0} | all-to-all | bytes 2097152 | tf_op jit(solution)/shard_map/all_to_all | solution.py:20
  33.6 5.2 %attend.1 = bf16[1024,512]{1,0:T(8,128)(2,1)} custom-call(bf16[1024,512]{1,0:T(8,128)(2,1)S(1)} %bitcast.17, f32[1,512]{1,0:T(1,128)S(1)} %bitcast.18, bf16[512,1536]{1,0:T(8,128)(2,1)S(1)} %copy-done.1), custom_call_target="tpu_custom_call" | custom-call | tf_op jit(solution)/shard_map/attend/pallas_call | solution.py:31
  38.8 3.7 %all-to-all-start.1 = ((bf16[8,128,512]{2,1,0:T(8,128)(2,1)}), bf16[8,128,512]{2,1,0:T(8,128)(2,1)S(1)}, u32[]{:S(2)}, u32[]{:S(2)}) async-start(bf16[8,128,512]{2,1,0:T(8,128)(2,1)} %bitcast.4), calls=%async_computation.1 | async-start | bytes 2097152 | tf_op jit(solution)/shard_map/all_to_all | solution.py:20
  42.5 0.1 pad_add_fusion.place_ref
  42.5 10.7 %all-to-all-done.1 = bf16[8,128,512]{2,1,0:T(8,128)(2,1)S(1)} async-done(((bf16[8,128,512]{2,1,0:T(8,128)(2,1)}), bf16[8,128,512]{2,1,0:T(8,128)(2,1)S(1)}, u32[]{:S(2)}, u32[]{:S(2)}) %all-to-all-start.1) | async-done | bytes 1048608 | tf_op jit(solution)/shard_map/all_to_all | solution.py:20
  53.3 1.3 %grad.1 = (f32[256,512]{1,0:T(8,128)S(1)}, bf16[256,512]{1,0:T(8,128)(2,1)S(1)}) custom-call(s32[2]{0:T(128)S(1)} %pad_add_fusion.place_ref, s32[4]{0:T(128)S(1)} %copy-done.6, bf16[1024,512]{1,0:T(8,128)(2,1)S(1)} %bitcast.13, bf16[4,2,128,512]{3,2,1,0:T(8,128)(2,1)S(1)} %copy-done.3), custom_call_target="tpu_custom_call" | custom-call | tf_op jit(solution)/shard_map/grad/pallas_call | solution.py:31
  54.6 6.1 %collective-permute-start.3 = (bf16[256,512]{1,0:T(8,128)(2,1)S(1)}, bf16[256,512]{1,0:T(8,128)(2,1)S(1)}, u32[]{:S(2)}, u32[]{:S(2)}) collective-permute-start(bf16[256,512]{1,0:T(8,128)(2,1)S(1)} %get-tuple-element.5), channel_id=1, source_target_pairs={{0,32},{32,0},{1,33},{33,1},{2,34},{34,2},{3,35},{35,3},{4,36},{36... | collective-permute-start | bytes 786440 | tf_op jit(solution)/shard_map/ppermute | solution.py:159
  60.7 1.2 %collective-permute-done.3 = bf16[256,512]{1,0:T(8,128)(2,1)S(1)} collective-permute-done((bf16[256,512]{1,0:T(8,128)(2,1)S(1)}, bf16[256,512]{1,0:T(8,128)(2,1)S(1)}, u32[]{:S(2)}, u32[]{:S(2)}) %collective-permute-start.3) | collective-permute-done | bytes 262176 | tf_op jit(solution)/shard_map/ppermute | solution.py:159
  61.9 0.1 add_convert_fusion
  62.0 12.0 %all_to_all.26 = bf16[16,16,512]{2,1,0:T(8,128)(2,1)S(1)} all-to-all(bf16[16,16,512]{2,1,0:T(8,128)(2,1)S(1)} %bitcast.21), channel_id=1, replica_groups=mesh['y'=4,'core'=2,'x'=4,'zl'=2,'clip'=4] {'y','x'}, dimensions={0} | all-to-all | bytes 524288 | tf_op jit(solution)/shard_map/all_to_all | solution.py:20
  74.0 14.1 %all_to_all.27 = bf16[8,16,512]{2,1,0:T(8,128)(2,1)S(1)} all-to-all(bf16[8,16,512]{2,1,0:T(8,128)(2,1)S(1)} %broadcast_in_dim.4), channel_id=1, replica_groups=mesh['y'=4,'core'=2,'x'=4,'zl'=2,'clip'=4] {'zl','clip'}, dimensions={0} | all-to-all | bytes 262144 | tf_op jit(solution)/shard_map/all_to_all | solution.py:20
  88.2 10.2 %all_to_all.28 = bf16[16,16,512]{2,1,0:T(8,128)(2,1)S(1)} all-to-all(bf16[16,16,512]{2,1,0:T(8,128)(2,1)S(1)} %broadcast_in_dim.5), channel_id=1, replica_groups=mesh['y'=4,'core'=2,'x'=4,'zl'=2,'clip'=4] {'y','x'}, dimensions={0} | all-to-all | bytes 524288 | tf_op jit(solution)/shard_map/all_to_all | solution.py:20
  98.3 4.4 %collective-permute-start.4 = (bf16[256,512]{1,0:T(8,128)(2,1)S(1)}, bf16[256,512]{1,0:T(8,128)(2,1)S(1)}, u32[]{:S(2)}, u32[]{:S(2)}) collective-permute-start(bf16[256,512]{1,0:T(8,128)(2,1)S(1)} %bitcast.20), channel_id=1, source_target_pairs={{0,32},{32,0},{1,33},{33,1},{2,34},{34,2},{3,35},{35,3},{4,36},{36... | collective-permute-start | bytes 786440 | tf_op jit(solution)/shard_map/ppermute | solution.py:159
  102.7 1.7 %out.1 = bf16[1024,512]{1,0:T(8,128)(2,1)} custom-call(bf16[1024,512]{1,0:T(8,128)(2,1)S(1)} %bitcast.16, bf16[1024,512]{1,0:T(8,128)(2,1)S(1)} %bitcast.14, bf16[512,512]{1,0:T(8,128)(2,1)S(1)} %copy-done.4), custom_call_target="tpu_custom_call" | custom-call | tf_op jit(solution)/shard_map/out/pallas_call | solution.py:31
  104.4 0.1 broadcast_select_fusion.1
  104.4 1.1 %maximum_convert_fusion = f32[512,512]{1,0:T(8,128)} fusion(bf16[256,512]{1,0:T(8,128)(2,1)S(1)} %get-tuple-element.7, bf16[256,512]{1,0:T(8,128)(2,1)S(1)} %get-tuple-element.6), kind=kLoop, calls=%fused_computation | loop fusion | flops 1048576 | bytes 1572864 | tf_op jit(solution)/shard_map/convert_element_type | solution.py:178
  (21 shorter events, 0.2 us)
Async XLA Ops:
  0.6 7.1 %copy-start = (bf16[4,2,128,512]{3,2,1,0:T(8,128)(2,1)S(1)}, bf16[4,2,128,512]{3,2,1,0:T(8,128)(2,1)}, u32[]{:S(2)}) copy-start(bf16[4,2,128,512]{3,2,1,0:T(8,128)(2,1)} %video_ref.1) | copy-start | bytes 3145732
  0.6 6.3 %collective-permute-start.1 = (bf16[4,2,128,512]{3,2,1,0:T(8,128)(2,1)}, bf16[4,2,128,512]{3,2,1,0:T(8,128)(2,1)S(1)}, u32[]{:S(2)}, u32[]{:S(2)}) collective-permute-start(bf16[4,2,128,512]{3,2,1,0:T(8,128)(2,1)} %video_ref.1), channel_id=1, source_target_pairs={{0,32},{32,0},{1,33},{33,1},{2,34},{34,2},{3,35},{35,3},{4,36},{36... | collective-permute-start | bytes 3145736 | tf_op jit(solution)/shard_map/ppermute | solution.py:159
  5.0 11.1 %collective-permute-start = (bf16[2,2,128,512]{3,2,1,0:T(8,128)(2,1)S(1)}, bf16[2,2,128,512]{3,2,1,0:T(8,128)(2,1)S(1)}, u32[]{:S(2)}, u32[]{:S(2)}) collective-permute-start(bf16[2,2,128,512]{3,2,1,0:T(8,128)(2,1)S(1)} %slice.6), channel_id=1, source_target_pairs={{0,32},{32,64},{64,96},{96,128},{128,160},{160,192},{192,224},{1,3... | collective-permute-start | bytes 1572872 | tf_op jit(solution)/shard_map/ppermute | solution.py:186
  7.0 9.1 %collective-permute-start.2 = (bf16[2,2,128,512]{3,2,1,0:T(8,128)(2,1)S(1)}, bf16[2,2,128,512]{3,2,1,0:T(8,128)(2,1)S(1)}, u32[]{:S(2)}, u32[]{:S(2)}) collective-permute-start(bf16[2,2,128,512]{3,2,1,0:T(8,128)(2,1)S(1)} %slice.8), channel_id=1, source_target_pairs={{0,64},{64,128},{128,192},{32,32},{96,96},{160,160},{224,224},{1,6... | collective-permute-start | bytes 1572872 | tf_op jit(solution)/shard_map/ppermute | solution.py:189
  7.7 1.4 %copy-start.2 = (bf16[3,512,512]{2,1,0:T(8,128)(2,1)S(1)}, bf16[3,512,512]{2,1,0:T(8,128)(2,1)}, u32[]{:S(2)}) copy-start(bf16[3,512,512]{2,1,0:T(8,128)(2,1)} %weight_ref.3) | copy-start | bytes 4718596
  17.1 16.4 %copy-start.1 = (bf16[512,1536]{1,0:T(8,128)(2,1)S(1)}, bf16[512,1536]{1,0:T(8,128)(2,1)}, u32[]{:S(2)}) copy-start(bf16[512,1536]{1,0:T(8,128)(2,1)} %qkv_ref.1) | copy-start | bytes 4718596
  17.1 16.4 %copy-start.5 = (f32[512]{0:T(512)S(1)}, f32[512]{0:T(512)}, u32[]{:S(2)}) copy-start(f32[512]{0:T(512)} %param.9) | copy-start | bytes 6148
  38.7 14.5 %copy-start.3 = (bf16[4,2,128,512]{3,2,1,0:T(8,128)(2,1)S(1)}, bf16[4,2,128,512]{3,2,1,0:T(8,128)(2,1)}, u32[]{:S(2)}) copy-start(bf16[4,2,128,512]{3,2,1,0:T(8,128)(2,1)} %cot_ref.1) | copy-start | bytes 3145732
  38.8 14.5 %copy-start.6 = (s32[4]{0:T(128)S(1)}, s32[4]{0:T(128)}, u32[]{:S(2)}) copy-start(s32[4]{0:T(128)} %lengths_ref.1) | copy-start | bytes 52
  38.8 14.5 %all-to-all-start.1 = ((bf16[8,128,512]{2,1,0:T(8,128)(2,1)}), bf16[8,128,512]{2,1,0:T(8,128)(2,1)S(1)}, u32[]{:S(2)}, u32[]{:S(2)}) async-start(bf16[8,128,512]{2,1,0:T(8,128)(2,1)} %bitcast.4), calls=%async_computation.1 | async-start | bytes 2097152 | tf_op jit(solution)/shard_map/all_to_all | solution.py:20
  54.6 7.3 %collective-permute-start.3 = (bf16[256,512]{1,0:T(8,128)(2,1)S(1)}, bf16[256,512]{1,0:T(8,128)(2,1)S(1)}, u32[]{:S(2)}, u32[]{:S(2)}) collective-permute-start(bf16[256,512]{1,0:T(8,128)(2,1)S(1)} %get-tuple-element.5), channel_id=1, source_target_pairs={{0,32},{32,0},{1,33},{33,1},{2,34},{34,2},{3,35},{35,3},{4,36},{36... | collective-permute-start | bytes 786440 | tf_op jit(solution)/shard_map/ppermute | solution.py:159
  61.9 40.8 %copy-start.4 = (bf16[512,512]{1,0:T(8,128)(2,1)S(1)}, bf16[512,512]{1,0:T(8,128)(2,1)}, u32[]{:S(2)}) copy-start(bf16[512,512]{1,0:T(8,128)(2,1)} %wo_ref.1) | copy-start | bytes 1572868
  98.3 6.0 %collective-permute-start.4 = (bf16[256,512]{1,0:T(8,128)(2,1)S(1)}, bf16[256,512]{1,0:T(8,128)(2,1)S(1)}, u32[]{:S(2)}, u32[]{:S(2)}) collective-permute-start(bf16[256,512]{1,0:T(8,128)(2,1)S(1)} %bitcast.20), channel_id=1, source_target_pairs={{0,32},{32,0},{1,33},{33,1},{2,34},{34,2},{3,35},{35,3},{4,36},{36... | collective-permute-start | bytes 786440 | tf_op jit(solution)/shard_map/ppermute | solution.py:159

commit v4 on v3

--- a/solution.py
+++ b/solution.py
@@ -55,7 +55,16 @@
     )
 
 
-def own_kernel(video_ref, weight_ref, own_ref):
+def own_kernel(place_ref, video_ref, weight_ref, qkv_ref, own_ref, pair_ref, value_ref):
+    channels = video_ref.shape[-1]
+    pair_ref[...] = lax.dot_general(
+        qkv_ref[:, :channels],
+        qkv_ref[:, channels : 2 * channels],
+        (((1,), (1,)), ((), ())),
+        preferred_element_type=F32,
+    ).astype(BF)
+    value_ref[...] = qkv_ref[:, 2 * channels :]
+
     def dot(rows, tap):
         return jnp.dot(rows, weight_ref[tap], preferred_element_type=F32)
 
@@ -83,7 +92,7 @@
 
 
 def attend_kernel(
-    hidden_ref, gain_ref, qkv_ref, att_ref, q_s, k_s, v_s
+    hidden_ref, gain_ref, pair_ref, value_ref, att_ref, q_s, k_s, v_s
 ):
     pixels, channels = att_ref.shape
     step = 256
@@ -100,10 +109,9 @@
     ready = normed(0)
     for i in range(steps):
         following = normed(i + 1) if i + 1 < steps else None
-        for j, dst in enumerate((q_s, k_s, v_s)):
-            dst[chunk(i), :] = jnp.dot(
-                ready, qkv_ref[:, j * channels : (j + 1) * channels], preferred_element_type=F32
-            ).astype(BF)
+        q_s[chunk(i), :] = jnp.dot(ready, pair_ref[...], preferred_element_type=F32).astype(BF)
+        k_s[chunk(i), :] = ready
+        v_s[chunk(i), :] = jnp.dot(ready, value_ref[...], preferred_element_type=F32).astype(BF)
         ready = following
     scale = 1.4426950408889634 / channels**0.5
 
@@ -187,13 +195,14 @@
     near = exchanged(video, "core", 1)[half:]
     ahead = [(i, i + 2) for i in range(0, slabs - 2, 2)]
     early.append(lax.ppermute(near, TIME, ahead + [(i, i) for i in range(1, slabs, 2)]))
-    own = call(
+    places = jnp.stack([lax.axis_index(TIME), lax.axis_index("core")])
+    own, pair, value = call(
         own_kernel,
         "own",
-        jax.ShapeDtypeStruct(video.shape, F32),
-        [VMEM] * 2,
-        VMEM,
-        video, conv_weight,
+        (jax.ShapeDtypeStruct(video.shape, F32),) + (jax.ShapeDtypeStruct(out_weight.shape, BF),) * 2,
+        [SMEM] + [VMEM] * 3,
+        (VMEM,) * 3,
+        places, video, conv_weight, qkv_weight,
     )
     hidden = call(
         early_kernel,
@@ -210,13 +219,12 @@
         attend_kernel,
         "attend",
         rows,
-        [VMEM] * 3,
+        [VMEM] * 4,
         VMEM,
-        frame, norm_gain.reshape(1, channels), qkv_weight,
+        frame, norm_gain.reshape(1, channels), pair, value,
         scratch_shapes=[pltpu.VMEM(rows.shape, BF)] * 3,
     )
     att = a2a(att.reshape(peers, tile, channels), TILE).reshape(rows.shape)
-    places = jnp.stack([lax.axis_index(TIME), lax.axis_index("core")])
     split = jax.ShapeDtypeStruct((channels // 2, channels), F32)
     mine, other = call(
         grad_kernel,

time: 106 us -> 103 us (0.972)
  blocking collectives: 52.6 us -> 66.4 us
  waiting for transfers between devices: 17.9 us -> 4.83 us
  starting transfers between devices: 20.1 us -> 15.9 us
  local copies, waits for them, and re-layouts: 2.57 us -> 3.99 us
    all_to_all x4 -> x5, blocking collectives: 52.6 us -> 66.4 us  [a2a(): return lax.all_to_all(x, axes, split_axis=0, concat_axis=0, tiled=True)]
    all_to_all x1 -> x0, waiting for transfers between devices: 10.7 us -> none  [a2a(): return lax.all_to_all(x, axes, split_axis=0, concat_axis=0, tiled=True)]
    all_to_all x1 -> x0, starting transfers between devices: 3.69 us -> none  [a2a(): return lax.all_to_all(x, axes, split_axis=0, concat_axis=0, tiled=True)]
    ppermute x1, waiting for transfers between devices: 6 us -> 3.66 us  [body(): lax.ppermute(video[:half], TIME, [(i, i + 1) for i in range(slabs - 1)])]
    unnamed x14 -> x16, local copies, waits for them, and re-layouts: 1.43 us -> 2.85 us
  transfers between devices with their start and end apart: 6 -> 5, of which waited for: 3 -> 2; matrix products, arithmetic and copies ran while one was open for 1% -> 1% of each run, Pallas kernels for 3% -> 3%
where the time goes in v4:
time: 103 us
  blocking collectives  66.4 us (64%)
  starting transfers between devices  15.9 us (15%)
  Pallas kernels  9.53 us (9%)
  waiting for transfers between devices  4.83 us (5%)
  local copies, waits for them, and re-layouts  3.99 us (4%)
  other arithmetic  1.38 us (1%)
    all_to_all x5, blocking collectives, a2a(): return lax.all_to_all(x, axes, split_axis=0, concat_axis=0, tiled=True)  66.4 us
    ppermute x3, starting transfers between devices, exchanged(): return lax.ppermute(x, axis, [(i, i ^ by) for i in range(n)])  13.3 us
    pallas_call x5, Pallas kernels, call(): pl.pallas_call(kernel, out_shape=out_shape, in_specs=in_specs, out_specs=...  9.53 us
    ppermute x1, waiting for transfers between devices, body(): lax.ppermute(video[:half], TIME, [(i, i + 1) for i in range(slabs - 1)])  3.66 us
    unnamed x16, local copies, waits for them, and re-layouts  2.85 us
  transfers between devices with their start and end apart: 5, of which 2 were waited for; matrix products, arithmetic and copies ran while one was open for 1% of the time, Pallas kernels for 3%

profile of v4, /device:TPU:1, one launch (start us, length us, event | category | flops | bytes accessed | tf_op | source)
XLA Modules:
  0.0 102.8 jit_solution(9632548334928671615)
XLA Ops:
  0.6 3.3 %collective-permute-start.1 = (bf16[4,2,128,512]{3,2,1,0:T(8,128)(2,1)}, bf16[4,2,128,512]{3,2,1,0:T(8,128)(2,1)S(1)}, u32[]{:S(2)}, u32[]{:S(2)}) collective-permute-start(bf16[4,2,128,512]{3,2,1,0:T(8,128)(2,1)} %video_ref.1), channel_id=1, source_target_pairs={{0,32},{32,0},{1,33},{33,1},{2,34},{34,2},{3,35},{35,3},{4,36},{36... | collective-permute-start | bytes 3145736 | tf_op jit(solution)/shard_map/ppermute | solution.py:167
  4.0 1.1 %slice.6 = bf16[2,2,128,512]{3,2,1,0:T(8,128)(2,1)S(1)} slice(bf16[4,2,128,512]{3,2,1,0:T(8,128)(2,1)} %video_ref.1), slice={[0:2], [0:2], [0:128], [0:512]} | slice | bytes 1048576 | tf_op jit(solution)/shard_map/slice | solution.py:194
  5.0 1.9 %collective-permute-start = (bf16[2,2,128,512]{3,2,1,0:T(8,128)(2,1)S(1)}, bf16[2,2,128,512]{3,2,1,0:T(8,128)(2,1)S(1)}, u32[]{:S(2)}, u32[]{:S(2)}) collective-permute-start(bf16[2,2,128,512]{3,2,1,0:T(8,128)(2,1)S(1)} %slice.6), channel_id=1, source_target_pairs={{0,32},{32,64},{64,96},{96,128},{128,160},{160,192},{192,224},{1,3... | collective-permute-start | bytes 1572872 | tf_op jit(solution)/shard_map/ppermute | solution.py:194
  7.0 0.7 collective-permute-start.2
  7.7 0.1 pad_add_fusion.place_ref
  7.8 1.4 %copy-done.1 = bf16[512,1536]{1,0:T(8,128)(2,1)S(1)} copy-done((bf16[512,1536]{1,0:T(8,128)(2,1)S(1)}, bf16[512,1536]{1,0:T(8,128)(2,1)}, u32[]{:S(2)}) %copy-start.1) | copy-done | bytes 1572888
  9.2 1.4 %copy-done.2 = bf16[3,512,512]{2,1,0:T(8,128)(2,1)S(1)} copy-done((bf16[3,512,512]{2,1,0:T(8,128)(2,1)S(1)}, bf16[3,512,512]{2,1,0:T(8,128)(2,1)}, u32[]{:S(2)}) %copy-start.2) | copy-done | bytes 1572888
  10.6 1.8 %own.1 = (f32[4,2,128,512]{3,2,1,0:T(8,128)S(1)}, bf16[512,512]{1,0:T(8,128)(2,1)S(1)}, bf16[512,512]{1,0:T(8,128)(2,1)S(1)}) custom-call(s32[2]{0:T(128)S(1)} %pad_add_fusion.place_ref, bf16[4,2,128,512]{3,2,1,0:T(8,128)(2,1)S(1)} %copy-done, bf16[3,512,512]{2,1,0:T(8,128)(2,1)S(1)} %copy-done.2, bf16[512,1536]{1,0:T(8,128)(2,1)S(1)} %copy-done.1), custom_call_target="tpu_custom_call" | custom-call | tf_op jit(solution)/shard_map/own/pallas_call | solution.py:31
  12.5 3.7 %collective-permute-done.first_ref = bf16[2,2,128,512]{3,2,1,0:T(8,128)(2,1)S(1)} collective-permute-done((bf16[2,2,128,512]{3,2,1,0:T(8,128)(2,1)S(1)}, bf16[2,2,128,512]{3,2,1,0:T(8,128)(2,1)S(1)}, u32[]{:S(2)}, u32[]{:S(2)}) %collective-permute-start) | collective-permute-done | bytes 524320 | tf_op jit(solution)/shard_map/ppermute | solution.py:194
  16.1 1.0 early.1
  17.2 16.3 %all_to_all.25 = bf16[8,128,512]{2,1,0:T(8,128)(2,1)S(1)} all-to-all(bf16[8,128,512]{2,1,0:T(8,128)(2,1)S(1)} %bitcast.15), channel_id=1, replica_groups=mesh['y'=4,'core'=2,'x'=4,'zl'=2,'clip'=4] {'x','zl'}, dimensions={0} | all-to-all | bytes 2097152 | tf_op jit(solution)/shard_map/all_to_all | solution.py:20
  33.4 3.7 %attend.1 = bf16[1024,512]{1,0:T(8,128)(2,1)S(1)} custom-call(bf16[1024,512]{1,0:T(8,128)(2,1)S(1)} %bitcast.17, f32[1,512]{1,0:T(1,128)S(1)} %bitcast.19, bf16[512,512]{1,0:T(8,128)(2,1)S(1)} %get-tuple-element.8.pair_ref, bf16[512,512]{1,0:T(8,128)(2,1)S(1)} %get-tuple-element.9.value_ref), custom_call_target="tpu_custom_call" | custom-call | tf_op jit(solution)/shard_map/attend/pallas_call | solution.py:31
  37.1 14.0 %all_to_all.26 = bf16[8,128,512]{2,1,0:T(8,128)(2,1)S(1)} all-to-all(bf16[8,128,512]{2,1,0:T(8,128)(2,1)S(1)} %bitcast.18), channel_id=1, replica_groups=mesh['y'=4,'core'=2,'x'=4,'zl'=2,'clip'=4] {'x','zl'}, dimensions={0} | all-to-all | bytes 2097152 | tf_op jit(solution)/shard_map/all_to_all | solution.py:20
  51.2 1.3 %grad.1 = (f32[256,512]{1,0:T(8,128)S(1)}, bf16[256,512]{1,0:T(8,128)(2,1)S(1)}) custom-call(s32[2]{0:T(128)S(1)} %pad_add_fusion.place_ref, s32[4]{0:T(128)S(1)} %copy-done.7, bf16[1024,512]{1,0:T(8,128)(2,1)S(1)} %bitcast.13, bf16[4,2,128,512]{3,2,1,0:T(8,128)(2,1)S(1)} %copy-done.4), custom_call_target="tpu_custom_call" | custom-call | tf_op jit(solution)/shard_map/grad/pallas_call | solution.py:31
  52.5 5.6 %collective-permute-start.3 = (bf16[256,512]{1,0:T(8,128)(2,1)S(1)}, bf16[256,512]{1,0:T(8,128)(2,1)S(1)}, u32[]{:S(2)}, u32[]{:S(2)}) collective-permute-start(bf16[256,512]{1,0:T(8,128)(2,1)S(1)} %get-tuple-element.11), channel_id=1, source_target_pairs={{0,32},{32,0},{1,33},{33,1},{2,34},{34,2},{3,35},{35,3},{4,36},{36... | collective-permute-start | bytes 786440 | tf_op jit(solution)/shard_map/ppermute | solution.py:167
  58.1 1.2 %collective-permute-done.3 = bf16[256,512]{1,0:T(8,128)(2,1)S(1)} collective-permute-done((bf16[256,512]{1,0:T(8,128)(2,1)S(1)}, bf16[256,512]{1,0:T(8,128)(2,1)S(1)}, u32[]{:S(2)}, u32[]{:S(2)}) %collective-permute-start.3) | collective-permute-done | bytes 262176 | tf_op jit(solution)/shard_map/ppermute | solution.py:167
  59.3 0.1 add_convert_fusion
  59.4 11.8 %all_to_all.27 = bf16[16,16,512]{2,1,0:T(8,128)(2,1)S(1)} all-to-all(bf16[16,16,512]{2,1,0:T(8,128)(2,1)S(1)} %bitcast.22), channel_id=1, replica_groups=mesh['y'=4,'core'=2,'x'=4,'zl'=2,'clip'=4] {'y','x'}, dimensions={0} | all-to-all | bytes 524288 | tf_op jit(solution)/shard_map/all_to_all | solution.py:20
  71.2 14.1 %all_to_all.28 = bf16[8,16,512]{2,1,0:T(8,128)(2,1)S(1)} all-to-all(bf16[8,16,512]{2,1,0:T(8,128)(2,1)S(1)} %broadcast_in_dim.4), channel_id=1, replica_groups=mesh['y'=4,'core'=2,'x'=4,'zl'=2,'clip'=4] {'zl','clip'}, dimensions={0} | all-to-all | bytes 262144 | tf_op jit(solution)/shard_map/all_to_all | solution.py:20
  85.4 10.2 %all_to_all.29 = bf16[16,16,512]{2,1,0:T(8,128)(2,1)S(1)} all-to-all(bf16[16,16,512]{2,1,0:T(8,128)(2,1)S(1)} %broadcast_in_dim.5), channel_id=1, replica_groups=mesh['y'=4,'core'=2,'x'=4,'zl'=2,'clip'=4] {'y','x'}, dimensions={0} | all-to-all | bytes 524288 | tf_op jit(solution)/shard_map/all_to_all | solution.py:20
  95.6 4.4 %collective-permute-start.4 = (bf16[256,512]{1,0:T(8,128)(2,1)S(1)}, bf16[256,512]{1,0:T(8,128)(2,1)S(1)}, u32[]{:S(2)}, u32[]{:S(2)}) collective-permute-start(bf16[256,512]{1,0:T(8,128)(2,1)S(1)} %bitcast.21), channel_id=1, source_target_pairs={{0,32},{32,0},{1,33},{33,1},{2,34},{34,2},{3,35},{35,3},{4,36},{36... | collective-permute-start | bytes 786440 | tf_op jit(solution)/shard_map/ppermute | solution.py:167
  99.9 1.7 %out.1 = bf16[1024,512]{1,0:T(8,128)(2,1)} custom-call(bf16[1024,512]{1,0:T(8,128)(2,1)S(1)} %bitcast.16, bf16[1024,512]{1,0:T(8,128)(2,1)S(1)} %bitcast.14, bf16[512,512]{1,0:T(8,128)(2,1)S(1)} %copy-done.5), custom_call_target="tpu_custom_call" | custom-call | tf_op jit(solution)/shard_map/out/pallas_call | solution.py:31
  101.6 0.1 broadcast_select_fusion.1
  101.7 1.1 %maximum_convert_fusion = f32[512,512]{1,0:T(8,128)} fusion(bf16[256,512]{1,0:T(8,128)(2,1)S(1)} %get-tuple-element.13, bf16[256,512]{1,0:T(8,128)(2,1)S(1)} %get-tuple-element.12), kind=kLoop, calls=%fused_computation | loop fusion | flops 1048576 | bytes 1572864 | tf_op jit(solution)/shard_map/convert_element_type | solution.py:186
  (22 shorter events, 0.2 us)
Async XLA Ops:
  0.6 7.2 %copy-start = (bf16[4,2,128,512]{3,2,1,0:T(8,128)(2,1)S(1)}, bf16[4,2,128,512]{3,2,1,0:T(8,128)(2,1)}, u32[]{:S(2)}) copy-start(bf16[4,2,128,512]{3,2,1,0:T(8,128)(2,1)} %video_ref.1) | copy-start | bytes 3145732
  0.6 6.3 %collective-permute-start.1 = (bf16[4,2,128,512]{3,2,1,0:T(8,128)(2,1)}, bf16[4,2,128,512]{3,2,1,0:T(8,128)(2,1)S(1)}, u32[]{:S(2)}, u32[]{:S(2)}) collective-permute-start(bf16[4,2,128,512]{3,2,1,0:T(8,128)(2,1)} %video_ref.1), channel_id=1, source_target_pairs={{0,32},{32,0},{1,33},{33,1},{2,34},{34,2},{3,35},{35,3},{4,36},{36... | collective-permute-start | bytes 3145736 | tf_op jit(solution)/shard_map/ppermute | solution.py:167
  5.0 11.1 %collective-permute-start = (bf16[2,2,128,512]{3,2,1,0:T(8,128)(2,1)S(1)}, bf16[2,2,128,512]{3,2,1,0:T(8,128)(2,1)S(1)}, u32[]{:S(2)}, u32[]{:S(2)}) collective-permute-start(bf16[2,2,128,512]{3,2,1,0:T(8,128)(2,1)S(1)} %slice.6), channel_id=1, source_target_pairs={{0,32},{32,64},{64,96},{96,128},{128,160},{160,192},{192,224},{1,3... | collective-permute-start | bytes 1572872 | tf_op jit(solution)/shard_map/ppermute | solution.py:194
  7.0 9.1 %collective-permute-start.2 = (bf16[2,2,128,512]{3,2,1,0:T(8,128)(2,1)S(1)}, bf16[2,2,128,512]{3,2,1,0:T(8,128)(2,1)S(1)}, u32[]{:S(2)}, u32[]{:S(2)}) collective-permute-start(bf16[2,2,128,512]{3,2,1,0:T(8,128)(2,1)S(1)} %slice.8), channel_id=1, source_target_pairs={{0,64},{64,128},{128,192},{32,32},{96,96},{160,160},{224,224},{1,6... | collective-permute-start | bytes 1572872 | tf_op jit(solution)/shard_map/ppermute | solution.py:197
  7.8 1.4 %copy-start.1 = (bf16[512,1536]{1,0:T(8,128)(2,1)S(1)}, bf16[512,1536]{1,0:T(8,128)(2,1)}, u32[]{:S(2)}) copy-start(bf16[512,1536]{1,0:T(8,128)(2,1)} %qkv_ref.1) | copy-start | bytes 4718596
  9.2 1.4 %copy-start.2 = (bf16[3,512,512]{2,1,0:T(8,128)(2,1)S(1)}, bf16[3,512,512]{2,1,0:T(8,128)(2,1)}, u32[]{:S(2)}) copy-start(bf16[3,512,512]{2,1,0:T(8,128)(2,1)} %weight_ref.3) | copy-start | bytes 4718596
  10.6 5.5 %copy-start.3 = (bf16[3,512,512]{2,1,0:T(8,128)(2,1)S(1)}, bf16[3,512,512]{2,1,0:T(8,128)(2,1)}, u32[]{:S(2)}) copy-start(bf16[3,512,512]{2,1,0:T(8,128)(2,1)} %weight_ref.3) | copy-start | bytes 4718596
  17.2 16.3 %copy-start.6 = (f32[512]{0:T(512)S(1)}, f32[512]{0:T(512)}, u32[]{:S(2)}) copy-start(f32[512]{0:T(512)} %param.9) | copy-start | bytes 6148
  37.1 14.1 %copy-start.4 = (bf16[4,2,128,512]{3,2,1,0:T(8,128)(2,1)S(1)}, bf16[4,2,128,512]{3,2,1,0:T(8,128)(2,1)}, u32[]{:S(2)}) copy-start(bf16[4,2,128,512]{3,2,1,0:T(8,128)(2,1)} %cot_ref.1) | copy-start | bytes 3145732
  37.1 14.1 %copy-start.7 = (s32[4]{0:T(128)S(1)}, s32[4]{0:T(128)}, u32[]{:S(2)}) copy-start(s32[4]{0:T(128)} %lengths_ref.1) | copy-start | bytes 52
  52.5 6.7 %collective-permute-start.3 = (bf16[256,512]{1,0:T(8,128)(2,1)S(1)}, bf16[256,512]{1,0:T(8,128)(2,1)S(1)}, u32[]{:S(2)}, u32[]{:S(2)}) collective-permute-start(bf16[256,512]{1,0:T(8,128)(2,1)S(1)} %get-tuple-element.11), channel_id=1, source_target_pairs={{0,32},{32,0},{1,33},{33,1},{2,34},{34,2},{3,35},{35,3},{4,36},{36... | collective-permute-start | bytes 786440 | tf_op jit(solution)/shard_map/ppermute | solution.py:167
  59.3 40.7 %copy-start.5 = (bf16[512,512]{1,0:T(8,128)(2,1)S(1)}, bf16[512,512]{1,0:T(8,128)(2,1)}, u32[]{:S(2)}) copy-start(bf16[512,512]{1,0:T(8,128)(2,1)} %wo_ref.1) | copy-start | bytes 1572868
  95.6 6.0 %collective-permute-start.4 = (bf16[256,512]{1,0:T(8,128)(2,1)S(1)}, bf16[256,512]{1,0:T(8,128)(2,1)S(1)}, u32[]{:S(2)}, u32[]{:S(2)}) collective-permute-start(bf16[256,512]{1,0:T(8,128)(2,1)S(1)} %bitcast.21), channel_id=1, source_target_pairs={{0,32},{32,0},{1,33},{33,1},{2,34},{34,2},{3,35},{35,3},{4,36},{36... | collective-permute-start | bytes 786440 | tf_op jit(solution)/shard_map/ppermute | solution.py:167

commit v5 on v4

--- a/solution.py
+++ b/solution.py
@@ -1,3 +1,5 @@
+import functools
+
 import jax
 import jax.numpy as jnp
 from jax import lax
@@ -74,21 +76,20 @@
     own_ref[:, 1] = (v1.astype(F32) + (dot(v1, 0) + dot(v0, 1))).reshape(own_ref[:, 0].shape)
 
 
-def early_kernel(own_ref, first_ref, second_ref, weight_ref, out_ref):
-    half = first_ref.shape[0]
-    shape = (half,) + own_ref.shape[2:]
+def early_kernel(start, own_ref, early_ref, weight_ref, *refs):
+    out_ref = refs[-1]
+    shape = (early_ref.shape[0],) + early_ref.shape[2:]
     rows = (shape[0] * shape[1], shape[2])
+    at = pl.ds(start, shape[0])
 
     def dot(rows, tap):
         return jnp.dot(rows, weight_ref[tap], preferred_element_type=F32)
 
-    for i, early_ref in enumerate((first_ref, second_ref)):
-        at = pl.ds(i * half, half)
-        e0, e1 = early_ref[:, 0].reshape(rows), early_ref[:, 1].reshape(rows)
-        h0 = own_ref[at, 0].reshape(rows) + (dot(e1, 1) + dot(e0, 2))
-        h1 = own_ref[at, 1].reshape(rows) + dot(e1, 2)
-        out_ref[at, 0] = h0.astype(BF).reshape(shape)
-        out_ref[at, 1] = h1.astype(BF).reshape(shape)
+    e0, e1 = early_ref[:, 0].reshape(rows), early_ref[:, 1].reshape(rows)
+    h0 = own_ref[at, 0].reshape(rows) + (dot(e1, 1) + dot(e0, 2))
+    h1 = own_ref[at, 1].reshape(rows) + dot(e1, 2)
+    out_ref[at, 0] = h0.astype(BF).reshape(shape)
+    out_ref[at, 1] = h1.astype(BF).reshape(shape)
 
 
 def attend_kernel(
@@ -139,20 +140,21 @@
             att_ref[chunk(t - 2), :] = attended(*stages[1].pop(t - 2))
 
 
-def grad_kernel(place_ref, lengths_ref, att_ref, cot_ref, mine_ref, other_ref, cot_s, g_s):
-    clips, frames, tile, channels = cot_ref.shape
+def grad_kernel(place_ref, lengths_ref, att_ref, cot_ref, grad_ref, live_ref, *, swap):
+    clips, frames, tile = cot_ref.shape[:3]
     for clip in range(clips):
         for frame in range(frames):
             live = place_ref[0] * frames + frame < lengths_ref[clip]
             rows = pl.ds((clip * frames + frame) * tile, tile)
-            cot_s[rows, :] = cot_ref[clip, frame] * jnp.where(live, 1.0, 0.0).astype(BF)
-    g_s[...] = lax.dot_general(
-        att_ref[...], cot_s[...], (((0,), (0,)), ((), ())), preferred_element_type=F32
-    )
-    core = place_ref[1]
-    split = channels // 2
-    mine_ref[...] = g_s[pl.ds(pl.multiple_of(core * split, split), split), :]
-    other_ref[...] = g_s[pl.ds(pl.multiple_of((1 - core) * split, split), split), :].astype(BF)
+            live_ref[rows, :] = cot_ref[clip, frame] * jnp.where(live, 1.0, 0.0).astype(BF)
+    split = grad_ref.shape[0]
+    half = 1 - place_ref[1] if swap else place_ref[1]
+    grad_ref[...] = lax.dot_general(
+        att_ref[:, pl.ds(pl.multiple_of(half * split, split), split)],
+        live_ref[...],
+        (((0,), (0,)), ((), ())),
+        preferred_element_type=F32,
+    ).astype(grad_ref.dtype)
 
 
 def out_kernel(hidden_ref, att_ref, wo_ref, out_ref):
@@ -204,15 +206,19 @@
         (VMEM,) * 3,
         places, video, conv_weight, qkv_weight,
     )
-    hidden = call(
-        early_kernel,
-        "early",
-        jax.ShapeDtypeStruct(video.shape, BF),
-        [VMEM] * 4,
-        VMEM,
-        own, *early, conv_weight,
-        cost_estimate=pl.CostEstimate(flops=30_000_000_000, bytes_accessed=1 << 22, transcendentals=0),
-    )
+    hidden = ()
+    for i in range(2):
+        hidden = call(
+            functools.partial(early_kernel, i * half),
+            "early%d" % i,
+            jax.ShapeDtypeStruct(video.shape, BF),
+            [VMEM] * (3 + i),
+            VMEM,
+            own, early[i], conv_weight, *hidden,
+            input_output_aliases={3: 0} if i else {},
+        )
+        hidden = (hidden,)
+    (hidden,) = hidden
     rows = jax.ShapeDtypeStruct((peers * tile, channels), BF)
     frame = a2a(hidden.reshape(peers, tile, channels), TILE).reshape(rows.shape)
     att = call(
@@ -225,15 +231,18 @@
         scratch_shapes=[pltpu.VMEM(rows.shape, BF)] * 3,
     )
     att = a2a(att.reshape(peers, tile, channels), TILE).reshape(rows.shape)
-    split = jax.ShapeDtypeStruct((channels // 2, channels), F32)
-    mine, other = call(
-        grad_kernel,
-        "grad",
-        (split, jax.ShapeDtypeStruct(split.shape, BF)),
-        [SMEM, SMEM, VMEM, VMEM],
-        (VMEM, VMEM),
-        places, lengths, att, cotangent,
-        scratch_shapes=[pltpu.VMEM(rows.shape, BF), pltpu.VMEM((channels, channels), F32)],
+    other, mine = (
+        call(
+            functools.partial(grad_kernel, swap=swap),
+            "other" if swap else "mine",
+            jax.ShapeDtypeStruct((channels // 2, channels), BF if swap else F32),
+            [SMEM, SMEM, VMEM, VMEM],
+            VMEM,
+            places, lengths, att, cotangent,
+            scratch_shapes=[pltpu.VMEM(rows.shape, BF)],
+            cost_estimate=pl.CostEstimate(flops=1 << 28, bytes_accessed=1 << 21, transcendentals=0),
+        )
+        for swap in (True, False)
     )
     out = call(
         out_kernel,

time: 103 us -> 102 us (level)
  waiting for transfers between devices: 4.83 us -> 1.24 us
  starting transfers between devices: 15.9 us -> 17.6 us
    ppermute x1, waiting for transfers between devices: 3.66 us -> 1.09 us  [body(): lax.ppermute(video[:half], TIME, [(i, i + 1) for i in range(slabs - 1)])]
    pallas_call x5 -> x7, Pallas kernels: 9.53 us -> 10.4 us  [call(): pl.pallas_call(kernel, out_shape=out_shape, in_specs=in_specs, out_specs=...]
  transfers between devices with their start and end apart: 5 -> 5, of which waited for: 2 -> 2; matrix products, arithmetic and copies ran while one was open for 1% -> 2% of each run, Pallas kernels for 3% -> 5%
where the time goes in v5:
time: 102 us
  blocking collectives  65.7 us (64%)
  starting transfers between devices  17.6 us (17%)
  Pallas kernels  10.4 us (10%)
  local copies, waits for them, and re-layouts  4.6 us (5%)
  other arithmetic  1.37 us (1%)
  waiting for transfers between devices  1.24 us (1%)
    all_to_all x5, blocking collectives, a2a(): return lax.all_to_all(x, axes, split_axis=0, concat_axis=0, tiled=True)  65.7 us
    ppermute x3, starting transfers between devices, exchanged(): return lax.ppermute(x, axis, [(i, i ^ by) for i in range(n)])  14 us
    pallas_call x7, Pallas kernels, call(): pl.pallas_call(kernel, out_shape=out_shape, in_specs=in_specs, out_specs=...  10.4 us
    unnamed x16, local copies, waits for them, and re-layouts  2.67 us
  transfers between devices with their start and end apart: 5, of which 2 were waited for; matrix products, arithmetic and copies ran while one was open for 2% of the time, Pallas kernels for 5%

profile of v5, /device:TPU:1, one launch (start us, length us, event | category | flops | bytes accessed | tf_op | source)
XLA Modules:
  0.0 101.7 jit_solution(2840068724015097320)
XLA Ops:
  0.6 3.3 %collective-permute-start = (bf16[4,2,128,512]{3,2,1,0:T(8,128)(2,1)}, bf16[4,2,128,512]{3,2,1,0:T(8,128)(2,1)S(1)}, u32[]{:S(2)}, u32[]{:S(2)}) collective-permute-start(bf16[4,2,128,512]{3,2,1,0:T(8,128)(2,1)} %video_ref.1), channel_id=1, source_target_pairs={{0,32},{32,0},{1,33},{33,1},{2,34},{34,2},{3,35},{35,3},{4,36},{36... | collective-permute-start | bytes 3145736 | tf_op jit(solution)/shard_map/ppermute | solution.py:169
  4.0 1.1 %slice.7 = bf16[2,2,128,512]{3,2,1,0:T(8,128)(2,1)S(1)} slice(bf16[4,2,128,512]{3,2,1,0:T(8,128)(2,1)} %video_ref.1), slice={[0:2], [0:2], [0:128], [0:512]} | slice | bytes 1048576 | tf_op jit(solution)/shard_map/slice | solution.py:196
  5.0 1.9 %collective-permute-start.2 = (bf16[2,2,128,512]{3,2,1,0:T(8,128)(2,1)S(1)}, bf16[2,2,128,512]{3,2,1,0:T(8,128)(2,1)S(1)}, u32[]{:S(2)}, u32[]{:S(2)}) collective-permute-start(bf16[2,2,128,512]{3,2,1,0:T(8,128)(2,1)S(1)} %slice.7), channel_id=1, source_target_pairs={{0,32},{32,64},{64,96},{96,128},{128,160},{160,192},{192,224},{1,3... | collective-permute-start | bytes 1572872 | tf_op jit(solution)/shard_map/ppermute | solution.py:196
  7.0 0.8 slice.8
  7.8 1.7 %collective-permute-start.1 = (bf16[2,2,128,512]{3,2,1,0:T(8,128)(2,1)}, bf16[2,2,128,512]{3,2,1,0:T(8,128)(2,1)S(1)}, u32[]{:S(2)}, u32[]{:S(2)}) collective-permute-start(bf16[2,2,128,512]{3,2,1,0:T(8,128)(2,1)} %slice.8), channel_id=1, source_target_pairs={{0,64},{64,128},{128,192},{32,32},{96,96},{160,160},{224,224},{1,6... | collective-permute-start | bytes 1572872 | tf_op jit(solution)/shard_map/ppermute | solution.py:199
  9.6 1.2 %copy-done.3 = bf16[4,2,128,512]{3,2,1,0:T(8,128)(2,1)S(1)} copy-done((bf16[4,2,128,512]{3,2,1,0:T(8,128)(2,1)S(1)}, bf16[4,2,128,512]{3,2,1,0:T(8,128)(2,1)}, u32[]{:S(2)}) %copy-start.3) | copy-done | bytes 1048600
  10.8 1.4 %copy-done.4 = bf16[512,1536]{1,0:T(8,128)(2,1)S(1)} copy-done((bf16[512,1536]{1,0:T(8,128)(2,1)S(1)}, bf16[512,1536]{1,0:T(8,128)(2,1)}, u32[]{:S(2)}) %copy-start.4) | copy-done | bytes 1572888
  12.2 1.8 %own.1 = (f32[4,2,128,512]{3,2,1,0:T(8,128)S(1)}, bf16[512,512]{1,0:T(8,128)(2,1)S(1)}, bf16[512,512]{1,0:T(8,128)(2,1)S(1)}) custom-call(s32[2]{0:T(128)S(1)} %pad_add_fusion.place_ref, bf16[4,2,128,512]{3,2,1,0:T(8,128)(2,1)S(1)} %copy-done.3, bf16[3,512,512]{2,1,0:T(8,128)(2,1)S(1)} %copy-done, bf16[512,1536]{1,0:T(8,128)(2,1)S(1)} %copy-done.4), custom_call_target="tpu_custom_call" | custom-call | tf_op jit(solution)/shard_map/own/pallas_call | solution.py:33
  14.1 1.1 %collective-permute-done.2.early_ref = bf16[2,2,128,512]{3,2,1,0:T(8,128)(2,1)S(1)} collective-permute-done((bf16[2,2,128,512]{3,2,1,0:T(8,128)(2,1)S(1)}, bf16[2,2,128,512]{3,2,1,0:T(8,128)(2,1)S(1)}, u32[]{:S(2)}, u32[]{:S(2)}) %collective-permute-start.2) | collective-permute-done | bytes 524320 | tf_op jit(solution)/shard_map/ppermute | solution.py:196
  15.2 0.6 early0.1.refs_0_
  15.8 0.6 early1.1
  16.4 15.8 %all_to_all.25 = bf16[8,128,512]{2,1,0:T(8,128)(2,1)S(1)} all-to-all(bf16[8,128,512]{2,1,0:T(8,128)(2,1)S(1)} %bitcast.16), channel_id=1, replica_groups=mesh['y'=4,'core'=2,'x'=4,'zl'=2,'clip'=4] {'x','zl'}, dimensions={0} | all-to-all | bytes 2097152 | tf_op jit(solution)/shard_map/all_to_all | solution.py:22
  32.2 3.7 %attend.1 = bf16[1024,512]{1,0:T(8,128)(2,1)S(1)} custom-call(bf16[1024,512]{1,0:T(8,128)(2,1)S(1)} %bitcast.18, f32[1,512]{1,0:T(1,128)S(1)} %bitcast.20, bf16[512,512]{1,0:T(8,128)(2,1)S(1)} %get-tuple-element.6.pair_ref, bf16[512,512]{1,0:T(8,128)(2,1)S(1)} %get-tuple-element.7.value_ref), custom_call_target="tpu_custom_call" | custom-call | tf_op jit(solution)/shard_map/attend/pallas_call | solution.py:33
  35.9 13.1 %all_to_all.26 = bf16[8,128,512]{2,1,0:T(8,128)(2,1)S(1)} all-to-all(bf16[8,128,512]{2,1,0:T(8,128)(2,1)S(1)} %bitcast.19), channel_id=1, replica_groups=mesh['y'=4,'core'=2,'x'=4,'zl'=2,'clip'=4] {'x','zl'}, dimensions={0} | all-to-all | bytes 2097152 | tf_op jit(solution)/shard_map/all_to_all | solution.py:22
  49.0 1.0 other.1
  50.1 6.3 %collective-permute-start.3 = (bf16[256,512]{1,0:T(8,128)(2,1)S(1)}, bf16[256,512]{1,0:T(8,128)(2,1)S(1)}, u32[]{:S(2)}, u32[]{:S(2)}) collective-permute-start(bf16[256,512]{1,0:T(8,128)(2,1)S(1)} %other.1), channel_id=1, source_target_pairs={{0,32},{32,0},{1,33},{33,1},{2,34},{34,2},{3,35},{35,3},{4,36},{36... | collective-permute-start | bytes 786440 | tf_op jit(solution)/shard_map/ppermute | solution.py:169
  56.4 1.0 mine.1
  57.4 0.1 collective-permute-done.3
  57.6 12.4 %all_to_all.27 = bf16[16,16,512]{2,1,0:T(8,128)(2,1)S(1)} all-to-all(bf16[16,16,512]{2,1,0:T(8,128)(2,1)S(1)} %bitcast.23), channel_id=1, replica_groups=mesh['y'=4,'core'=2,'x'=4,'zl'=2,'clip'=4] {'y','x'}, dimensions={0} | all-to-all | bytes 524288 | tf_op jit(solution)/shard_map/all_to_all | solution.py:22
  70.1 14.1 %all_to_all.28 = bf16[8,16,512]{2,1,0:T(8,128)(2,1)S(1)} all-to-all(bf16[8,16,512]{2,1,0:T(8,128)(2,1)S(1)} %broadcast_in_dim.4), channel_id=1, replica_groups=mesh['y'=4,'core'=2,'x'=4,'zl'=2,'clip'=4] {'zl','clip'}, dimensions={0} | all-to-all | bytes 262144 | tf_op jit(solution)/shard_map/all_to_all | solution.py:22
  84.3 10.2 %all_to_all.29 = bf16[16,16,512]{2,1,0:T(8,128)(2,1)S(1)} all-to-all(bf16[16,16,512]{2,1,0:T(8,128)(2,1)S(1)} %broadcast_in_dim.5), channel_id=1, replica_groups=mesh['y'=4,'core'=2,'x'=4,'zl'=2,'clip'=4] {'y','x'}, dimensions={0} | all-to-all | bytes 524288 | tf_op jit(solution)/shard_map/all_to_all | solution.py:22
  94.4 4.4 %collective-permute-start.4 = (bf16[256,512]{1,0:T(8,128)(2,1)S(1)}, bf16[256,512]{1,0:T(8,128)(2,1)S(1)}, u32[]{:S(2)}, u32[]{:S(2)}) collective-permute-start(bf16[256,512]{1,0:T(8,128)(2,1)S(1)} %bitcast.22), channel_id=1, source_target_pairs={{0,32},{32,0},{1,33},{33,1},{2,34},{34,2},{3,35},{35,3},{4,36},{36... | collective-permute-start | bytes 786440 | tf_op jit(solution)/shard_map/ppermute | solution.py:169
  98.8 1.7 %out.1 = bf16[1024,512]{1,0:T(8,128)(2,1)} custom-call(bf16[1024,512]{1,0:T(8,128)(2,1)S(1)} %bitcast.17, bf16[1024,512]{1,0:T(8,128)(2,1)S(1)} %bitcast.15, bf16[512,512]{1,0:T(8,128)(2,1)S(1)} %copy-done.5), custom_call_target="tpu_custom_call" | custom-call | tf_op jit(solution)/shard_map/out/pallas_call | solution.py:33
  100.5 1.1 %maximum_convert_fusion = f32[512,512]{1,0:T(8,128)} fusion(bf16[256,512]{1,0:T(8,128)(2,1)S(1)} %get-tuple-element.9, bf16[256,512]{1,0:T(8,128)(2,1)S(1)} %get-tuple-element.8), kind=kLoop, calls=%fused_computation | loop fusion | flops 1048576 | bytes 1572864 | tf_op jit(solution)/shard_map/convert_element_type | solution.py:188
  (24 shorter events, 0.3 us)
Async XLA Ops:
  0.6 9.0 %copy-start = (bf16[3,512,512]{2,1,0:T(8,128)(2,1)S(1)}, bf16[3,512,512]{2,1,0:T(8,128)(2,1)}, u32[]{:S(2)}) copy-start(bf16[3,512,512]{2,1,0:T(8,128)(2,1)} %weight_ref.5) | copy-start | bytes 4718596
  0.6 6.3 %collective-permute-start = (bf16[4,2,128,512]{3,2,1,0:T(8,128)(2,1)}, bf16[4,2,128,512]{3,2,1,0:T(8,128)(2,1)S(1)}, u32[]{:S(2)}, u32[]{:S(2)}) collective-permute-start(bf16[4,2,128,512]{3,2,1,0:T(8,128)(2,1)} %video_ref.1), channel_id=1, source_target_pairs={{0,32},{32,0},{1,33},{33,1},{2,34},{34,2},{3,35},{35,3},{4,36},{36... | collective-permute-start | bytes 3145736 | tf_op jit(solution)/shard_map/ppermute | solution.py:169
  5.0 10.1 %collective-permute-start.2 = (bf16[2,2,128,512]{3,2,1,0:T(8,128)(2,1)S(1)}, bf16[2,2,128,512]{3,2,1,0:T(8,128)(2,1)S(1)}, u32[]{:S(2)}, u32[]{:S(2)}) collective-permute-start(bf16[2,2,128,512]{3,2,1,0:T(8,128)(2,1)S(1)} %slice.7), channel_id=1, source_target_pairs={{0,32},{32,64},{64,96},{96,128},{128,160},{160,192},{192,224},{1,3... | collective-permute-start | bytes 1572872 | tf_op jit(solution)/shard_map/ppermute | solution.py:196
  7.8 7.9 %collective-permute-start.1 = (bf16[2,2,128,512]{3,2,1,0:T(8,128)(2,1)}, bf16[2,2,128,512]{3,2,1,0:T(8,128)(2,1)S(1)}, u32[]{:S(2)}, u32[]{:S(2)}) collective-permute-start(bf16[2,2,128,512]{3,2,1,0:T(8,128)(2,1)} %slice.8), channel_id=1, source_target_pairs={{0,64},{64,128},{128,192},{32,32},{96,96},{160,160},{224,224},{1,6... | collective-permute-start | bytes 1572872 | tf_op jit(solution)/shard_map/ppermute | solution.py:199
  9.6 1.2 %copy-start.3 = (bf16[4,2,128,512]{3,2,1,0:T(8,128)(2,1)S(1)}, bf16[4,2,128,512]{3,2,1,0:T(8,128)(2,1)}, u32[]{:S(2)}) copy-start(bf16[4,2,128,512]{3,2,1,0:T(8,128)(2,1)} %video_ref.1) | copy-start | bytes 3145732
  10.8 1.4 %copy-start.4 = (bf16[512,1536]{1,0:T(8,128)(2,1)S(1)}, bf16[512,1536]{1,0:T(8,128)(2,1)}, u32[]{:S(2)}) copy-start(bf16[512,1536]{1,0:T(8,128)(2,1)} %qkv_ref.1) | copy-start | bytes 4718596
  12.2 2.9 %copy-start.1 = (bf16[3,512,512]{2,1,0:T(8,128)(2,1)S(1)}, bf16[3,512,512]{2,1,0:T(8,128)(2,1)}, u32[]{:S(2)}) copy-start(bf16[3,512,512]{2,1,0:T(8,128)(2,1)} %weight_ref.5) | copy-start | bytes 4718596
  16.3 15.8 %copy-start.6 = (f32[512]{0:T(512)S(1)}, f32[512]{0:T(512)}, u32[]{:S(2)}) copy-start(f32[512]{0:T(512)} %param.9) | copy-start | bytes 6148
  35.9 13.2 %copy-start.2 = (bf16[4,2,128,512]{3,2,1,0:T(8,128)(2,1)S(1)}, bf16[4,2,128,512]{3,2,1,0:T(8,128)(2,1)}, u32[]{:S(2)}) copy-start(bf16[4,2,128,512]{3,2,1,0:T(8,128)(2,1)} %cot_ref.3) | copy-start | bytes 3145732
  35.9 13.2 %copy-start.7 = (s32[4]{0:T(128)S(1)}, s32[4]{0:T(128)}, u32[]{:S(2)}) copy-start(s32[4]{0:T(128)} %lengths_ref.3) | copy-start | bytes 52
  50.1 7.5 %collective-permute-start.3 = (bf16[256,512]{1,0:T(8,128)(2,1)S(1)}, bf16[256,512]{1,0:T(8,128)(2,1)S(1)}, u32[]{:S(2)}, u32[]{:S(2)}) collective-permute-start(bf16[256,512]{1,0:T(8,128)(2,1)S(1)} %other.1), channel_id=1, source_target_pairs={{0,32},{32,0},{1,33},{33,1},{2,34},{34,2},{3,35},{35,3},{4,36},{36... | collective-permute-start | bytes 786440 | tf_op jit(solution)/shard_map/ppermute | solution.py:169
  57.4 41.4 %copy-start.5 = (bf16[512,512]{1,0:T(8,128)(2,1)S(1)}, bf16[512,512]{1,0:T(8,128)(2,1)}, u32[]{:S(2)}) copy-start(bf16[512,512]{1,0:T(8,128)(2,1)} %wo_ref.1) | copy-start | bytes 1572868
  94.4 6.0 %collective-permute-start.4 = (bf16[256,512]{1,0:T(8,128)(2,1)S(1)}, bf16[256,512]{1,0:T(8,128)(2,1)S(1)}, u32[]{:S(2)}, u32[]{:S(2)}) collective-permute-start(bf16[256,512]{1,0:T(8,128)(2,1)S(1)} %bitcast.22), channel_id=1, source_target_pairs={{0,32},{32,0},{1,33},{33,1},{2,34},{34,2},{3,35},{35,3},{4,36},{36... | collective-permute-start | bytes 786440 | tf_op jit(solution)/shard_map/ppermute | solution.py:169

commit v6 on v5

--- a/solution.py
+++ b/solution.py
@@ -41,23 +41,9 @@
     )(*args)
 
 
-def after(x, *others):
-    def kernel(*refs):
-        pass
-
-    return call(
-        kernel,
-        "after",
-        jax.ShapeDtypeStruct(x.shape, x.dtype),
-        [ANY] * (1 + len(others)),
-        ANY,
-        x,
-        *others,
-        input_output_aliases={0: 0},
-    )
-
-
-def own_kernel(place_ref, video_ref, weight_ref, qkv_ref, own_ref, pair_ref, value_ref):
+def own_kernel(
+    place_ref, video_ref, weight_ref, qkv_ref, cot_ref, own_ref, pair_ref, value_ref
+):
     channels = video_ref.shape[-1]
     pair_ref[...] = lax.dot_general(
         qkv_ref[:, :channels],
@@ -76,20 +62,18 @@
     own_ref[:, 1] = (v1.astype(F32) + (dot(v1, 0) + dot(v0, 1))).reshape(own_ref[:, 0].shape)
 
 
-def early_kernel(start, own_ref, early_ref, weight_ref, *refs):
-    out_ref = refs[-1]
+def early_kernel(own_ref, early_ref, weight_ref, out_ref):
     shape = (early_ref.shape[0],) + early_ref.shape[2:]
     rows = (shape[0] * shape[1], shape[2])
-    at = pl.ds(start, shape[0])
 
     def dot(rows, tap):
         return jnp.dot(rows, weight_ref[tap], preferred_element_type=F32)
 
     e0, e1 = early_ref[:, 0].reshape(rows), early_ref[:, 1].reshape(rows)
-    h0 = own_ref[at, 0].reshape(rows) + (dot(e1, 1) + dot(e0, 2))
-    h1 = own_ref[at, 1].reshape(rows) + dot(e1, 2)
-    out_ref[at, 0] = h0.astype(BF).reshape(shape)
-    out_ref[at, 1] = h1.astype(BF).reshape(shape)
+    h0 = own_ref[:, 0].reshape(rows) + (dot(e1, 1) + dot(e0, 2))
+    h1 = own_ref[:, 1].reshape(rows) + dot(e1, 2)
+    out_ref[:, 0] = h0.astype(BF).reshape(shape)
+    out_ref[:, 1] = h1.astype(BF).reshape(shape)
 
 
 def attend_kernel(
@@ -164,6 +148,18 @@
     ).astype(BF)
 
 
+def deliver_kernel(src_ref, out_ref, sems):
+    each = src_ref.shape[0] // sems.shape[0]
+    copies = [
+        pltpu.make_async_copy(src_ref.at[pl.ds(i * each, each)], out_ref.at[pl.ds(i * each, each)], sems.at[i])
+        for i in range(sems.shape[0])
+    ]
+    for copy in copies:
+        copy.start()
+    for copy in copies:
+        copy.wait()
+
+
 def exchanged(x, axis, by):
     n = lax.axis_size(axis)
     return lax.ppermute(x, axis, [(i, i ^ by) for i in range(n)])
@@ -192,33 +188,28 @@
     clips, frames, tile, channels = video.shape
     peers = clips * frames
     slabs = lax.axis_size(TIME)
-    half = clips // 2
-    early = [lax.ppermute(video[:half], TIME, [(i, i + 1) for i in range(slabs - 1)])]
-    near = exchanged(video, "core", 1)[half:]
-    ahead = [(i, i + 2) for i in range(0, slabs - 2, 2)]
-    early.append(lax.ppermute(near, TIME, ahead + [(i, i) for i in range(1, slabs, 2)]))
-    places = jnp.stack([lax.axis_index(TIME), lax.axis_index("core")])
+    onward = [(i, i + 2) for i in range(1, slabs - 2, 2)] + [(i, i) for i in range(0, slabs, 2)]
+    early = lax.ppermute(video, TIME, onward)
+    video = exchanged(video, "core", 1)
+    cotangent = exchanged(cotangent, "core", 1)
+    core = lax.axis_index("core")
+    places = jnp.stack([lax.axis_index(TIME) + 1 - 2 * core, core])
     own, pair, value = call(
         own_kernel,
         "own",
         (jax.ShapeDtypeStruct(video.shape, F32),) + (jax.ShapeDtypeStruct(out_weight.shape, BF),) * 2,
-        [SMEM] + [VMEM] * 3,
+        [SMEM] + [VMEM] * 3 + [ANY],
         (VMEM,) * 3,
-        places, video, conv_weight, qkv_weight,
-    )
-    hidden = ()
-    for i in range(2):
-        hidden = call(
-            functools.partial(early_kernel, i * half),
-            "early%d" % i,
-            jax.ShapeDtypeStruct(video.shape, BF),
-            [VMEM] * (3 + i),
-            VMEM,
-            own, early[i], conv_weight, *hidden,
-            input_output_aliases={3: 0} if i else {},
-        )
-        hidden = (hidden,)
-    (hidden,) = hidden
+        places, video, conv_weight, qkv_weight, cotangent,
+    )
+    hidden = call(
+        early_kernel,
+        "early",
+        jax.ShapeDtypeStruct(video.shape, BF),
+        [VMEM] * 3,
+        VMEM,
+        own, early, conv_weight,
+    )
     rows = jax.ShapeDtypeStruct((peers * tile, channels), BF)
     frame = a2a(hidden.reshape(peers, tile, channels), TILE).reshape(rows.shape)
     att = call(
@@ -252,6 +243,16 @@
         VMEM,
         hidden.reshape(rows.shape), att, out_weight,
     )
+    out = call(
+        deliver_kernel,
+        "deliver",
+        rows,
+        [ANY],
+        ANY,
+        exchanged(out, "core", 1),
+        scratch_shapes=[pltpu.SemaphoreType.DMA((peers,))],
+        cost_estimate=pl.CostEstimate(flops=1 << 28, bytes_accessed=1 << 21, transcendentals=0),
+    )
     return out.reshape(video.shape), total_sum(mine, other)
 
 

time: 102 us -> 99.7 us (0.977)
  starting transfers between devices: 17.6 us -> 9.29 us
  waiting for transfers between devices: 1.24 us -> 7.36 us
  local copies, waits for them, and re-layouts: 4.6 us -> 2.87 us
  blocking collectives: 65.7 us -> 67.4 us
    ppermute x3 -> x5, starting transfers between devices: 14 us -> 7.77 us  [exchanged(): return lax.ppermute(x, axis, [(i, i ^ by) for i in range(n)])]
    ppermute x2 -> x1, waiting for transfers between devices: 1.09 us -> 4.94 us  [body(): early = lax.ppermute(video, TIME, onward)]
    ppermute x3 -> x5, waiting for transfers between devices: 0.15 us -> 2.42 us  [exchanged(): return lax.ppermute(x, axis, [(i, i ^ by) for i in range(n)])]
    ppermute x2 -> x1, starting transfers between devices: 3.61 us -> 1.52 us  [body(): early = lax.ppermute(video, TIME, onward)]
    slice x2 -> x0, local copies, waits for them, and re-layouts: 1.9 us -> none  [the longest x1 1.08 us: body(): video[:half]]
    all_to_all x5, blocking collectives: 65.7 us -> 67.4 us  [a2a(): return lax.all_to_all(x, axes, split_axis=0, concat_axis=0, tiled=True)]
    unnamed x16 -> x12, local copies, waits for them, and re-layouts: 2.67 us -> 2.83 us
  transfers between devices with their start and end apart: 5 -> 6, of which waited for: 2 -> 4; matrix products, arithmetic and copies ran while one was open for 2% -> 0% of each run, Pallas kernels for 5% -> 5%
where the time goes in v6:
time: 99.7 us; the launch traced here: 99.3 us
  blocking collectives  67.4 us (68%)
  Pallas kernels  10.2 us (10%)
  starting transfers between devices  9.29 us (9%)
  waiting for transfers between devices  7.36 us (7%)
  local copies, waits for them, and re-layouts  2.87 us (3%)
  other arithmetic  1.38 us (1%)
    all_to_all x5, blocking collectives, a2a(): return lax.all_to_all(x, axes, split_axis=0, concat_axis=0, tiled=True)  67.4 us
    pallas_call x7, Pallas kernels, call(): pl.pallas_call(kernel, out_shape=out_shape, in_specs=in_specs, out_specs=...  10.2 us
    ppermute x5, starting transfers between devices, exchanged(): return lax.ppermute(x, axis, [(i, i ^ by) for i in range(n)])  7.77 us
    ppermute x1, waiting for transfers between devices, body(): early = lax.ppermute(video, TIME, onward)  4.94 us
    unnamed x12, local copies, waits for them, and re-layouts  2.83 us
    ppermute x5, waiting for transfers between devices, exchanged(): return lax.ppermute(x, axis, [(i, i ^ by) for i in range(n)])  2.42 us
  transfers between devices with their start and end apart: 6, of which 4 were waited for; matrix products, arithmetic and copies ran while one was open for 0% of the time, Pallas kernels for 5%

profile of v6, /device:TPU:1, one launch (start us, length us, event | category | flops | bytes accessed | tf_op | source)
XLA Modules:
  0.0 99.3 jit_solution(926183581077496845)
XLA Ops:
  0.6 3.3 %collective-permute-start.1 = (bf16[4,2,128,512]{3,2,1,0:T(8,128)(2,1)}, bf16[4,2,128,512]{3,2,1,0:T(8,128)(2,1)S(1)}, u32[]{:S(2)}, u32[]{:S(2)}) collective-permute-start(bf16[4,2,128,512]{3,2,1,0:T(8,128)(2,1)} %param.12), channel_id=1, source_target_pairs={{0,32},{32,0},{1,33},{33,1},{2,34},{34,2},{3,35},{35,3},{4,36},{36... | collective-permute-start | bytes 3145736 | tf_op jit(solution)/shard_map/ppermute | solution.py:165
  4.0 0.1 collective-permute-start
  4.1 1.5 %collective-permute-start.2 = (bf16[4,2,128,512]{3,2,1,0:T(8,128)(2,1)}, bf16[4,2,128,512]{3,2,1,0:T(8,128)(2,1)S(1)}, u32[]{:S(2)}, u32[]{:S(2)}) collective-permute-start(bf16[4,2,128,512]{3,2,1,0:T(8,128)(2,1)} %param.7), channel_id=1, source_target_pairs={{32,96},{96,160},{160,224},{0,0},{64,64},{128,128},{192,192},{33,9... | collective-permute-start | bytes 3145736 | tf_op jit(solution)/shard_map/ppermute | solution.py:192
  5.7 0.8 collective-permute-done.1.cot_ref
  6.5 1.5 %collective-permute-done.video_ref = bf16[4,2,128,512]{3,2,1,0:T(8,128)(2,1)S(1)} collective-permute-done((bf16[4,2,128,512]{3,2,1,0:T(8,128)(2,1)}, bf16[4,2,128,512]{3,2,1,0:T(8,128)(2,1)S(1)}, u32[]{:S(2)}, u32[]{:S(2)}) %collective-permute-start) | collective-permute-done | bytes 1048608 | tf_op jit(solution)/shard_map/ppermute | solution.py:165
  8.0 1.4 %copy-done = bf16[3,512,512]{2,1,0:T(8,128)(2,1)S(1)} copy-done((bf16[3,512,512]{2,1,0:T(8,128)(2,1)S(1)}, bf16[3,512,512]{2,1,0:T(8,128)(2,1)}, u32[]{:S(2)}) %copy-start) | copy-done | bytes 1572888
  9.4 1.4 %copy-done.2 = bf16[512,1536]{1,0:T(8,128)(2,1)S(1)} copy-done((bf16[512,1536]{1,0:T(8,128)(2,1)S(1)}, bf16[512,1536]{1,0:T(8,128)(2,1)}, u32[]{:S(2)}) %copy-start.2) | copy-done | bytes 1572888
  10.8 1.8 %own.1 = (f32[4,2,128,512]{3,2,1,0:T(8,128)S(1)}, bf16[512,512]{1,0:T(8,128)(2,1)S(1)}, bf16[512,512]{1,0:T(8,128)(2,1)S(1)}) custom-call(s32[2]{0:T(128)S(1)} %pad_add_fusion.place_ref, bf16[4,2,128,512]{3,2,1,0:T(8,128)(2,1)S(1)} %collective-permute-done.video_ref, bf16[3,512,512]{2,1,0:T(8,128)(2,1)S(1)} %copy-done, bf16[512,1536]{1,0:T(8,128)(2,1)S(1)} %copy-done.2, ...), custom_call_target="tpu_custom_call" | custom-call | tf_op jit(solution)/shard_map/own/pallas_call | solution.py:33
  12.6 4.9 %collective-permute-done.2.early_ref = bf16[4,2,128,512]{3,2,1,0:T(8,128)(2,1)S(1)} collective-permute-done((bf16[4,2,128,512]{3,2,1,0:T(8,128)(2,1)}, bf16[4,2,128,512]{3,2,1,0:T(8,128)(2,1)S(1)}, u32[]{:S(2)}, u32[]{:S(2)}) %collective-permute-start.2) | collective-permute-done | bytes 1048608 | tf_op jit(solution)/shard_map/ppermute | solution.py:192
  17.6 1.0 %early.1 = bf16[4,2,128,512]{3,2,1,0:T(8,128)(2,1)S(1)} custom-call(f32[4,2,128,512]{3,2,1,0:T(8,128)S(1)} %get-tuple-element.5.own_ref, bf16[4,2,128,512]{3,2,1,0:T(8,128)(2,1)S(1)} %collective-permute-done.2.early_ref, bf16[3,512,512]{2,1,0:T(8,128)(2,1)S(1)} %copy-done.1), custom_call_target="tpu_custom_call" | custom-call | tf_op jit(solution)/shard_map/early/pallas_call | solution.py:33
  18.6 15.6 %all_to_all.25 = bf16[8,128,512]{2,1,0:T(8,128)(2,1)S(1)} all-to-all(bf16[8,128,512]{2,1,0:T(8,128)(2,1)S(1)} %bitcast.16), channel_id=1, replica_groups=mesh['y'=4,'core'=2,'x'=4,'zl'=2,'clip'=4] {'x','zl'}, dimensions={0} | all-to-all | bytes 2097152 | tf_op jit(solution)/shard_map/all_to_all | solution.py:22
  34.2 3.6 %attend.1 = bf16[1024,512]{1,0:T(8,128)(2,1)S(1)} custom-call(bf16[1024,512]{1,0:T(8,128)(2,1)S(1)} %bitcast.18, f32[1,512]{1,0:T(1,128)S(1)} %bitcast.20, bf16[512,512]{1,0:T(8,128)(2,1)S(1)} %get-tuple-element.6.pair_ref, bf16[512,512]{1,0:T(8,128)(2,1)S(1)} %get-tuple-element.7.value_ref), custom_call_target="tpu_custom_call" | custom-call | tf_op jit(solution)/shard_map/attend/pallas_call | solution.py:33
  37.8 14.5 %all_to_all.26 = bf16[8,128,512]{2,1,0:T(8,128)(2,1)S(1)} all-to-all(bf16[8,128,512]{2,1,0:T(8,128)(2,1)S(1)} %bitcast.19), channel_id=1, replica_groups=mesh['y'=4,'core'=2,'x'=4,'zl'=2,'clip'=4] {'x','zl'}, dimensions={0} | all-to-all | bytes 2097152 | tf_op jit(solution)/shard_map/all_to_all | solution.py:22
  52.3 1.0 %other.1 = bf16[256,512]{1,0:T(8,128)(2,1)S(1)} custom-call(s32[2]{0:T(128)S(1)} %pad_add_fusion.place_ref, s32[4]{0:T(128)S(1)} %copy-done.5, bf16[1024,512]{1,0:T(8,128)(2,1)S(1)} %bitcast.13, bf16[4,2,128,512]{3,2,1,0:T(8,128)(2,1)S(1)} %collective-permute-done.1.cot_ref), custom_call_target="tpu_custom_call" | custom-call | flops 268435456 | bytes 2097152 | tf_op jit(solution)/shard_map/other/pallas_call | solution.py:33
  53.4 0.7 out.1
  54.2 0.6 collective-permute-start.3
  54.7 1.0 %mine.1 = f32[256,512]{1,0:T(8,128)S(1)} custom-call(s32[2]{0:T(128)S(1)} %pad_add_fusion.place_ref, s32[4]{0:T(128)S(1)} %copy-done.5, bf16[1024,512]{1,0:T(8,128)(2,1)S(1)} %bitcast.15, bf16[4,2,128,512]{3,2,1,0:T(8,128)(2,1)S(1)} %collective-permute-done.1.cot_ref), custom_call_target="tpu_custom_call" | custom-call | flops 268435456 | bytes 2097152 | tf_op jit(solution)/shard_map/mine/pallas_call | solution.py:33
  55.8 13.0 %all_to_all.27 = bf16[16,16,512]{2,1,0:T(8,128)(2,1)S(1)} all-to-all(bf16[16,16,512]{2,1,0:T(8,128)(2,1)S(1)} %bitcast.23), channel_id=1, replica_groups=mesh['y'=4,'core'=2,'x'=4,'zl'=2,'clip'=4] {'y','x'}, dimensions={0} | all-to-all | bytes 524288 | tf_op jit(solution)/shard_map/all_to_all | solution.py:22
  68.9 14.1 %all_to_all.28 = bf16[8,16,512]{2,1,0:T(8,128)(2,1)S(1)} all-to-all(bf16[8,16,512]{2,1,0:T(8,128)(2,1)S(1)} %broadcast_in_dim.4), channel_id=1, replica_groups=mesh['y'=4,'core'=2,'x'=4,'zl'=2,'clip'=4] {'zl','clip'}, dimensions={0} | all-to-all | bytes 262144 | tf_op jit(solution)/shard_map/all_to_all | solution.py:22
  83.1 10.2 %all_to_all.29 = bf16[16,16,512]{2,1,0:T(8,128)(2,1)S(1)} all-to-all(bf16[16,16,512]{2,1,0:T(8,128)(2,1)S(1)} %broadcast_in_dim.5), channel_id=1, replica_groups=mesh['y'=4,'core'=2,'x'=4,'zl'=2,'clip'=4] {'y','x'}, dimensions={0} | all-to-all | bytes 524288 | tf_op jit(solution)/shard_map/all_to_all | solution.py:22
  93.3 3.7 %collective-permute-start.5 = (bf16[256,512]{1,0:T(8,128)(2,1)S(1)}, bf16[256,512]{1,0:T(8,128)(2,1)S(1)}, u32[]{:S(2)}, u32[]{:S(2)}) collective-permute-start(bf16[256,512]{1,0:T(8,128)(2,1)S(1)} %bitcast.22), channel_id=1, source_target_pairs={{0,32},{32,0},{1,33},{33,1},{2,34},{34,2},{3,35},{35,3},{4,36},{36... | collective-permute-start | bytes 786440 | tf_op jit(solution)/shard_map/ppermute | solution.py:165
  97.0 1.0 %deliver.1 = bf16[1024,512]{1,0:T(8,128)(2,1)} custom-call(bf16[1024,512]{1,0:T(8,128)(2,1)S(1)} %collective-permute-done.3.src_ref), custom_call_target="tpu_custom_call" | custom-call | flops 268435456 | bytes 2097152 | tf_op jit(solution)/shard_map/deliver/pallas_call | solution.py:33
  98.0 0.1 collective-permute-done.5
  98.2 1.1 %maximum_convert_fusion = f32[512,512]{1,0:T(8,128)} fusion(bf16[256,512]{1,0:T(8,128)(2,1)S(1)} %get-tuple-element.9, bf16[256,512]{1,0:T(8,128)(2,1)S(1)} %get-tuple-element.8), kind=kLoop, calls=%fused_computation | loop fusion | flops 1048576 | bytes 1572864 | tf_op jit(solution)/shard_map/convert_element_type | solution.py:184
  (20 shorter events, 0.4 us)
Async XLA Ops:
  0.6 5.8 %collective-permute-start.1 = (bf16[4,2,128,512]{3,2,1,0:T(8,128)(2,1)}, bf16[4,2,128,512]{3,2,1,0:T(8,128)(2,1)S(1)}, u32[]{:S(2)}, u32[]{:S(2)}) collective-permute-start(bf16[4,2,128,512]{3,2,1,0:T(8,128)(2,1)} %param.12), channel_id=1, source_target_pairs={{0,32},{32,0},{1,33},{33,1},{2,34},{34,2},{3,35},{35,3},{4,36},{36... | collective-permute-start | bytes 3145736 | tf_op jit(solution)/shard_map/ppermute | solution.py:165
  4.0 4.0 %collective-permute-start = (bf16[4,2,128,512]{3,2,1,0:T(8,128)(2,1)}, bf16[4,2,128,512]{3,2,1,0:T(8,128)(2,1)S(1)}, u32[]{:S(2)}, u32[]{:S(2)}) collective-permute-start(bf16[4,2,128,512]{3,2,1,0:T(8,128)(2,1)} %param.7), channel_id=1, source_target_pairs={{0,32},{32,0},{1,33},{33,1},{2,34},{34,2},{3,35},{35,3},{4,36},{36... | collective-permute-start | bytes 3145736 | tf_op jit(solution)/shard_map/ppermute | solution.py:165
  4.1 13.5 %collective-permute-start.2 = (bf16[4,2,128,512]{3,2,1,0:T(8,128)(2,1)}, bf16[4,2,128,512]{3,2,1,0:T(8,128)(2,1)S(1)}, u32[]{:S(2)}, u32[]{:S(2)}) collective-permute-start(bf16[4,2,128,512]{3,2,1,0:T(8,128)(2,1)} %param.7), channel_id=1, source_target_pairs={{32,96},{96,160},{160,224},{0,0},{64,64},{128,128},{192,192},{33,9... | collective-permute-start | bytes 3145736 | tf_op jit(solution)/shard_map/ppermute | solution.py:192
  8.0 1.4 %copy-start = (bf16[3,512,512]{2,1,0:T(8,128)(2,1)S(1)}, bf16[3,512,512]{2,1,0:T(8,128)(2,1)}, u32[]{:S(2)}) copy-start(bf16[3,512,512]{2,1,0:T(8,128)(2,1)} %weight_ref.3) | copy-start | bytes 4718596
  9.4 1.4 %copy-start.2 = (bf16[512,1536]{1,0:T(8,128)(2,1)S(1)}, bf16[512,1536]{1,0:T(8,128)(2,1)}, u32[]{:S(2)}) copy-start(bf16[512,1536]{1,0:T(8,128)(2,1)} %qkv_ref.1) | copy-start | bytes 4718596
  10.8 6.8 %copy-start.1 = (bf16[3,512,512]{2,1,0:T(8,128)(2,1)S(1)}, bf16[3,512,512]{2,1,0:T(8,128)(2,1)}, u32[]{:S(2)}) copy-start(bf16[3,512,512]{2,1,0:T(8,128)(2,1)} %weight_ref.3) | copy-start | bytes 4718596
  18.6 15.6 %copy-start.4 = (f32[512]{0:T(512)S(1)}, f32[512]{0:T(512)}, u32[]{:S(2)}) copy-start(f32[512]{0:T(512)} %param.9) | copy-start | bytes 6148
  37.8 14.5 %copy-start.5 = (s32[4]{0:T(128)S(1)}, s32[4]{0:T(128)}, u32[]{:S(2)}) copy-start(s32[4]{0:T(128)} %lengths_ref.3) | copy-start | bytes 52
  52.3 1.1 %copy-start.3 = (bf16[512,512]{1,0:T(8,128)(2,1)S(1)}, bf16[512,512]{1,0:T(8,128)(2,1)}, u32[]{:S(2)}) copy-start(bf16[512,512]{1,0:T(8,128)(2,1)} %wo_ref.1) | copy-start | bytes 1572868
  53.3 2.4 %collective-permute-start.4 = (bf16[256,512]{1,0:T(8,128)(2,1)S(1)}, bf16[256,512]{1,0:T(8,128)(2,1)S(1)}, u32[]{:S(2)}, u32[]{:S(2)}) collective-permute-start(bf16[256,512]{1,0:T(8,128)(2,1)S(1)} %other.1), channel_id=1, source_target_pairs={{0,32},{32,0},{1,33},{33,1},{2,34},{34,2},{3,35},{35,3},{4,36},{36... | collective-permute-start | bytes 786440 | tf_op jit(solution)/shard_map/ppermute | solution.py:165
  54.2 42.8 %collective-permute-start.3 = (bf16[1024,512]{1,0:T(8,128)(2,1)S(1)}, bf16[1024,512]{1,0:T(8,128)(2,1)S(1)}, u32[]{:S(2)}, u32[]{:S(2)}) collective-permute-start(bf16[1024,512]{1,0:T(8,128)(2,1)S(1)} %out.1), channel_id=1, source_target_pairs={{0,32},{32,0},{1,33},{33,1},{2,34},{34,2},{3,35},{35,3},{4,36},{36... | collective-permute-start | bytes 3145736 | tf_op jit(solution)/shard_map/ppermute | solution.py:165
  93.3 4.8 %collective-permute-start.5 = (bf16[256,512]{1,0:T(8,128)(2,1)S(1)}, bf16[256,512]{1,0:T(8,128)(2,1)S(1)}, u32[]{:S(2)}, u32[]{:S(2)}) collective-permute-start(bf16[256,512]{1,0:T(8,128)(2,1)S(1)} %bitcast.22), channel_id=1, source_target_pairs={{0,32},{32,0},{1,33},{33,1},{2,34},{34,2},{3,35},{35,3},{4,36},{36... | collective-permute-start | bytes 786440 | tf_op jit(solution)/shard_map/ppermute | solution.py:165

commit v7 on v6

--- a/solution.py
+++ b/solution.py
@@ -124,28 +124,57 @@
             att_ref[chunk(t - 2), :] = attended(*stages[1].pop(t - 2))
 
 
-def grad_kernel(place_ref, lengths_ref, att_ref, cot_ref, grad_ref, live_ref, *, swap):
+def masked_into(live_ref, place_ref, lengths_ref, cot_ref):
     clips, frames, tile = cot_ref.shape[:3]
     for clip in range(clips):
         for frame in range(frames):
             live = place_ref[0] * frames + frame < lengths_ref[clip]
             rows = pl.ds((clip * frames + frame) * tile, tile)
             live_ref[rows, :] = cot_ref[clip, frame] * jnp.where(live, 1.0, 0.0).astype(BF)
-    split = grad_ref.shape[0]
-    half = 1 - place_ref[1] if swap else place_ref[1]
-    grad_ref[...] = lax.dot_general(
+
+
+def half_grad(att_ref, live_ref, half, split):
+    return lax.dot_general(
         att_ref[:, pl.ds(pl.multiple_of(half * split, split), split)],
         live_ref[...],
         (((0,), (0,)), ((), ())),
         preferred_element_type=F32,
-    ).astype(grad_ref.dtype)
-
-
-def out_kernel(hidden_ref, att_ref, wo_ref, out_ref):
+    )
+
+
+def own_rows(hidden_ref, att_ref, wo_ref, out_ref):
     out_ref[...] = (
         hidden_ref[...].astype(F32)
         + jnp.dot(att_ref[...], wo_ref[...], preferred_element_type=F32)
     ).astype(BF)
+
+
+def before_kernel(
+    place_ref, lengths_ref, att_ref, cot_ref, hidden_ref, wo_ref,
+    other_ref, live_ref, mine_ref, out_ref,
+):
+    masked_into(live_ref, place_ref, lengths_ref, cot_ref)
+    split = other_ref.shape[0]
+    other_ref[...] = half_grad(att_ref, live_ref, 1 - place_ref[1], split).astype(BF)
+
+    @pl.when(place_ref[1] == 0)
+    def _():
+        mine_ref[...] = half_grad(att_ref, live_ref, 0, split)
+        own_rows(hidden_ref, att_ref, wo_ref, out_ref)
+
+
+def during_kernel(
+    place_ref, att_ref, live_ref, hidden_ref, wo_ref, mine_in, out_in, mine_ref, out_ref
+):
+    @pl.when(place_ref[1] == 1)
+    def _():
+        own_rows(hidden_ref, att_ref, wo_ref, out_ref)
+        mine_ref[...] = half_grad(att_ref, live_ref, 1, mine_ref.shape[0])
+
+    @pl.when(place_ref[1] == 0)
+    def _():
+        mine_ref[...] = mine_in[...]
+        out_ref[...] = out_in[...]
 
 
 def deliver_kernel(src_ref, out_ref, sems):
@@ -222,26 +251,25 @@
         scratch_shapes=[pltpu.VMEM(rows.shape, BF)] * 3,
     )
     att = a2a(att.reshape(peers, tile, channels), TILE).reshape(rows.shape)
-    other, mine = (
-        call(
-            functools.partial(grad_kernel, swap=swap),
-            "other" if swap else "mine",
-            jax.ShapeDtypeStruct((channels // 2, channels), BF if swap else F32),
-            [SMEM, SMEM, VMEM, VMEM],
-            VMEM,
-            places, lengths, att, cotangent,
-            scratch_shapes=[pltpu.VMEM(rows.shape, BF)],
-            cost_estimate=pl.CostEstimate(flops=1 << 28, bytes_accessed=1 << 21, transcendentals=0),
-        )
-        for swap in (True, False)
-    )
-    out = call(
-        out_kernel,
-        "out",
-        rows,
-        [VMEM] * 3,
-        VMEM,
-        hidden.reshape(rows.shape), att, out_weight,
+    kept = jax.ShapeDtypeStruct((channels // 2, channels), F32)
+    flat = hidden.reshape(rows.shape)
+    other, live, mine, out = call(
+        before_kernel,
+        "before",
+        (jax.ShapeDtypeStruct(kept.shape, BF), rows, kept, rows),
+        [SMEM] * 2 + [VMEM] * 4,
+        (VMEM,) * 4,
+        places, lengths, att, cotangent, flat, out_weight,
+    )
+    mine, out = call(
+        during_kernel,
+        "during",
+        (kept, rows),
+        [SMEM] + [VMEM] * 6,
+        (VMEM,) * 2,
+        places, att, live, flat, out_weight, mine, out,
+        input_output_aliases={5: 0, 6: 1},
+        cost_estimate=pl.CostEstimate(flops=1 << 29, bytes_accessed=1 << 21, transcendentals=0),
     )
     out = call(
         deliver_kernel,

time: 99.7 us -> 99.4 us (level)
    pallas_call x7 -> x6, Pallas kernels: 10.2 us -> 10 us  [call(): pl.pallas_call(kernel, out_shape=out_shape, in_specs=in_specs, out_specs=...]
  transfers between devices with their start and end apart: 6 -> 6, of which waited for: 4 -> 4; matrix products, arithmetic and copies ran while one was open for 0% -> 0% of each run, Pallas kernels for 5% -> 4%
where the time goes in v7:
time: 99.4 us; the launch traced here: 99 us
  blocking collectives  66.9 us (67%)
  Pallas kernels  10 us (10%)
  starting transfers between devices  9.63 us (10%)
  waiting for transfers between devices  7.36 us (7%)
  local copies, waits for them, and re-layouts  2.87 us (3%)
  other arithmetic  1.37 us (1%)
    all_to_all x5, blocking collectives, a2a(): return lax.all_to_all(x, axes, split_axis=0, concat_axis=0, tiled=True)  66.9 us
    pallas_call x6, Pallas kernels, call(): pl.pallas_call(kernel, out_shape=out_shape, in_specs=in_specs, out_specs=...  10 us
    ppermute x5, starting transfers between devices, exchanged(): return lax.ppermute(x, axis, [(i, i ^ by) for i in range(n)])  8.11 us
    ppermute x1, waiting for transfers between devices, body(): early = lax.ppermute(video, TIME, onward)  4.94 us
    unnamed x12, local copies, waits for them, and re-layouts  2.84 us
    ppermute x5, waiting for transfers between devices, exchanged(): return lax.ppermute(x, axis, [(i, i ^ by) for i in range(n)])  2.42 us
  transfers between devices with their start and end apart: 6, of which 4 were waited for; matrix products, arithmetic and copies ran while one was open for 0% of the time, Pallas kernels for 4%

profile of v7, /device:TPU:1, one launch (start us, length us, event | category | flops | bytes accessed | tf_op | source)
XLA Modules:
  0.0 99.0 jit_solution(3768964410598649086)
XLA Ops:
  0.6 3.3 %collective-permute-start.1 = (bf16[4,2,128,512]{3,2,1,0:T(8,128)(2,1)}, bf16[4,2,128,512]{3,2,1,0:T(8,128)(2,1)S(1)}, u32[]{:S(2)}, u32[]{:S(2)}) collective-permute-start(bf16[4,2,128,512]{3,2,1,0:T(8,128)(2,1)} %param.12), channel_id=1, source_target_pairs={{0,32},{32,0},{1,33},{33,1},{2,34},{34,2},{3,35},{35,3},{4,36},{36... | collective-permute-start | bytes 3145736 | tf_op jit(solution)/shard_map/ppermute | solution.py:194
  4.0 0.1 collective-permute-start
  4.1 1.5 %collective-permute-start.2 = (bf16[4,2,128,512]{3,2,1,0:T(8,128)(2,1)}, bf16[4,2,128,512]{3,2,1,0:T(8,128)(2,1)S(1)}, u32[]{:S(2)}, u32[]{:S(2)}) collective-permute-start(bf16[4,2,128,512]{3,2,1,0:T(8,128)(2,1)} %param.7), channel_id=1, source_target_pairs={{32,96},{96,160},{160,224},{0,0},{64,64},{128,128},{192,192},{33,9... | collective-permute-start | bytes 3145736 | tf_op jit(solution)/shard_map/ppermute | solution.py:221
  5.7 0.8 collective-permute-done.1.cot_ref
  6.5 1.5 %collective-permute-done.video_ref = bf16[4,2,128,512]{3,2,1,0:T(8,128)(2,1)S(1)} collective-permute-done((bf16[4,2,128,512]{3,2,1,0:T(8,128)(2,1)}, bf16[4,2,128,512]{3,2,1,0:T(8,128)(2,1)S(1)}, u32[]{:S(2)}, u32[]{:S(2)}) %collective-permute-start) | collective-permute-done | bytes 1048608 | tf_op jit(solution)/shard_map/ppermute | solution.py:194
  8.0 1.4 %copy-done = bf16[3,512,512]{2,1,0:T(8,128)(2,1)S(1)} copy-done((bf16[3,512,512]{2,1,0:T(8,128)(2,1)S(1)}, bf16[3,512,512]{2,1,0:T(8,128)(2,1)}, u32[]{:S(2)}) %copy-start) | copy-done | bytes 1572888
  9.4 1.4 %copy-done.3 = bf16[512,1536]{1,0:T(8,128)(2,1)S(1)} copy-done((bf16[512,1536]{1,0:T(8,128)(2,1)S(1)}, bf16[512,1536]{1,0:T(8,128)(2,1)}, u32[]{:S(2)}) %copy-start.3) | copy-done | bytes 1572888
  10.8 1.8 %own.1 = (f32[4,2,128,512]{3,2,1,0:T(8,128)S(1)}, bf16[512,512]{1,0:T(8,128)(2,1)S(1)}, bf16[512,512]{1,0:T(8,128)(2,1)S(1)}) custom-call(s32[2]{0:T(128)S(1)} %pad_add_fusion.place_ref, bf16[4,2,128,512]{3,2,1,0:T(8,128)(2,1)S(1)} %collective-permute-done.video_ref, bf16[3,512,512]{2,1,0:T(8,128)(2,1)S(1)} %copy-done, bf16[512,1536]{1,0:T(8,128)(2,1)S(1)} %copy-done.3, ...), custom_call_target="tpu_custom_call" | custom-call | tf_op jit(solution)/shard_map/own/pallas_call | solution.py:33
  12.6 4.9 %collective-permute-done.2.early_ref = bf16[4,2,128,512]{3,2,1,0:T(8,128)(2,1)S(1)} collective-permute-done((bf16[4,2,128,512]{3,2,1,0:T(8,128)(2,1)}, bf16[4,2,128,512]{3,2,1,0:T(8,128)(2,1)S(1)}, u32[]{:S(2)}, u32[]{:S(2)}) %collective-permute-start.2) | collective-permute-done | bytes 1048608 | tf_op jit(solution)/shard_map/ppermute | solution.py:221
  17.6 1.0 %early.1 = bf16[4,2,128,512]{3,2,1,0:T(8,128)(2,1)S(1)} custom-call(f32[4,2,128,512]{3,2,1,0:T(8,128)S(1)} %get-tuple-element.11.own_ref, bf16[4,2,128,512]{3,2,1,0:T(8,128)(2,1)S(1)} %collective-permute-done.2.early_ref, bf16[3,512,512]{2,1,0:T(8,128)(2,1)S(1)} %copy-done.1), custom_call_target="tpu_custom_call" | custom-call | tf_op jit(solution)/shard_map/early/pallas_call | solution.py:33
  18.6 15.6 %all_to_all.25 = bf16[8,128,512]{2,1,0:T(8,128)(2,1)S(1)} all-to-all(bf16[8,128,512]{2,1,0:T(8,128)(2,1)S(1)} %bitcast.13), channel_id=1, replica_groups=mesh['y'=4,'core'=2,'x'=4,'zl'=2,'clip'=4] {'x','zl'}, dimensions={0} | all-to-all | bytes 2097152 | tf_op jit(solution)/shard_map/all_to_all | solution.py:22
  34.2 3.7 %attend.1 = bf16[1024,512]{1,0:T(8,128)(2,1)S(1)} custom-call(bf16[1024,512]{1,0:T(8,128)(2,1)S(1)} %bitcast.18, f32[1,512]{1,0:T(1,128)S(1)} %bitcast.20, bf16[512,512]{1,0:T(8,128)(2,1)S(1)} %get-tuple-element.12.pair_ref, bf16[512,512]{1,0:T(8,128)(2,1)S(1)} %get-tuple-element.13.value_ref), custom_call_target="tpu_custom_call" | custom-call | tf_op jit(solution)/shard_map/attend/pallas_call | solution.py:33
  37.9 14.6 %all_to_all.26 = bf16[8,128,512]{2,1,0:T(8,128)(2,1)S(1)} all-to-all(bf16[8,128,512]{2,1,0:T(8,128)(2,1)S(1)} %bitcast.19), channel_id=1, replica_groups=mesh['y'=4,'core'=2,'x'=4,'zl'=2,'clip'=4] {'x','zl'}, dimensions={0} | all-to-all | bytes 2097152 | tf_op jit(solution)/shard_map/all_to_all | solution.py:22
  52.5 1.0 %before.1 = (bf16[256,512]{1,0:T(8,128)(2,1)S(1)}, bf16[1024,512]{1,0:T(8,128)(2,1)S(1)}, f32[256,512]{1,0:T(8,128)S(1)}, bf16[1024,512]{1,0:T(8,128)(2,1)S(1)}) custom-call(s32[2]{0:T(128)S(1)} %pad_add_fusion.place_ref, s32[4]{0:T(128)S(1)} %copy-done.5, bf16[1024,512]{1,0:T(8,128)(2,1)S(1)} %bitcast.16, ...), custom_call_target="tpu_custom_call" | custom-call | tf_op jit(solution)/shard_map/before/pallas_call | solution.py:33
  53.5 0.1 collective-permute-start.4
  53.6 1.5 %during.1 = (f32[256,512]{1,0:T(8,128)S(1)}, bf16[1024,512]{1,0:T(8,128)(2,1)S(1)}) custom-call(s32[2]{0:T(128)S(1)} %pad_add_fusion.place_ref, bf16[1024,512]{1,0:T(8,128)(2,1)S(1)} %bitcast.17, bf16[1024,512]{1,0:T(8,128)(2,1)S(1)} %get-tuple-element.14.live_ref, bf16[1024,512]{1,0:T(8,128)(2,1)S(1)} %bitcast.15, ...), custom_call_target="tpu_custom_call", output_to_operand_aliasing={{0}: (5, {}), {1}: (6, {})} | custom-call | flops 536870912 | bytes 2097152 | tf_op jit(solution)/shard_map/during/pallas_call | solution.py:33
  55.1 0.1 collective-permute-start.3
  55.3 12.5 %all_to_all.27 = bf16[16,16,512]{2,1,0:T(8,128)(2,1)S(1)} all-to-all(bf16[16,16,512]{2,1,0:T(8,128)(2,1)S(1)} %bitcast.23), channel_id=1, replica_groups=mesh['y'=4,'core'=2,'x'=4,'zl'=2,'clip'=4] {'y','x'}, dimensions={0} | all-to-all | bytes 524288 | tf_op jit(solution)/shard_map/all_to_all | solution.py:22
  67.9 14.1 %all_to_all.28 = bf16[8,16,512]{2,1,0:T(8,128)(2,1)S(1)} all-to-all(bf16[8,16,512]{2,1,0:T(8,128)(2,1)S(1)} %broadcast_in_dim.4), channel_id=1, replica_groups=mesh['y'=4,'core'=2,'x'=4,'zl'=2,'clip'=4] {'zl','clip'}, dimensions={0} | all-to-all | bytes 262144 | tf_op jit(solution)/shard_map/all_to_all | solution.py:22
  82.0 10.1 %all_to_all.29 = bf16[16,16,512]{2,1,0:T(8,128)(2,1)S(1)} all-to-all(bf16[16,16,512]{2,1,0:T(8,128)(2,1)S(1)} %broadcast_in_dim.5), channel_id=1, replica_groups=mesh['y'=4,'core'=2,'x'=4,'zl'=2,'clip'=4] {'y','x'}, dimensions={0} | all-to-all | bytes 524288 | tf_op jit(solution)/shard_map/all_to_all | solution.py:22
  92.2 4.5 %collective-permute-start.5 = (bf16[256,512]{1,0:T(8,128)(2,1)S(1)}, bf16[256,512]{1,0:T(8,128)(2,1)S(1)}, u32[]{:S(2)}, u32[]{:S(2)}) collective-permute-start(bf16[256,512]{1,0:T(8,128)(2,1)S(1)} %bitcast.22), channel_id=1, source_target_pairs={{0,32},{32,0},{1,33},{33,1},{2,34},{34,2},{3,35},{35,3},{4,36},{36... | collective-permute-start | bytes 786440 | tf_op jit(solution)/shard_map/ppermute | solution.py:194
  96.7 1.0 %deliver.1 = bf16[1024,512]{1,0:T(8,128)(2,1)} custom-call(bf16[1024,512]{1,0:T(8,128)(2,1)S(1)} %collective-permute-done.3.src_ref), custom_call_target="tpu_custom_call" | custom-call | flops 268435456 | bytes 2097152 | tf_op jit(solution)/shard_map/deliver/pallas_call | solution.py:33
  97.7 0.1 collective-permute-done.5
  97.9 1.1 %maximum_convert_fusion = f32[512,512]{1,0:T(8,128)} fusion(bf16[256,512]{1,0:T(8,128)(2,1)S(1)} %get-tuple-element.21, bf16[256,512]{1,0:T(8,128)(2,1)S(1)} %get-tuple-element.20), kind=kLoop, calls=%fused_computation | loop fusion | flops 1048576 | bytes 1572864 | tf_op jit(solution)/shard_map/convert_element_type | solution.py:213
  (19 shorter events, 0.3 us)
Async XLA Ops:
  0.6 5.8 %collective-permute-start.1 = (bf16[4,2,128,512]{3,2,1,0:T(8,128)(2,1)}, bf16[4,2,128,512]{3,2,1,0:T(8,128)(2,1)S(1)}, u32[]{:S(2)}, u32[]{:S(2)}) collective-permute-start(bf16[4,2,128,512]{3,2,1,0:T(8,128)(2,1)} %param.12), channel_id=1, source_target_pairs={{0,32},{32,0},{1,33},{33,1},{2,34},{34,2},{3,35},{35,3},{4,36},{36... | collective-permute-start | bytes 3145736 | tf_op jit(solution)/shard_map/ppermute | solution.py:194
  4.0 4.0 %collective-permute-start = (bf16[4,2,128,512]{3,2,1,0:T(8,128)(2,1)}, bf16[4,2,128,512]{3,2,1,0:T(8,128)(2,1)S(1)}, u32[]{:S(2)}, u32[]{:S(2)}) collective-permute-start(bf16[4,2,128,512]{3,2,1,0:T(8,128)(2,1)} %param.7), channel_id=1, source_target_pairs={{0,32},{32,0},{1,33},{33,1},{2,34},{34,2},{3,35},{35,3},{4,36},{36... | collective-permute-start | bytes 3145736 | tf_op jit(solution)/shard_map/ppermute | solution.py:194
  4.1 13.5 %collective-permute-start.2 = (bf16[4,2,128,512]{3,2,1,0:T(8,128)(2,1)}, bf16[4,2,128,512]{3,2,1,0:T(8,128)(2,1)S(1)}, u32[]{:S(2)}, u32[]{:S(2)}) collective-permute-start(bf16[4,2,128,512]{3,2,1,0:T(8,128)(2,1)} %param.7), channel_id=1, source_target_pairs={{32,96},{96,160},{160,224},{0,0},{64,64},{128,128},{192,192},{33,9... | collective-permute-start | bytes 3145736 | tf_op jit(solution)/shard_map/ppermute | solution.py:221
  8.0 1.4 %copy-start = (bf16[3,512,512]{2,1,0:T(8,128)(2,1)S(1)}, bf16[3,512,512]{2,1,0:T(8,128)(2,1)}, u32[]{:S(2)}) copy-start(bf16[3,512,512]{2,1,0:T(8,128)(2,1)} %weight_ref.3) | copy-start | bytes 4718596
  9.4 1.4 %copy-start.3 = (bf16[512,1536]{1,0:T(8,128)(2,1)S(1)}, bf16[512,1536]{1,0:T(8,128)(2,1)}, u32[]{:S(2)}) copy-start(bf16[512,1536]{1,0:T(8,128)(2,1)} %qkv_ref.1) | copy-start | bytes 4718596
  10.8 6.8 %copy-start.1 = (bf16[3,512,512]{2,1,0:T(8,128)(2,1)S(1)}, bf16[3,512,512]{2,1,0:T(8,128)(2,1)}, u32[]{:S(2)}) copy-start(bf16[3,512,512]{2,1,0:T(8,128)(2,1)} %weight_ref.3) | copy-start | bytes 4718596
  18.6 15.6 %copy-start.4 = (f32[512]{0:T(512)S(1)}, f32[512]{0:T(512)}, u32[]{:S(2)}) copy-start(f32[512]{0:T(512)} %param.9) | copy-start | bytes 6148
  37.8 14.6 %copy-start.2 = (bf16[512,512]{1,0:T(8,128)(2,1)S(1)}, bf16[512,512]{1,0:T(8,128)(2,1)}, u32[]{:S(2)}) copy-start(bf16[512,512]{1,0:T(8,128)(2,1)} %wo_ref.3) | copy-start | bytes 1572868
  37.9 14.6 %copy-start.5 = (s32[4]{0:T(128)S(1)}, s32[4]{0:T(128)}, u32[]{:S(2)}) copy-start(s32[4]{0:T(128)} %lengths_ref.1) | copy-start | bytes 52
  53.5 1.7 %collective-permute-start.4 = (bf16[256,512]{1,0:T(8,128)(2,1)S(1)}, bf16[256,512]{1,0:T(8,128)(2,1)S(1)}, u32[]{:S(2)}, u32[]{:S(2)}) collective-permute-start(bf16[256,512]{1,0:T(8,128)(2,1)S(1)} %get-tuple-element.19), channel_id=1, source_target_pairs={{0,32},{32,0},{1,33},{33,1},{2,34},{34,2},{3,35},{35,3},{4,36},{36... | collective-permute-start | bytes 786440 | tf_op jit(solution)/shard_map/ppermute | solution.py:194
  55.1 41.6 %collective-permute-start.3 = (bf16[1024,512]{1,0:T(8,128)(2,1)S(1)}, bf16[1024,512]{1,0:T(8,128)(2,1)S(1)}, u32[]{:S(2)}, u32[]{:S(2)}) collective-permute-start(bf16[1024,512]{1,0:T(8,128)(2,1)S(1)} %get-tuple-element.17), channel_id=1, source_target_pairs={{0,32},{32,0},{1,33},{33,1},{2,34},{34,2},{3,35},{35,3},{4,36},{36... | collective-permute-start | bytes 3145736 | tf_op jit(solution)/shard_map/ppermute | solution.py:194
  92.2 5.7 %collective-permute-start.5 = (bf16[256,512]{1,0:T(8,128)(2,1)S(1)}, bf16[256,512]{1,0:T(8,128)(2,1)S(1)}, u32[]{:S(2)}, u32[]{:S(2)}) collective-permute-start(bf16[256,512]{1,0:T(8,128)(2,1)S(1)} %bitcast.22), channel_id=1, source_target_pairs={{0,32},{32,0},{1,33},{33,1},{2,34},{34,2},{3,35},{35,3},{4,36},{36... | collective-permute-start | bytes 786440 | tf_op jit(solution)/shard_map/ppermute | solution.py:194

commit v8 on v7

--- a/solution.py
+++ b/solution.py
@@ -14,7 +14,6 @@
 DEPTH = ("zl", "clip")
 ANY = pl.BlockSpec(memory_space=pl.ANY)
 VMEM = pl.BlockSpec(memory_space=pltpu.VMEM)
-SMEM = pl.BlockSpec(memory_space=pltpu.SMEM)
 PARAMS = pltpu.CompilerParams(vmem_limit_bytes=12 * 1024 * 1024)
 
 
@@ -42,7 +41,7 @@
 
 
 def own_kernel(
-    place_ref, video_ref, weight_ref, qkv_ref, cot_ref, own_ref, pair_ref, value_ref
+    mask_ref, video_ref, weight_ref, qkv_ref, cot_ref, own_ref, pair_ref, value_ref
 ):
     channels = video_ref.shape[-1]
     pair_ref[...] = lax.dot_general(
@@ -124,13 +123,12 @@
             att_ref[chunk(t - 2), :] = attended(*stages[1].pop(t - 2))
 
 
-def masked_into(live_ref, place_ref, lengths_ref, cot_ref):
+def masked_into(live_ref, mask_ref, cot_ref):
     clips, frames, tile = cot_ref.shape[:3]
     for clip in range(clips):
         for frame in range(frames):
-            live = place_ref[0] * frames + frame < lengths_ref[clip]
-            rows = pl.ds((clip * frames + frame) * tile, tile)
-            live_ref[rows, :] = cot_ref[clip, frame] * jnp.where(live, 1.0, 0.0).astype(BF)
+            at = clip * frames + frame
+            live_ref[pl.ds(at * tile, tile), :] = cot_ref[clip, frame] * mask_ref[at : at + 1, :]
 
 
 def half_grad(att_ref, live_ref, half, split):
@@ -150,28 +148,31 @@
 
 
 def before_kernel(
-    place_ref, lengths_ref, att_ref, cot_ref, hidden_ref, wo_ref,
+    mask_ref, att_ref, cot_ref, hidden_ref, wo_ref,
     other_ref, live_ref, mine_ref, out_ref,
 ):
-    masked_into(live_ref, place_ref, lengths_ref, cot_ref)
+    masked_into(live_ref, mask_ref, cot_ref)
+    core = lax.axis_index("core")
     split = other_ref.shape[0]
-    other_ref[...] = half_grad(att_ref, live_ref, 1 - place_ref[1], split).astype(BF)
-
-    @pl.when(place_ref[1] == 0)
+    other_ref[...] = half_grad(att_ref, live_ref, 1 - core, split).astype(BF)
+
+    @pl.when(core == 0)
     def _():
         mine_ref[...] = half_grad(att_ref, live_ref, 0, split)
         own_rows(hidden_ref, att_ref, wo_ref, out_ref)
 
 
 def during_kernel(
-    place_ref, att_ref, live_ref, hidden_ref, wo_ref, mine_in, out_in, mine_ref, out_ref
-):
-    @pl.when(place_ref[1] == 1)
+    att_ref, live_ref, hidden_ref, wo_ref, mine_in, out_in, mine_ref, out_ref
+):
+    core = lax.axis_index("core")
+
+    @pl.when(core == 1)
     def _():
         own_rows(hidden_ref, att_ref, wo_ref, out_ref)
         mine_ref[...] = half_grad(att_ref, live_ref, 1, mine_ref.shape[0])
 
-    @pl.when(place_ref[1] == 0)
+    @pl.when(core == 0)
     def _():
         mine_ref[...] = mine_in[...]
         out_ref[...] = out_in[...]
@@ -222,14 +223,17 @@
     video = exchanged(video, "core", 1)
     cotangent = exchanged(cotangent, "core", 1)
     core = lax.axis_index("core")
-    places = jnp.stack([lax.axis_index(TIME) + 1 - 2 * core, core])
+    slab = lax.axis_index(TIME) + 1 - 2 * core
+    moments = slab * frames + jnp.arange(frames, dtype=jnp.int32)
+    mask = (moments[None, :] < lengths[:, None]).astype(BF).reshape(peers, 1)
+    mask = jnp.broadcast_to(mask, (peers, channels))
     own, pair, value = call(
         own_kernel,
         "own",
         (jax.ShapeDtypeStruct(video.shape, F32),) + (jax.ShapeDtypeStruct(out_weight.shape, BF),) * 2,
-        [SMEM] + [VMEM] * 3 + [ANY],
+        [VMEM] * 4 + [ANY],
         (VMEM,) * 3,
-        places, video, conv_weight, qkv_weight, cotangent,
+        mask, video, conv_weight, qkv_weight, cotangent,
     )
     hidden = call(
         early_kernel,
@@ -257,18 +261,18 @@
         before_kernel,
         "before",
         (jax.ShapeDtypeStruct(kept.shape, BF), rows, kept, rows),
-        [SMEM] * 2 + [VMEM] * 4,
+        [VMEM] * 5,
         (VMEM,) * 4,
-        places, lengths, att, cotangent, flat, out_weight,
+        mask, att, cotangent, flat, out_weight,
     )
     mine, out = call(
         during_kernel,
         "during",
         (kept, rows),
-        [SMEM] + [VMEM] * 6,
+        [VMEM] * 6,
         (VMEM,) * 2,
-        places, att, live, flat, out_weight, mine, out,
-        input_output_aliases={5: 0, 6: 1},
+        att, live, flat, out_weight, mine, out,
+        input_output_aliases={4: 0, 5: 1},
         cost_estimate=pl.CostEstimate(flops=1 << 29, bytes_accessed=1 << 21, transcendentals=0),
     )
     out = call(

time: 99.4 us -> 98.1 us (0.987)
  Pallas kernels: 10 us -> 8.36 us
    pallas_call x6, Pallas kernels: 10 us -> 8.36 us  [call(): pl.pallas_call(kernel, out_shape=out_shape, in_specs=in_specs, out_specs=...]
    unnamed x12 -> x10, local copies, waits for them, and re-layouts: 2.84 us -> 2.83 us
  transfers between devices with their start and end apart: 6 -> 6, of which waited for: 4 -> 4; matrix products, arithmetic and copies ran while one was open for 0% -> 1% of each run, Pallas kernels for 4% -> 3%
where the time goes in v8:
time: 98.1 us; the launch traced here: 97.7 us
  blocking collectives  67.2 us (69%)
  starting transfers between devices  8.81 us (9%)
  Pallas kernels  8.36 us (9%)
  waiting for transfers between devices  7.51 us (8%)
  local copies, waits for them, and re-layouts  3.02 us (3%)
  other arithmetic  2.04 us (2%)
    all_to_all x5, blocking collectives, a2a(): return lax.all_to_all(x, axes, split_axis=0, concat_axis=0, tiled=True)  67.2 us
    pallas_call x6, Pallas kernels, call(): pl.pallas_call(kernel, out_shape=out_shape, in_specs=in_specs, out_specs=...  8.36 us
    ppermute x5, starting transfers between devices, exchanged(): return lax.ppermute(x, axis, [(i, i ^ by) for i in range(n)])  7.29 us
    ppermute x1, waiting for transfers between devices, body(): early = lax.ppermute(video, TIME, onward)  5.42 us
    unnamed x10, local copies, waits for them, and re-layouts  2.83 us
    ppermute x5, waiting for transfers between devices, exchanged(): return lax.ppermute(x, axis, [(i, i ^ by) for i in range(n)])  2.09 us
  transfers between devices with their start and end apart: 6, of which 4 were waited for; matrix products, arithmetic and copies ran while one was open for 1% of the time, Pallas kernels for 3%

profile of v8, /device:TPU:1, one launch (start us, length us, event | category | flops | bytes accessed | tf_op | source)
XLA Modules:
  0.0 97.7 jit_solution(14821397422044913894)
XLA Ops:
  0.6 3.3 %collective-permute-start.1 = (bf16[4,2,128,512]{3,2,1,0:T(8,128)(2,1)}, bf16[4,2,128,512]{3,2,1,0:T(8,128)(2,1)S(1)}, u32[]{:S(2)}, u32[]{:S(2)}) collective-permute-start(bf16[4,2,128,512]{3,2,1,0:T(8,128)(2,1)} %param.12), channel_id=1, source_target_pairs={{0,32},{32,0},{1,33},{33,1},{2,34},{34,2},{3,35},{35,3},{4,36},{36... | collective-permute-start | bytes 3145736 | tf_op jit(solution)/shard_map/ppermute | solution.py:195
  4.0 0.1 collective-permute-start
  4.1 1.5 %collective-permute-start.2 = (bf16[4,2,128,512]{3,2,1,0:T(8,128)(2,1)}, bf16[4,2,128,512]{3,2,1,0:T(8,128)(2,1)S(1)}, u32[]{:S(2)}, u32[]{:S(2)}) collective-permute-start(bf16[4,2,128,512]{3,2,1,0:T(8,128)(2,1)} %param.7), channel_id=1, source_target_pairs={{32,96},{96,160},{160,224},{0,0},{64,64},{128,128},{192,192},{33,9... | collective-permute-start | bytes 3145736 | tf_op jit(solution)/shard_map/ppermute | solution.py:222
  5.6 0.7 compare_convert_fusion
  6.5 1.5 %collective-permute-done.video_ref = bf16[4,2,128,512]{3,2,1,0:T(8,128)(2,1)S(1)} collective-permute-done((bf16[4,2,128,512]{3,2,1,0:T(8,128)(2,1)}, bf16[4,2,128,512]{3,2,1,0:T(8,128)(2,1)S(1)}, u32[]{:S(2)}, u32[]{:S(2)}) %collective-permute-start) | collective-permute-done | bytes 1048608 | tf_op jit(solution)/shard_map/ppermute | solution.py:195
  8.0 1.4 %copy-done = bf16[3,512,512]{2,1,0:T(8,128)(2,1)S(1)} copy-done((bf16[3,512,512]{2,1,0:T(8,128)(2,1)S(1)}, bf16[3,512,512]{2,1,0:T(8,128)(2,1)}, u32[]{:S(2)}) %copy-start) | copy-done | bytes 1572888
  9.4 1.4 %copy-done.3 = bf16[512,1536]{1,0:T(8,128)(2,1)S(1)} copy-done((bf16[512,1536]{1,0:T(8,128)(2,1)S(1)}, bf16[512,1536]{1,0:T(8,128)(2,1)}, u32[]{:S(2)}) %copy-start.3) | copy-done | bytes 1572888
  10.8 1.3 %own.1 = (f32[4,2,128,512]{3,2,1,0:T(8,128)S(1)}, bf16[512,512]{1,0:T(8,128)(2,1)S(1)}, bf16[512,512]{1,0:T(8,128)(2,1)S(1)}) custom-call(bf16[8,512]{1,0:T(8,128)(2,1)S(1)} %broadcast_in_dim.6.mask_ref, bf16[4,2,128,512]{3,2,1,0:T(8,128)(2,1)S(1)} %collective-permute-done.video_ref, bf16[3,512,512]{2,1,0:T(8,128)(2,1)S(1)} %copy-done, ...), custom_call_target="tpu_custom_call" | custom-call | tf_op jit(solution)/shard_map/own/pallas_call | solution.py:32
  12.1 5.4 %collective-permute-done.2.early_ref = bf16[4,2,128,512]{3,2,1,0:T(8,128)(2,1)S(1)} collective-permute-done((bf16[4,2,128,512]{3,2,1,0:T(8,128)(2,1)}, bf16[4,2,128,512]{3,2,1,0:T(8,128)(2,1)S(1)}, u32[]{:S(2)}, u32[]{:S(2)}) %collective-permute-start.2) | collective-permute-done | bytes 1048608 | tf_op jit(solution)/shard_map/ppermute | solution.py:222
  17.6 1.0 %early.1 = bf16[4,2,128,512]{3,2,1,0:T(8,128)(2,1)S(1)} custom-call(f32[4,2,128,512]{3,2,1,0:T(8,128)S(1)} %get-tuple-element.11.own_ref, bf16[4,2,128,512]{3,2,1,0:T(8,128)(2,1)S(1)} %collective-permute-done.2.early_ref, bf16[3,512,512]{2,1,0:T(8,128)(2,1)S(1)} %copy-done.1), custom_call_target="tpu_custom_call" | custom-call | tf_op jit(solution)/shard_map/early/pallas_call | solution.py:32
  18.6 15.5 %all_to_all.25 = bf16[8,128,512]{2,1,0:T(8,128)(2,1)S(1)} all-to-all(bf16[8,128,512]{2,1,0:T(8,128)(2,1)S(1)} %bitcast.11), channel_id=1, replica_groups=mesh['y'=4,'core'=2,'x'=4,'zl'=2,'clip'=4] {'x','zl'}, dimensions={0} | all-to-all | bytes 2097152 | tf_op jit(solution)/shard_map/all_to_all | solution.py:21
  34.1 3.6 %attend.1 = bf16[1024,512]{1,0:T(8,128)(2,1)S(1)} custom-call(bf16[1024,512]{1,0:T(8,128)(2,1)S(1)} %bitcast.16, f32[1,512]{1,0:T(1,128)S(1)} %bitcast.18, bf16[512,512]{1,0:T(8,128)(2,1)S(1)} %get-tuple-element.12.pair_ref, bf16[512,512]{1,0:T(8,128)(2,1)S(1)} %get-tuple-element.13.value_ref), custom_call_target="tpu_custom_call" | custom-call | tf_op jit(solution)/shard_map/attend/pallas_call | solution.py:32
  37.7 14.0 %all_to_all.26 = bf16[8,128,512]{2,1,0:T(8,128)(2,1)S(1)} all-to-all(bf16[8,128,512]{2,1,0:T(8,128)(2,1)S(1)} %bitcast.17), channel_id=1, replica_groups=mesh['y'=4,'core'=2,'x'=4,'zl'=2,'clip'=4] {'x','zl'}, dimensions={0} | all-to-all | bytes 2097152 | tf_op jit(solution)/shard_map/all_to_all | solution.py:21
  51.8 0.5 before.1
  52.3 1.0 %during.1 = (f32[256,512]{1,0:T(8,128)S(1)}, bf16[1024,512]{1,0:T(8,128)(2,1)S(1)}) custom-call(bf16[1024,512]{1,0:T(8,128)(2,1)S(1)} %bitcast.15, bf16[1024,512]{1,0:T(8,128)(2,1)S(1)} %get-tuple-element.14.live_ref, bf16[1024,512]{1,0:T(8,128)(2,1)S(1)} %bitcast.13, bf16[512,512]{1,0:T(8,128)(2,1)S(1)} %copy-done.2, ...), custom_call_target="tpu_custom_call", output_to_operand_aliasing={{0}: (4, {}), {1}: (5, {})} | custom-call | flops 536870912 | bytes 2097152 | tf_op jit(solution)/shard_map/during/pallas_call | solution.py:32
  53.3 0.1 collective-permute-start.3
  53.4 0.4 collective-permute-done.4
  53.9 13.1 %all_to_all.27 = bf16[16,16,512]{2,1,0:T(8,128)(2,1)S(1)} all-to-all(bf16[16,16,512]{2,1,0:T(8,128)(2,1)S(1)} %bitcast.21), channel_id=1, replica_groups=mesh['y'=4,'core'=2,'x'=4,'zl'=2,'clip'=4] {'y','x'}, dimensions={0} | all-to-all | bytes 524288 | tf_op jit(solution)/shard_map/all_to_all | solution.py:21
  67.2 14.2 %all_to_all.28 = bf16[8,16,512]{2,1,0:T(8,128)(2,1)S(1)} all-to-all(bf16[8,16,512]{2,1,0:T(8,128)(2,1)S(1)} %broadcast_in_dim.7), channel_id=1, replica_groups=mesh['y'=4,'core'=2,'x'=4,'zl'=2,'clip'=4] {'zl','clip'}, dimensions={0} | all-to-all | bytes 262144 | tf_op jit(solution)/shard_map/all_to_all | solution.py:21
  81.4 10.3 %all_to_all.29 = bf16[16,16,512]{2,1,0:T(8,128)(2,1)S(1)} all-to-all(bf16[16,16,512]{2,1,0:T(8,128)(2,1)S(1)} %broadcast_in_dim.8), channel_id=1, replica_groups=mesh['y'=4,'core'=2,'x'=4,'zl'=2,'clip'=4] {'y','x'}, dimensions={0} | all-to-all | bytes 524288 | tf_op jit(solution)/shard_map/all_to_all | solution.py:21
  91.7 3.7 %collective-permute-start.5 = (bf16[256,512]{1,0:T(8,128)(2,1)S(1)}, bf16[256,512]{1,0:T(8,128)(2,1)S(1)}, u32[]{:S(2)}, u32[]{:S(2)}) collective-permute-start(bf16[256,512]{1,0:T(8,128)(2,1)S(1)} %bitcast.20), channel_id=1, source_target_pairs={{0,32},{32,0},{1,33},{33,1},{2,34},{34,2},{3,35},{35,3},{4,36},{36... | collective-permute-start | bytes 786440 | tf_op jit(solution)/shard_map/ppermute | solution.py:195
  95.4 1.0 %deliver.1 = bf16[1024,512]{1,0:T(8,128)(2,1)} custom-call(bf16[1024,512]{1,0:T(8,128)(2,1)S(1)} %collective-permute-done.3.src_ref), custom_call_target="tpu_custom_call" | custom-call | flops 268435456 | bytes 2097152 | tf_op jit(solution)/shard_map/deliver/pallas_call | solution.py:32
  96.4 0.1 collective-permute-done.5
  96.6 1.1 %maximum_convert_fusion = f32[512,512]{1,0:T(8,128)} fusion(bf16[256,512]{1,0:T(8,128)(2,1)S(1)} %get-tuple-element.21, bf16[256,512]{1,0:T(8,128)(2,1)S(1)} %get-tuple-element.20), kind=kLoop, calls=%fused_computation | loop fusion | flops 1048576 | bytes 1572864 | tf_op jit(solution)/shard_map/convert_element_type | solution.py:214
  (20 shorter events, 0.5 us)
Async XLA Ops:
  0.6 5.8 %collective-permute-start.1 = (bf16[4,2,128,512]{3,2,1,0:T(8,128)(2,1)}, bf16[4,2,128,512]{3,2,1,0:T(8,128)(2,1)S(1)}, u32[]{:S(2)}, u32[]{:S(2)}) collective-permute-start(bf16[4,2,128,512]{3,2,1,0:T(8,128)(2,1)} %param.12), channel_id=1, source_target_pairs={{0,32},{32,0},{1,33},{33,1},{2,34},{34,2},{3,35},{35,3},{4,36},{36... | collective-permute-start | bytes 3145736 | tf_op jit(solution)/shard_map/ppermute | solution.py:195
  4.0 4.0 %collective-permute-start = (bf16[4,2,128,512]{3,2,1,0:T(8,128)(2,1)}, bf16[4,2,128,512]{3,2,1,0:T(8,128)(2,1)S(1)}, u32[]{:S(2)}, u32[]{:S(2)}) collective-permute-start(bf16[4,2,128,512]{3,2,1,0:T(8,128)(2,1)} %param.7), channel_id=1, source_target_pairs={{0,32},{32,0},{1,33},{33,1},{2,34},{34,2},{3,35},{35,3},{4,36},{36... | collective-permute-start | bytes 3145736 | tf_op jit(solution)/shard_map/ppermute | solution.py:195
  4.1 13.5 %collective-permute-start.2 = (bf16[4,2,128,512]{3,2,1,0:T(8,128)(2,1)}, bf16[4,2,128,512]{3,2,1,0:T(8,128)(2,1)S(1)}, u32[]{:S(2)}, u32[]{:S(2)}) collective-permute-start(bf16[4,2,128,512]{3,2,1,0:T(8,128)(2,1)} %param.7), channel_id=1, source_target_pairs={{32,96},{96,160},{160,224},{0,0},{64,64},{128,128},{192,192},{33,9... | collective-permute-start | bytes 3145736 | tf_op jit(solution)/shard_map/ppermute | solution.py:222
  8.0 1.4 %copy-start = (bf16[3,512,512]{2,1,0:T(8,128)(2,1)S(1)}, bf16[3,512,512]{2,1,0:T(8,128)(2,1)}, u32[]{:S(2)}) copy-start(bf16[3,512,512]{2,1,0:T(8,128)(2,1)} %weight_ref.3) | copy-start | bytes 4718596
  9.4 1.4 %copy-start.3 = (bf16[512,1536]{1,0:T(8,128)(2,1)S(1)}, bf16[512,1536]{1,0:T(8,128)(2,1)}, u32[]{:S(2)}) copy-start(bf16[512,1536]{1,0:T(8,128)(2,1)} %qkv_ref.1) | copy-start | bytes 4718596
  10.8 6.7 %copy-start.1 = (bf16[3,512,512]{2,1,0:T(8,128)(2,1)S(1)}, bf16[3,512,512]{2,1,0:T(8,128)(2,1)}, u32[]{:S(2)}) copy-start(bf16[3,512,512]{2,1,0:T(8,128)(2,1)} %weight_ref.3) | copy-start | bytes 4718596
  18.5 15.5 %copy-start.4 = (f32[512]{0:T(512)S(1)}, f32[512]{0:T(512)}, u32[]{:S(2)}) copy-start(f32[512]{0:T(512)} %param.9) | copy-start | bytes 6148
  37.7 14.1 %copy-start.2 = (bf16[512,512]{1,0:T(8,128)(2,1)S(1)}, bf16[512,512]{1,0:T(8,128)(2,1)}, u32[]{:S(2)}) copy-start(bf16[512,512]{1,0:T(8,128)(2,1)} %wo_ref.3) | copy-start | bytes 1572868
  52.2 1.6 %collective-permute-start.4 = (bf16[256,512]{1,0:T(8,128)(2,1)S(1)}, bf16[256,512]{1,0:T(8,128)(2,1)S(1)}, u32[]{:S(2)}, u32[]{:S(2)}) collective-permute-start(bf16[256,512]{1,0:T(8,128)(2,1)S(1)} %get-tuple-element.19), channel_id=1, source_target_pairs={{0,32},{32,0},{1,33},{33,1},{2,34},{34,2},{3,35},{35,3},{4,36},{36... | collective-permute-start | bytes 786440 | tf_op jit(solution)/shard_map/ppermute | solution.py:195
  53.3 42.0 %collective-permute-start.3 = (bf16[1024,512]{1,0:T(8,128)(2,1)S(1)}, bf16[1024,512]{1,0:T(8,128)(2,1)S(1)}, u32[]{:S(2)}, u32[]{:S(2)}) collective-permute-start(bf16[1024,512]{1,0:T(8,128)(2,1)S(1)} %get-tuple-element.17), channel_id=1, source_target_pairs={{0,32},{32,0},{1,33},{33,1},{2,34},{34,2},{3,35},{35,3},{4,36},{36... | collective-permute-start | bytes 3145736 | tf_op jit(solution)/shard_map/ppermute | solution.py:195
  91.7 4.8 %collective-permute-start.5 = (bf16[256,512]{1,0:T(8,128)(2,1)S(1)}, bf16[256,512]{1,0:T(8,128)(2,1)S(1)}, u32[]{:S(2)}, u32[]{:S(2)}) collective-permute-start(bf16[256,512]{1,0:T(8,128)(2,1)S(1)} %bitcast.20), channel_id=1, source_target_pairs={{0,32},{32,0},{1,33},{33,1},{2,34},{34,2},{3,35},{35,3},{4,36},{36... | collective-permute-start | bytes 786440 | tf_op jit(solution)/shard_map/ppermute | solution.py:195

commit v9 on v8

--- a/solution.py
+++ b/solution.py
@@ -178,7 +178,7 @@
         out_ref[...] = out_in[...]
 
 
-def deliver_kernel(src_ref, out_ref, sems):
+def deliver_kernel(src_ref, half_ref, out_ref, total_ref, wide, sems, sem):
     each = src_ref.shape[0] // sems.shape[0]
     copies = [
         pltpu.make_async_copy(src_ref.at[pl.ds(i * each, each)], out_ref.at[pl.ds(i * each, each)], sems.at[i])
@@ -186,8 +186,22 @@
     ]
     for copy in copies:
         copy.start()
+    rows = half_ref.shape[0]
+    wide[...] = half_ref[...].astype(F32)
+    at = pl.ds(pl.multiple_of(lax.axis_index("core") * rows, rows), rows)
+    copies.append(pltpu.make_async_copy(wide, total_ref.at[at], sem))
+    copies[-1].start()
     for copy in copies:
         copy.wait()
+
+
+def complete_kernel(half_ref, total_in, total_ref, wide, sem):
+    rows = half_ref.shape[0]
+    wide[...] = half_ref[...].astype(F32)
+    at = pl.ds(pl.multiple_of((1 - lax.axis_index("core")) * rows, rows), rows)
+    copy = pltpu.make_async_copy(wide, total_ref.at[at], sem)
+    copy.start()
+    copy.wait()
 
 
 def exchanged(x, axis, by):
@@ -201,17 +215,13 @@
 
 
 def total_sum(mine, other):
-    core = lax.axis_index("core")
     x = mine + exchanged(other, "core", 1).astype(F32)
     n = group_size(PLANE)
     x = a2a(x.astype(BF).reshape(n, x.shape[0] // n, x.shape[1]), PLANE)
     x = jnp.sum(x.astype(F32), axis=0)
     x = jnp.sum(spread(x, DEPTH).astype(F32), axis=0).astype(BF)
     x = spread(x, PLANE).reshape(mine.shape)
-    other = exchanged(x, "core", 1)
-    first = jnp.where(core == 0, x, other)
-    second = jnp.where(core == 0, other, x)
-    return jnp.concatenate([first, second], 0).astype(F32)
+    return x
 
 
 def body(video, conv_weight, norm_gain, qkv_weight, out_weight, cotangent, lengths):
@@ -275,17 +285,33 @@
         input_output_aliases={4: 0, 5: 1},
         cost_estimate=pl.CostEstimate(flops=1 << 29, bytes_accessed=1 << 21, transcendentals=0),
     )
-    out = call(
+    half = total_sum(mine, other)
+    whole = jax.ShapeDtypeStruct((channels, channels), F32)
+    out, total = call(
         deliver_kernel,
         "deliver",
-        rows,
-        [ANY],
+        (rows, whole),
+        [ANY, VMEM],
+        (ANY, ANY),
+        exchanged(out, "core", 1), half,
+        scratch_shapes=[
+            pltpu.VMEM(half.shape, F32),
+            pltpu.SemaphoreType.DMA((peers,)),
+            pltpu.SemaphoreType.DMA,
+        ],
+        cost_estimate=pl.CostEstimate(flops=1 << 28, bytes_accessed=1 << 21, transcendentals=0),
+    )
+    total = call(
+        complete_kernel,
+        "complete",
+        whole,
+        [VMEM, ANY],
         ANY,
-        exchanged(out, "core", 1),
-        scratch_shapes=[pltpu.SemaphoreType.DMA((peers,))],
-        cost_estimate=pl.CostEstimate(flops=1 << 28, bytes_accessed=1 << 21, transcendentals=0),
-    )
-    return out.reshape(video.shape), total_sum(mine, other)
+        exchanged(half, "core", 1), total,
+        input_output_aliases={1: 0},
+        scratch_shapes=[pltpu.VMEM(half.shape, F32), pltpu.SemaphoreType.DMA],
+    )
+    return out.reshape(video.shape), total
 
 
 def solution(mesh):

time: 98.1 us -> 97.9 us (level)
  other arithmetic: 2.04 us -> 0.88 us
  Pallas kernels: 8.36 us -> 9.39 us
    convert_element_type x1 -> x0, other arithmetic: 1.1 us -> none  [total_sum(): return jnp.concatenate([first, second], 0).astype(F32)]
    pallas_call x6 -> x7, Pallas kernels: 8.36 us -> 9.39 us  [call(): pl.pallas_call(kernel, out_shape=out_shape, in_specs=in_specs, out_specs=...]
  transfers between devices with their start and end apart: 6 -> 6, of which waited for: 4 -> 3; matrix products, arithmetic and copies ran while one was open for 1% -> 1% of each run, Pallas kernels for 3% -> 4%
where the time goes in v9:
time: 97.9 us; the launch traced here: 97.5 us
  blocking collectives  67.2 us (69%)
  Pallas kernels  9.39 us (10%)
  starting transfers between devices  8.81 us (9%)
  waiting for transfers between devices  7.39 us (8%)
  local copies, waits for them, and re-layouts  3.02 us (3%)
    all_to_all x5, blocking collectives, a2a(): return lax.all_to_all(x, axes, split_axis=0, concat_axis=0, tiled=True)  67.2 us
    pallas_call x7, Pallas kernels, call(): pl.pallas_call(kernel, out_shape=out_shape, in_specs=in_specs, out_specs=...  9.39 us
    ppermute x5, starting transfers between devices, exchanged(): return lax.ppermute(x, axis, [(i, i ^ by) for i in range(n)])  7.29 us
    ppermute x1, waiting for transfers between devices, body(): early = lax.ppermute(video, TIME, onward)  5.42 us
    unnamed x10, local copies, waits for them, and re-layouts  2.83 us
    ppermute x5, waiting for transfers between devices, exchanged(): return lax.ppermute(x, axis, [(i, i ^ by) for i in range(n)])  1.97 us
  transfers between devices with their start and end apart: 6, of which 3 were waited for; matrix products, arithmetic and copies ran while one was open for 1% of the time, Pallas kernels for 4%

profile of v9, /device:TPU:1, one launch (start us, length us, event | category | flops | bytes accessed | tf_op | source)
XLA Modules:
  0.0 97.5 jit_solution(18132262394410051218)
XLA Ops:
  0.6 3.3 %collective-permute-start.1 = (bf16[4,2,128,512]{3,2,1,0:T(8,128)(2,1)}, bf16[4,2,128,512]{3,2,1,0:T(8,128)(2,1)S(1)}, u32[]{:S(2)}, u32[]{:S(2)}) collective-permute-start(bf16[4,2,128,512]{3,2,1,0:T(8,128)(2,1)} %param.12), channel_id=1, source_target_pairs={{0,32},{32,0},{1,33},{33,1},{2,34},{34,2},{3,35},{35,3},{4,36},{36... | collective-permute-start | bytes 3145736 | tf_op jit(solution)/shard_map/ppermute | solution.py:209
  4.0 0.1 collective-permute-start
  4.1 1.5 %collective-permute-start.2 = (bf16[4,2,128,512]{3,2,1,0:T(8,128)(2,1)}, bf16[4,2,128,512]{3,2,1,0:T(8,128)(2,1)S(1)}, u32[]{:S(2)}, u32[]{:S(2)}) collective-permute-start(bf16[4,2,128,512]{3,2,1,0:T(8,128)(2,1)} %param.7), channel_id=1, source_target_pairs={{32,96},{96,160},{160,224},{0,0},{64,64},{128,128},{192,192},{33,9... | collective-permute-start | bytes 3145736 | tf_op jit(solution)/shard_map/ppermute | solution.py:232
  5.6 0.7 compare_convert_fusion
  6.5 1.5 %collective-permute-done.video_ref = bf16[4,2,128,512]{3,2,1,0:T(8,128)(2,1)S(1)} collective-permute-done((bf16[4,2,128,512]{3,2,1,0:T(8,128)(2,1)}, bf16[4,2,128,512]{3,2,1,0:T(8,128)(2,1)S(1)}, u32[]{:S(2)}, u32[]{:S(2)}) %collective-permute-start) | collective-permute-done | bytes 1048608 | tf_op jit(solution)/shard_map/ppermute | solution.py:209
  8.0 1.4 %copy-done = bf16[3,512,512]{2,1,0:T(8,128)(2,1)S(1)} copy-done((bf16[3,512,512]{2,1,0:T(8,128)(2,1)S(1)}, bf16[3,512,512]{2,1,0:T(8,128)(2,1)}, u32[]{:S(2)}) %copy-start) | copy-done | bytes 1572888
  9.4 1.4 %copy-done.3 = bf16[512,1536]{1,0:T(8,128)(2,1)S(1)} copy-done((bf16[512,1536]{1,0:T(8,128)(2,1)S(1)}, bf16[512,1536]{1,0:T(8,128)(2,1)}, u32[]{:S(2)}) %copy-start.3) | copy-done | bytes 1572888
  10.8 1.3 %own.1 = (f32[4,2,128,512]{3,2,1,0:T(8,128)S(1)}, bf16[512,512]{1,0:T(8,128)(2,1)S(1)}, bf16[512,512]{1,0:T(8,128)(2,1)S(1)}) custom-call(bf16[8,512]{1,0:T(8,128)(2,1)S(1)} %broadcast_in_dim.6.mask_ref, bf16[4,2,128,512]{3,2,1,0:T(8,128)(2,1)S(1)} %collective-permute-done.video_ref, bf16[3,512,512]{2,1,0:T(8,128)(2,1)S(1)} %copy-done, ...), custom_call_target="tpu_custom_call" | custom-call | tf_op jit(solution)/shard_map/own/pallas_call | solution.py:32
  12.1 5.4 %collective-permute-done.2.early_ref = bf16[4,2,128,512]{3,2,1,0:T(8,128)(2,1)S(1)} collective-permute-done((bf16[4,2,128,512]{3,2,1,0:T(8,128)(2,1)}, bf16[4,2,128,512]{3,2,1,0:T(8,128)(2,1)S(1)}, u32[]{:S(2)}, u32[]{:S(2)}) %collective-permute-start.2) | collective-permute-done | bytes 1048608 | tf_op jit(solution)/shard_map/ppermute | solution.py:232
  17.6 1.0 %early.1 = bf16[4,2,128,512]{3,2,1,0:T(8,128)(2,1)S(1)} custom-call(f32[4,2,128,512]{3,2,1,0:T(8,128)S(1)} %get-tuple-element.13.own_ref, bf16[4,2,128,512]{3,2,1,0:T(8,128)(2,1)S(1)} %collective-permute-done.2.early_ref, bf16[3,512,512]{2,1,0:T(8,128)(2,1)S(1)} %copy-done.1), custom_call_target="tpu_custom_call" | custom-call | tf_op jit(solution)/shard_map/early/pallas_call | solution.py:32
  18.6 15.5 %all_to_all.25 = bf16[8,128,512]{2,1,0:T(8,128)(2,1)S(1)} all-to-all(bf16[8,128,512]{2,1,0:T(8,128)(2,1)S(1)} %bitcast.9), channel_id=1, replica_groups=mesh['y'=4,'core'=2,'x'=4,'zl'=2,'clip'=4] {'x','zl'}, dimensions={0} | all-to-all | bytes 2097152 | tf_op jit(solution)/shard_map/all_to_all | solution.py:21
  34.1 3.6 %attend.1 = bf16[1024,512]{1,0:T(8,128)(2,1)S(1)} custom-call(bf16[1024,512]{1,0:T(8,128)(2,1)S(1)} %bitcast.14, f32[1,512]{1,0:T(1,128)S(1)} %bitcast.18, bf16[512,512]{1,0:T(8,128)(2,1)S(1)} %get-tuple-element.14.pair_ref, bf16[512,512]{1,0:T(8,128)(2,1)S(1)} %get-tuple-element.15.value_ref), custom_call_target="tpu_custom_call" | custom-call | tf_op jit(solution)/shard_map/attend/pallas_call | solution.py:32
  37.7 14.0 %all_to_all.26 = bf16[8,128,512]{2,1,0:T(8,128)(2,1)S(1)} all-to-all(bf16[8,128,512]{2,1,0:T(8,128)(2,1)S(1)} %bitcast.15), channel_id=1, replica_groups=mesh['y'=4,'core'=2,'x'=4,'zl'=2,'clip'=4] {'x','zl'}, dimensions={0} | all-to-all | bytes 2097152 | tf_op jit(solution)/shard_map/all_to_all | solution.py:21
  51.8 0.5 before.1
  52.2 0.1 collective-permute-start.4
  52.3 1.0 %during.1 = (f32[256,512]{1,0:T(8,128)S(1)}, bf16[1024,512]{1,0:T(8,128)(2,1)S(1)}) custom-call(bf16[1024,512]{1,0:T(8,128)(2,1)S(1)} %bitcast.13, bf16[1024,512]{1,0:T(8,128)(2,1)S(1)} %get-tuple-element.16.live_ref, bf16[1024,512]{1,0:T(8,128)(2,1)S(1)} %bitcast.11, bf16[512,512]{1,0:T(8,128)(2,1)S(1)} %copy-done.2, ...), custom_call_target="tpu_custom_call", output_to_operand_aliasing={{0}: (4, {}), {1}: (5, {})} | custom-call | flops 536870912 | bytes 2097152 | tf_op jit(solution)/shard_map/during/pallas_call | solution.py:32
  53.3 0.1 collective-permute-start.3
  53.4 0.4 collective-permute-done.4
  53.9 13.1 %all_to_all.27 = bf16[16,16,512]{2,1,0:T(8,128)(2,1)S(1)} all-to-all(bf16[16,16,512]{2,1,0:T(8,128)(2,1)S(1)} %bitcast.19), channel_id=1, replica_groups=mesh['y'=4,'core'=2,'x'=4,'zl'=2,'clip'=4] {'y','x'}, dimensions={0} | all-to-all | bytes 524288 | tf_op jit(solution)/shard_map/all_to_all | solution.py:21
  67.2 14.2 %all_to_all.28 = bf16[8,16,512]{2,1,0:T(8,128)(2,1)S(1)} all-to-all(bf16[8,16,512]{2,1,0:T(8,128)(2,1)S(1)} %broadcast_in_dim.7), channel_id=1, replica_groups=mesh['y'=4,'core'=2,'x'=4,'zl'=2,'clip'=4] {'zl','clip'}, dimensions={0} | all-to-all | bytes 262144 | tf_op jit(solution)/shard_map/all_to_all | solution.py:21
  81.4 10.3 %all_to_all.29 = bf16[16,16,512]{2,1,0:T(8,128)(2,1)S(1)} all-to-all(bf16[16,16,512]{2,1,0:T(8,128)(2,1)S(1)} %broadcast_in_dim.8), channel_id=1, replica_groups=mesh['y'=4,'core'=2,'x'=4,'zl'=2,'clip'=4] {'y','x'}, dimensions={0} | all-to-all | bytes 524288 | tf_op jit(solution)/shard_map/all_to_all | solution.py:21
  91.7 3.7 %collective-permute-start.5 = (bf16[256,512]{1,0:T(8,128)(2,1)S(1)}, bf16[256,512]{1,0:T(8,128)(2,1)S(1)}, u32[]{:S(2)}, u32[]{:S(2)}) collective-permute-start(bf16[256,512]{1,0:T(8,128)(2,1)S(1)} %bitcast.16), channel_id=1, source_target_pairs={{0,32},{32,0},{1,33},{33,1},{2,34},{34,2},{3,35},{35,3},{4,36},{36... | collective-permute-start | bytes 786440 | tf_op jit(solution)/shard_map/ppermute | solution.py:209
  95.4 1.2 %deliver.1 = (bf16[1024,512]{1,0:T(8,128)(2,1)}, f32[512,512]{1,0:T(8,128)}) custom-call(bf16[1024,512]{1,0:T(8,128)(2,1)S(1)} %collective-permute-done.3.src_ref, bf16[256,512]{1,0:T(8,128)(2,1)S(1)} %bitcast.17), custom_call_target="tpu_custom_call" | custom-call | flops 268435456 | bytes 2097152 | tf_op jit(solution)/shard_map/deliver/pallas_call | solution.py:32
  96.6 0.8 complete.1
  (19 shorter events, 0.4 us)
Async XLA Ops:
  0.6 5.8 %collective-permute-start.1 = (bf16[4,2,128,512]{3,2,1,0:T(8,128)(2,1)}, bf16[4,2,128,512]{3,2,1,0:T(8,128)(2,1)S(1)}, u32[]{:S(2)}, u32[]{:S(2)}) collective-permute-start(bf16[4,2,128,512]{3,2,1,0:T(8,128)(2,1)} %param.12), channel_id=1, source_target_pairs={{0,32},{32,0},{1,33},{33,1},{2,34},{34,2},{3,35},{35,3},{4,36},{36... | collective-permute-start | bytes 3145736 | tf_op jit(solution)/shard_map/ppermute | solution.py:209
  4.0 4.0 %collective-permute-start = (bf16[4,2,128,512]{3,2,1,0:T(8,128)(2,1)}, bf16[4,2,128,512]{3,2,1,0:T(8,128)(2,1)S(1)}, u32[]{:S(2)}, u32[]{:S(2)}) collective-permute-start(bf16[4,2,128,512]{3,2,1,0:T(8,128)(2,1)} %param.7), channel_id=1, source_target_pairs={{0,32},{32,0},{1,33},{33,1},{2,34},{34,2},{3,35},{35,3},{4,36},{36... | collective-permute-start | bytes 3145736 | tf_op jit(solution)/shard_map/ppermute | solution.py:209
  4.1 13.5 %collective-permute-start.2 = (bf16[4,2,128,512]{3,2,1,0:T(8,128)(2,1)}, bf16[4,2,128,512]{3,2,1,0:T(8,128)(2,1)S(1)}, u32[]{:S(2)}, u32[]{:S(2)}) collective-permute-start(bf16[4,2,128,512]{3,2,1,0:T(8,128)(2,1)} %param.7), channel_id=1, source_target_pairs={{32,96},{96,160},{160,224},{0,0},{64,64},{128,128},{192,192},{33,9... | collective-permute-start | bytes 3145736 | tf_op jit(solution)/shard_map/ppermute | solution.py:232
  8.0 1.4 %copy-start = (bf16[3,512,512]{2,1,0:T(8,128)(2,1)S(1)}, bf16[3,512,512]{2,1,0:T(8,128)(2,1)}, u32[]{:S(2)}) copy-start(bf16[3,512,512]{2,1,0:T(8,128)(2,1)} %weight_ref.3) | copy-start | bytes 4718596
  9.4 1.4 %copy-start.3 = (bf16[512,1536]{1,0:T(8,128)(2,1)S(1)}, bf16[512,1536]{1,0:T(8,128)(2,1)}, u32[]{:S(2)}) copy-start(bf16[512,1536]{1,0:T(8,128)(2,1)} %qkv_ref.1) | copy-start | bytes 4718596
  10.8 6.7 %copy-start.1 = (bf16[3,512,512]{2,1,0:T(8,128)(2,1)S(1)}, bf16[3,512,512]{2,1,0:T(8,128)(2,1)}, u32[]{:S(2)}) copy-start(bf16[3,512,512]{2,1,0:T(8,128)(2,1)} %weight_ref.3) | copy-start | bytes 4718596
  18.5 15.5 %copy-start.4 = (f32[512]{0:T(512)S(1)}, f32[512]{0:T(512)}, u32[]{:S(2)}) copy-start(f32[512]{0:T(512)} %param.9) | copy-start | bytes 6148
  37.7 14.1 %copy-start.2 = (bf16[512,512]{1,0:T(8,128)(2,1)S(1)}, bf16[512,512]{1,0:T(8,128)(2,1)}, u32[]{:S(2)}) copy-start(bf16[512,512]{1,0:T(8,128)(2,1)} %wo_ref.3) | copy-start | bytes 1572868
  52.2 1.6 %collective-permute-start.4 = (bf16[256,512]{1,0:T(8,128)(2,1)S(1)}, bf16[256,512]{1,0:T(8,128)(2,1)S(1)}, u32[]{:S(2)}, u32[]{:S(2)}) collective-permute-start(bf16[256,512]{1,0:T(8,128)(2,1)S(1)} %get-tuple-element.21), channel_id=1, source_target_pairs={{0,32},{32,0},{1,33},{33,1},{2,34},{34,2},{3,35},{35,3},{4,36},{36... | collective-permute-start | bytes 786440 | tf_op jit(solution)/shard_map/ppermute | solution.py:209
  53.3 42.0 %collective-permute-start.3 = (bf16[1024,512]{1,0:T(8,128)(2,1)S(1)}, bf16[1024,512]{1,0:T(8,128)(2,1)S(1)}, u32[]{:S(2)}, u32[]{:S(2)}) collective-permute-start(bf16[1024,512]{1,0:T(8,128)(2,1)S(1)} %get-tuple-element.19), channel_id=1, source_target_pairs={{0,32},{32,0},{1,33},{33,1},{2,34},{34,2},{3,35},{35,3},{4,36},{36... | collective-permute-start | bytes 3145736 | tf_op jit(solution)/shard_map/ppermute | solution.py:209
  91.7 4.9 %collective-permute-start.5 = (bf16[256,512]{1,0:T(8,128)(2,1)S(1)}, bf16[256,512]{1,0:T(8,128)(2,1)S(1)}, u32[]{:S(2)}, u32[]{:S(2)}) collective-permute-start(bf16[256,512]{1,0:T(8,128)(2,1)S(1)} %bitcast.16), channel_id=1, source_target_pairs={{0,32},{32,0},{1,33},{33,1},{2,34},{34,2},{3,35},{35,3},{4,36},{36... | collective-permute-start | bytes 786440 | tf_op jit(solution)/shard_map/ppermute | solution.py:209
